TPU v7x, 256 devices: a whole 4x4x8 slice. The times are simulated.
256 devices in a mesh: seq: 128 (over x, y, z_lo, core), dp: 2 (over z_hi).
Axes of the slice: x: 4, y: 4, z: 8 (z_hi: 2, z_lo: 4; z = z_hi * 4 + z_lo), core: 2. Of those that a mesh axis runs over, the one named last changes fastest.
Arguments:
- inputs: bfloat16 [2, 16384, 1024], P('dp', 'seq'), may hold values from -6 to 6
- cotangent: bfloat16 [2, 16384, 1024], P('dp', 'seq'), may hold values from -6 to 6
- value_weight: bfloat16 [1024, 1024], replicated, may hold values from -0.1875 to 0.1875
- gate_weight: bfloat16 [1024, 1024], replicated, may hold values from -0.1875 to 0.1875
- filter_taps: bfloat16 [16384, 1024], P('seq'), as said below
Outputs:
- input_grad: bfloat16 [2, 16384, 1024], P('dp', 'seq')
- projection_grads: float32 [2048, 1024], P('seq', 'dp')
- filter_grad: float32 [16384, 1024], P('seq')
Inputs may be any that keep to these rules, and one draw needn't show every extreme that they name: `filter_taps`: real filter taps of order 16384^(-1/2), independent over positions and channels.
All inputs are finite; a program needn't handle non-finite values.
Results may differ from a plain program's by a relative error of at most 0.014.
Values may be sent and summed in bfloat16 or wider, within the bound.
No kernel may reach another device: no remote copies, remote signals or barrier semaphores. Data moves between devices by JAX's collectives and lax.ppermute only.
A program may use at most 128 MiB of HBM per device.

v0:
```python
import math

import jax
import jax.numpy as jnp
from jax import lax
from jax.sharding import PartitionSpec as P

HIGH = lax.Precision.HIGHEST


def outer_tables(shards):
    freq_idx = jnp.arange(2 * shards, dtype=jnp.int32)[:, None]
    shard_idx = jnp.arange(shards, dtype=jnp.int32)[None, :]
    angle = 2.0 * math.pi / (2 * shards) * (freq_idx * shard_idx % (2 * shards)).astype(jnp.float32)
    return (jnp.cos(angle), jnp.sin(angle))


def inner_tables(block):
    index = jnp.arange(block, dtype=jnp.int32)
    angle = 2.0 * math.pi / block * (index[:, None] * index[None, :] % block).astype(jnp.float32)
    return (jnp.cos(angle), jnp.sin(angle))


def inner_forward(moved_re, moved_im, block):
    inner_re, inner_im = inner_tables(block)
    spec_re = jnp.einsum("kj,sljc->slkc", inner_re, moved_re, precision=HIGH) + jnp.einsum(
        "kj,sljc->slkc", inner_im, moved_im, precision=HIGH
    )
    spec_im = jnp.einsum("kj,sljc->slkc", inner_re, moved_im, precision=HIGH) - jnp.einsum(
        "kj,sljc->slkc", inner_im, moved_re, precision=HIGH
    )
    return (spec_re, spec_im)


def forward_transform(signal):
    shards = lax.axis_size("seq")
    where = lax.axis_index("seq")
    stacks, block, width = signal.shape
    piece = block // shards
    total = 2 * shards * block
    spread = lax.all_to_all(
        signal.reshape(stacks, 1, block, width), "seq", split_axis=2, concat_axis=1, tiled=True
    )
    spread = spread.astype(jnp.float32)
    outer_re, outer_im = outer_tables(shards)
    global_pos = where * piece + jnp.arange(piece, dtype=jnp.int32)[None, :]
    part_re = jnp.einsum("kp,spjc->skjc", outer_re, spread, precision=HIGH)
    part_im = -jnp.einsum("kp,spjc->skjc", outer_im, spread, precision=HIGH)
    freq_idx = jnp.arange(2 * shards, dtype=jnp.int32)[:, None]
    angle = 2.0 * math.pi / total * (freq_idx * global_pos % total).astype(jnp.float32)
    twist_re = jnp.cos(angle)[:, :, None]
    twist_im = jnp.sin(angle)[:, :, None]
    turned_re = part_re * twist_re + part_im * twist_im
    turned_im = part_im * twist_re - part_re * twist_im
    moved = lax.all_to_all(
        jnp.stack([turned_re, turned_im]), "seq", split_axis=2, concat_axis=3, tiled=True
    )
    return inner_forward(moved[0], moved[1], block)


def inverse_transform(spec_re, spec_im):
    shards = lax.axis_size("seq")
    where = lax.axis_index("seq")
    stacks, pair, block, width = spec_re.shape
    total = 2 * shards * block
    inner_re, inner_im = inner_tables(block)
    back_re = jnp.einsum("jk,slkc->sljc", inner_re, spec_re, precision=HIGH) - jnp.einsum(
        "jk,slkc->sljc", inner_im, spec_im, precision=HIGH
    )
    back_im = jnp.einsum("jk,slkc->sljc", inner_im, spec_re, precision=HIGH) + jnp.einsum(
        "jk,slkc->sljc", inner_re, spec_im, precision=HIGH
    )
    positions = jnp.arange(block, dtype=jnp.int32)[None, :]
    outer_re, outer_im = outer_tables(shards)
    local_freq = 2 * where + jnp.arange(2, dtype=jnp.int32)[:, None]
    angle = 2.0 * math.pi / total * (local_freq * positions % total).astype(jnp.float32)
    twist_re = jnp.cos(angle)[:, :, None]
    twist_im = jnp.sin(angle)[:, :, None]
    turned_re = back_re * twist_re - back_im * twist_im
    turned_im = back_re * twist_im + back_im * twist_re
    moved = lax.all_to_all(
        jnp.stack([turned_re, turned_im]), "seq", split_axis=3, concat_axis=2, tiled=True
    )
    result = (
        jnp.einsum("kp,skjc->spjc", outer_re, moved[0], precision=HIGH)
        - jnp.einsum("kp,skjc->spjc", outer_im, moved[1], precision=HIGH)
    ) / total
    home = lax.all_to_all(
        result.astype(jnp.bfloat16), "seq", split_axis=1, concat_axis=2, tiled=True
    ).astype(result.dtype)
    return home.reshape(stacks, block, width)


def complex_mul(left_re, left_im, right_re, right_im):
    return (left_re * right_re - left_im * right_im, left_re * right_im + left_im * right_re)


def local(inputs, cotangent, value_weight, gate_weight, filter_taps):
    shards = lax.axis_size("seq")
    replicas = lax.axis_size("dp")
    stacks, block, width = inputs.shape
    scale = float(stacks * block * shards * replicas) ** (-0.5)
    value = jnp.einsum(
        "sjd,de->sje", inputs, value_weight, preferred_element_type=jnp.float32
    ).astype(jnp.bfloat16)
    gate = jnp.einsum("sjd,de->sje", inputs, gate_weight, preferred_element_type=jnp.float32)
    filt_re, filt_im = forward_transform(filter_taps[None])
    vals_re, vals_im = forward_transform(value)
    flip_re = vals_re[..., ::-1]
    flip_im = vals_im[..., ::-1]
    direct_re, direct_im = complex_mul(filt_re, filt_im, vals_re, vals_im)
    strand_re, strand_im = complex_mul(filt_re, -filt_im, flip_re, flip_im)
    mixed = inverse_transform(direct_re + strand_re, direct_im + strand_im)
    cot = cotangent.astype(jnp.float32)
    gate_grad = (cot * mixed).astype(jnp.bfloat16)
    mix_grad = (cot * gate).astype(jnp.bfloat16)
    grads_re, grads_im = forward_transform(mix_grad)
    conj_re, conj_im = complex_mul(filt_re, -filt_im, grads_re, grads_im)
    prod_re, prod_im = complex_mul(filt_re, filt_im, grads_re, grads_im)
    value_grad = inverse_transform(
        conj_re + prod_re[..., ::-1], conj_im + prod_im[..., ::-1]
    ).astype(jnp.bfloat16)
    input_grad = (
        jnp.einsum("sje,de->sjd", value_grad, value_weight, preferred_element_type=jnp.float32)
        + jnp.einsum("sje,de->sjd", gate_grad, gate_weight, preferred_element_type=jnp.float32)
    ).astype(jnp.bfloat16)
    joined = jnp.concatenate([value_grad, gate_grad], axis=-1).reshape(stacks * block, 2 * width)
    flat_in = inputs.reshape(stacks * block, width)
    row_sums = lax.psum_scatter(
        lax.dot_general(
            joined, flat_in, (((0,), (0,)), ((), ())), preferred_element_type=jnp.float32
        ),
        "seq",
        scatter_dimension=0,
        tiled=True,
    )
    projection_grads = (
        lax.psum_scatter(
            row_sums.astype(jnp.bfloat16), "dp", scatter_dimension=1, tiled=True
        ).astype(jnp.float32)
        * scale
    )
    first_re, first_im = complex_mul(vals_re, -vals_im, grads_re, grads_im)
    second_re, second_im = complex_mul(grads_re, -grads_im, flip_re, flip_im)
    spec_re = jnp.sum(first_re + second_re, axis=0, keepdims=True)
    spec_im = jnp.sum(first_im + second_im, axis=0, keepdims=True)
    partial_value = inverse_transform(spec_re, spec_im)[0]
    filter_grad = lax.psum(partial_value.astype(jnp.bfloat16), "dp").astype(jnp.float32) * scale
    return (input_grad, projection_grads, filter_grad)


def solution(mesh):
    in_specs = (P("dp", "seq", None), P("dp", "seq", None), P(), P(), P("seq", None))
    out_specs = (P("dp", "seq", None), P("seq", "dp"), P("seq", None))
    return jax.shard_map(local, mesh=mesh, in_specs=in_specs, out_specs=out_specs, check_vma=False)
```

profile of v0, /device:TPU:32, one launch (start us, length us, event | category | flops | bytes accessed | tf_op | source)
XLA Modules:
  0.0 1256.7 jit_solution(11650748903448661819)
XLA Ops:
  15.0 12.4 all-to-all-start.6
  51.5 7.9 all-to-all-done.2
  59.3 7.4 all-to-all-start
  91.5 10.4 all-to-all-start.1
  106.8 44.6 %all-to-all-done.1 = f32[2,1,256,1,1024]{4,3,1,0,2:T(1,128)} async-done(((f32[2,1,256,1,1024]{4,3,1,0,2:T(1,128)}), f32[2,1,256,1,1024]{4,3,1,0,2:T(1,128)}, u32[]{:S(2)}, u32[]{:S(2)}) %all-to-all-start.1) | async-done | bytes 2097184 | tf_op jit(solution)/shard_map/all_to_all | solution.py:55
  151.4 9.6 all-to-all-start.7
  165.9 44.7 %all-to-all-done.7 = f32[2,1,256,1,1024]{4,3,1,0,2:T(1,128)} async-done(((f32[2,1,256,1,1024]{4,3,1,0,2:T(1,128)}), f32[2,1,256,1,1024]{4,3,1,0,2:T(1,128)}, u32[]{:S(2)}, u32[]{:S(2)}) %all-to-all-start.7) | async-done | bytes 2097184 | tf_op jit(solution)/shard_map/all_to_all | solution.py:55
  210.6 10.2 all-to-all-start.3
  246.5 23.7 %all-to-all-done.3 = f32[2,1,256,1,1024]{4,3,1,0,2:T(1,128)} async-done(((f32[2,1,256,1,1024]{4,3,1,0,2:T(1,128)}), f32[2,1,256,1,1024]{4,3,1,0,2:T(1,128)}, u32[]{:S(2)}, u32[]{:S(2)}) %all-to-all-start.3) | async-done | bytes 2097184 | tf_op jit(solution)/shard_map/all_to_all | solution.py:55
  301.5 8.9 rev.14
  310.4 8.6 add_add_fusion
  319.0 8.9 rev.12
  327.9 9.0 rev.13
  363.3 9.5 all-to-all-start.8
  379.8 42.7 %all-to-all-done.8 = f32[2,1,2,128,1024]{4,2,1,0,3:T(2,128)} async-done(((f32[2,1,2,128,1024]{4,2,1,0,3:T(2,128)}), f32[2,1,2,128,1024]{4,2,1,0,3:T(2,128)}, u32[]{:S(2)}, u32[]{:S(2)}) %all-to-all-start.8) | async-done | bytes 2097184 | tf_op jit(solution)/shard_map/all_to_all | solution.py:81
  422.5 9.9 all-to-all-start.4
  448.5 33.3 %all-to-all-done.4 = f32[2,1,2,128,1024]{4,2,1,0,3:T(2,128)} async-done(((f32[2,1,2,128,1024]{4,2,1,0,3:T(2,128)}), f32[2,1,2,128,1024]{4,2,1,0,3:T(2,128)}, u32[]{:S(2)}, u32[]{:S(2)}) %all-to-all-start.4) | async-done | bytes 2097184 | tf_op jit(solution)/shard_map/all_to_all | solution.py:81
  481.8 10.1 all-to-all-start.9
  507.9 12.0 all-to-all-start.5
  523.2 9.0 all-to-all-done.5
  545.3 67.0 %all_to_all.153 = f32[2,1,2,128,1024]{4,2,1,0,3:T(2,128)S(1)} all-to-all(f32[2,1,2,128,1024]{4,2,1,0,3:T(2,128)} %copy.74), channel_id=1, replica_groups=mesh['seq'=128,'dp'=2] {'seq'}, dimensions={3} | all-to-all | bytes 4194304 | tf_op jit(solution)/shard_map/all_to_all | solution.py:81
  629.4 20.9 %all_to_all.154 = bf16[128,2,512]{2,1,0:T(2,128)(2,1)} all-to-all(bf16[128,2,512]{2,1,0:T(2,128)(2,1)S(1)} %reshape.418), channel_id=1, replica_groups=mesh['seq'=128,'dp'=2] {'seq'}, dimensions={0} | all-to-all | bytes 524288 | tf_op jit(solution)/shard_map/all_to_all | solution.py:88
  656.5 567.0 %reduce-scatter.3.cloned.1.call-done = f32[16,1024]{1,0:T(8,128)} async-done(((f32[2048,1024]{1,0:T(8,128)}), f32[16,1024]{1,0:T(8,128)}) %reduce-scatter.3.cloned.1.call-update) | async-done | bytes 65552 | tf_op jit(solution)/shard_map/reduce_scatter | solution.py:129
  1226.9 20.9 %reduce-scatter.5.cloned.1.call-done = bf16[16,512]{1,0:T(8,128)(2,1)} async-done(((bf16[16,1024]{1,0:T(8,128)(2,1)}), bf16[16,512]{1,0:T(8,128)(2,1)}) %reduce-scatter.5.cloned.1.call-update) | async-done | bytes 16400 | tf_op jit(solution)/shard_map/reduce_scatter | solution.py:138
  (160 shorter events, 231.8 us)
Async XLA Ops:
  8.0 19.4 %copy-start.17 = (bf16[1,128,1024]{2,1,0:T(8,128)(2,1)S(1)}, bf16[1,128,1024]{2,1,0:T(8,128)(2,1)}, u32[]{:S(2)}) copy-start(bf16[1,128,1024]{2,1,0:T(8,128)(2,1)} %param.5) | copy-start | bytes 786436
  8.0 19.4 %copy-start.21 = (bf16[1,128,1024]{2,1,0:T(8,128)(2,1)S(1)}, bf16[1,128,1024]{2,1,0:T(8,128)(2,1)}, u32[]{:S(2)}) copy-start(bf16[1,128,1024]{2,1,0:T(8,128)(2,1)} %param.6) | copy-start | bytes 786436
  15.0 24.8 %all-to-all-start.6 = ((bf16[128,2,512]{2,1,0:T(2,128)(2,1)}), bf16[128,2,512]{2,1,0:T(2,128)(2,1)S(1)}, u32[]{:S(2)}, u32[]{:S(2)}) async-start(bf16[128,2,512]{2,1,0:T(2,128)(2,1)} %reshape.414), calls=%async_computation.6 | async-start | bytes 524288 | tf_op jit(solution)/shard_map/all_to_all | solution.py:41
  29.5 17.5 %copy-start.22 = (bf16[128,1024]{1,0:T(8,128)(2,1)S(1)}, bf16[128,1024]{1,0:T(8,128)(2,1)}, u32[]{:S(2)}) copy-start(bf16[128,1024]{1,0:T(8,128)(2,1)} %param.9) | copy-start | bytes 786436
  39.7 19.6 %all-to-all-start.2 = ((bf16[128,2,512]{2,1,0:T(2,128)(2,1)}), bf16[128,2,512]{2,1,0:T(2,128)(2,1)S(1)}, u32[]{:S(2)}, u32[]{:S(2)}) async-start(bf16[128,2,512]{2,1,0:T(2,128)(2,1)} %reshape.410), calls=%async_computation.2 | async-start | bytes 524288 | tf_op jit(solution)/shard_map/all_to_all | solution.py:41
  59.3 19.8 %all-to-all-start = ((bf16[128,2,512]{2,1,0:T(2,128)(2,1)}), bf16[128,2,512]{2,1,0:T(2,128)(2,1)S(1)}, u32[]{:S(2)}, u32[]{:S(2)}) async-start(bf16[128,2,512]{2,1,0:T(2,128)(2,1)} %reshape.408), calls=%async_computation | async-start | bytes 524288 | tf_op jit(solution)/shard_map/all_to_all | solution.py:41
  67.7 5.3 copy-start.19
  67.7 7.3 copy-start.20
  91.5 10.4 copy-start.14
  91.5 59.9 %all-to-all-start.1 = ((f32[2,1,256,1,1024]{4,3,1,0,2:T(1,128)}), f32[2,1,256,1,1024]{4,3,1,0,2:T(1,128)}, u32[]{:S(2)}, u32[]{:S(2)}) async-start(f32[2,1,256,1,1024]{4,3,1,0,2:T(1,128)} %copy.57), calls=%async_computation.1 | async-start | bytes 4194304 | tf_op jit(solution)/shard_map/all_to_all | solution.py:55
  106.8 54.2 %copy-start.13 = (f32[1,1,256,1,1024]{4,2,3,1,0:T(8,128)S(1)}, f32[1,1,256,1,1024]{4,2,3,1,0:T(8,128)}, u32[]{:S(2)}) copy-start(f32[1,1,256,1,1024]{4,2,3,1,0:T(8,128)} %get-tuple-element.35) | copy-start | bytes 3145732
  151.4 59.2 %all-to-all-start.7 = ((f32[2,1,256,1,1024]{4,3,1,0,2:T(1,128)}), f32[2,1,256,1,1024]{4,3,1,0,2:T(1,128)}, u32[]{:S(2)}, u32[]{:S(2)}) async-start(f32[2,1,256,1,1024]{4,3,1,0,2:T(1,128)} %copy.69), calls=%async_computation.7 | async-start | bytes 4194304 | tf_op jit(solution)/shard_map/all_to_all | solution.py:55
  210.6 59.6 %all-to-all-start.3 = ((f32[2,1,256,1,1024]{4,3,1,0,2:T(1,128)}), f32[2,1,256,1,1024]{4,3,1,0,2:T(1,128)}, u32[]{:S(2)}, u32[]{:S(2)}) async-start(f32[2,1,256,1,1024]{4,3,1,0,2:T(1,128)} %copy.62), calls=%async_computation.3 | async-start | bytes 4194304 | tf_op jit(solution)/shard_map/all_to_all | solution.py:55
  237.2 4.8 copy-start.1
  292.5 9.1 copy-start.7
  363.3 59.2 %all-to-all-start.8 = ((f32[2,1,2,128,1024]{4,2,1,0,3:T(2,128)}), f32[2,1,2,128,1024]{4,2,1,0,3:T(2,128)}, u32[]{:S(2)}, u32[]{:S(2)}) async-start(f32[2,1,2,128,1024]{4,2,1,0,3:T(2,128)} %copy.71), calls=%async_computation.8 | async-start | bytes 4194304 | tf_op jit(solution)/shard_map/all_to_all | solution.py:81
  422.5 59.3 %all-to-all-start.4 = ((f32[2,1,2,128,1024]{4,2,1,0,3:T(2,128)}), f32[2,1,2,128,1024]{4,2,1,0,3:T(2,128)}, u32[]{:S(2)}, u32[]{:S(2)}) async-start(f32[2,1,2,128,1024]{4,2,1,0,3:T(2,128)} %copy.64), calls=%async_computation.4 | async-start | bytes 4194304 | tf_op jit(solution)/shard_map/all_to_all | solution.py:81
  481.8 26.1 %all-to-all-start.9 = ((bf16[128,2,512]{2,1,0:T(2,128)(2,1)}), bf16[128,2,512]{2,1,0:T(2,128)(2,1)}, u32[]{:S(2)}, u32[]{:S(2)}) async-start(bf16[128,2,512]{2,1,0:T(2,128)(2,1)} %reshape.416), calls=%async_computation.9 | async-start | bytes 524288 | tf_op jit(solution)/shard_map/all_to_all | solution.py:88
  507.9 24.6 %copy-start.18 = (bf16[1,128,1024]{2,1,0:T(8,128)(2,1)S(1)}, bf16[1,128,1024]{2,1,0:T(8,128)(2,1)}, u32[]{:S(2)}) copy-start(bf16[1,128,1024]{2,1,0:T(8,128)(2,1)} %param.5) | copy-start | bytes 786436
  507.9 24.3 %all-to-all-start.5 = ((bf16[128,2,512]{2,1,0:T(2,128)(2,1)}), bf16[128,2,512]{2,1,0:T(2,128)(2,1)S(1)}, u32[]{:S(2)}, u32[]{:S(2)}) async-start(bf16[128,2,512]{2,1,0:T(2,128)(2,1)} %reshape.412), calls=%async_computation.5 | async-start | bytes 524288 | tf_op jit(solution)/shard_map/all_to_all | solution.py:88
  519.9 703.7 %reduce-scatter.3.cloned.1.call-start = ((), (), s32[]{:S(2)}) async-start(), calls=%async_computation.14 | async-start | bytes 8454144 | tf_op jit(solution)/shard_map/reduce_scatter | solution.py:129
  537.1 688.0 %all-reduce.2.cloned.1.call-start = ((), (), s32[]{:S(2)}) async-start(), calls=%async_computation.16 | async-start | bytes 524288 | tf_op jit(solution)/shard_map/psum | solution.py:148
  624.0 29.4 %copy-start.16 = (bf16[128,1,1,1024]{3,2,1,0:T(2,128)(2,1)S(1)}, bf16[128,1,1,1024]{3,2,1,0:T(2,128)(2,1)}, u32[]{:S(2)}) copy-start(bf16[128,1,1,1024]{3,2,1,0:T(2,128)(2,1)} %copy-done.15) | copy-start | bytes 786436
  653.3 594.5 %reduce-scatter.5.cloned.1.call-start = ((), (), s32[]{:S(2)}) async-start(), calls=%async_computation.15 | async-start | bytes 49152 | tf_op jit(solution)/shard_map/reduce_scatter | solution.py:138
  (12 other events, 32.0 us)
Sparse Core Ops, SparseCore 0:
  537.2 686.2 reduce-scatter.2
Sparse Core Ops, SparseCore 1:
  653.4 41.4 all-reduce.1
  1225.1 22.6 reduce-scatter.4
where the time goes:
time: 1270 us; the launch traced here: 1260 us
  waiting for transfers between devices  803 us (63%)
  local copies, waits for them, and re-layouts  121 us (10%)
  starting transfers between devices  98.9 us (8%)
  matrix products  97.9 us (8%)
  blocking collectives  87.9 us (7%)
  other arithmetic  32.5 us (3%)
  between operations  16.3 us (1%)
    reduce_scatter x1, waiting for transfers between devices, local(): lax.psum_scatter(lax.dot_general(joined, flat_in, (((0,), (0,)), ((), ())...  567 us
    all_to_all x3, waiting for transfers between devices, forward_transform(): lax.all_to_all(jnp.stack([turned_re, turned_im]), 'seq', split_axis=2, co...  113 us
    all_to_all x2, waiting for transfers between devices, inverse_transform(): lax.all_to_all(jnp.stack([turned_re, turned_im]), 'seq', split_axis=3, co...  76 us
    all_to_all x1, blocking collectives, inverse_transform(): lax.all_to_all(jnp.stack([turned_re, turned_im]), 'seq', split_axis=3, co...  67 us
    all_to_all x3, starting transfers between devices, forward_transform(): lax.all_to_all(jnp.stack([turned_re, turned_im]), 'seq', split_axis=2, co...  30.1 us
    unnamed x64, local copies, waits for them, and re-layouts  29.9 us
    all_to_all x3, starting transfers between devices, forward_transform(): lax.all_to_all(signal.reshape(stacks, 1, block, width), 'seq', split_axis...  27.1 us
  transfers between devices with their start and end apart: 13, of which 11 were waited for; matrix products, arithmetic and copies ran while one was open for 10% of the time, Pallas kernels for 0%

commit v1 on v0

v1 whole, which is shorter than its diff:
```python
import math

import jax
import jax.numpy as jnp
import numpy as np
from jax import lax
from jax.experimental import pallas as pl
from jax.experimental.pallas import tpu as pltpu
from jax.sharding import Mesh, PartitionSpec as P

F32 = jnp.float32
BF16 = jnp.bfloat16
D = 1024
L = 16384
SIDE = 128
CHIPS = 64
ARRS = 3
ROWS = ARRS * 8
SEQ = ("x", "y", "z", "c")
RING = ("x", "y", "z")
VMEM = pl.BlockSpec(memory_space=pltpu.VMEM)
SMEM = pl.BlockSpec(memory_space=pltpu.SMEM)
PARAMS = pltpu.CompilerParams(vmem_limit_bytes=56 * 1024 * 1024)


def owned(core):
    chans = np.zeros((CHIPS, 8), np.int64)
    q = 4 * np.arange(CHIPS)[:, None] + np.arange(4)[None, :]
    chans[:, :4] = 32 * (q // 16) + 16 * core + q % 16
    chans[:, 4:] = D - 1 - chans[:, :4]
    return chans.reshape(-1)


def one_hot_rows(index, width):
    return (index[:, None] == np.arange(width)[None, :]).astype(jnp.bfloat16)


def channel_order():
    return np.stack([one_hot_rows(owned(core), D) for core in range(2)])


def block_order():
    chans = owned(0)
    order = []
    for m in range(32):
        half = 0 if m < 16 else 1
        for i in range(16):
            order.append(int(np.nonzero(chans == 32 * m + 16 * half + i)[0][0]))
    return one_hot_rows(np.array(order), 512)


def tables():
    k = np.arange(SIDE)
    quarter = k + 0.25
    outer = 2 * math.pi / SIDE * np.outer(quarter, k)
    both = np.concatenate([np.cos(outer), -np.sin(outer)], axis=0)
    swapped = both.reshape(2 * SIDE, CHIPS, 2)[:, :, ::-1].reshape(2 * SIDE, SIDE)
    outer_table = np.stack([both, swapped])
    twist = 2 * math.pi / L * np.outer(quarter, k)
    inner = 2 * math.pi / SIDE * np.outer(k, k)
    cos, sin = np.cos(inner), np.sin(inner)
    inner_table = np.block([[cos, -sin], [sin, cos]])
    return (
        outer_table.astype(jnp.bfloat16),
        outer_table.transpose(0, 2, 1).astype(jnp.bfloat16),
        np.cos(twist).astype(np.float32),
        np.sin(twist).astype(np.float32),
        inner_table.astype(jnp.bfloat16),
        inner_table.T.astype(jnp.bfloat16),
    )


def dot(a, b, ca=1, cb=0):
    return lax.dot_general(a, b, (((ca,), (cb,)), ((), ())), preferred_element_type=F32)


def project_kernel(core, inputs, cot, taps, value_w, gate_w, order, keep, give, cot_keep, cot_give):
    value = dot(inputs[...], value_w[...]).astype(BF16)
    gate = dot(inputs[...], gate_w[...])
    mix = (cot[...].astype(F32) * gate).astype(BF16)
    stacked = jnp.concatenate([value, mix, taps[...], cot[...]], axis=0)
    for side, (out, cot_out) in enumerate(((keep, cot_keep), (give, cot_give))):
        pick = order[core[0] ^ side]
        moved = dot(pick, stacked, 1, 1)
        parts = [moved[:, a * SIDE:(a + 1) * SIDE].reshape(CHIPS, 8, SIDE) for a in range(3)]
        out[...] = jnp.concatenate(parts, axis=1).reshape(CHIPS * ROWS, SIDE).astype(BF16)
        cot_out[...] = moved[:, 3 * SIDE:].astype(BF16)


def convolve_kernel(core, signal, outer, outer_t, tw_re, tw_im, inner, inner_t, result, flat, spec):
    flat[...] = signal[...].astype(F32)
    outer_m = outer[core[0]]
    outer_tm = outer_t[core[0]]
    cos = tw_re[...]
    sin = tw_im[...]
    inner_m = inner[...]
    inner_tm = inner_t[...]

    for j in range(ROWS):
        sig = flat[pl.ds(j, SIDE, stride=ROWS), :].astype(BF16)
        part = dot(outer_m, sig)
        re, im = part[:SIDE], part[SIDE:]
        turned = jnp.concatenate([re * cos + im * sin, im * cos - re * sin], axis=1)
        spec[j] = dot(turned.astype(BF16), inner_m)

    def back(j, re, im):
        both = jnp.concatenate([re, im], axis=1).astype(BF16)
        part = dot(both, inner_tm)
        re, im = part[:, :SIDE], part[:, SIDE:]
        turned = jnp.concatenate([re * cos - im * sin, re * sin + im * cos], axis=0)
        out = dot(outer_tm, turned.astype(BF16))
        flat[pl.ds(j, SIDE, stride=ROWS), :] = out * (1.0 / L)

    def mul(a, b):
        return (a[0] * b[0] - a[1] * b[1], a[0] * b[1] + a[1] * b[0])

    def mulc(a, b):
        return (a[0] * b[0] + a[1] * b[1], a[0] * b[1] - a[1] * b[0])

    def add(a, b):
        return (a[0] + b[0], a[1] + b[1])

    def load(j):
        both = spec[j]
        return (both[:, :SIDE], both[:, SIDE:])

    for s in range(8):
        t = (s + 4) % 8
        vals, grads, filt = load(s), load(8 + s), load(16 + s)
        vals_f, grads_f, filt_f = load(t), load(8 + t), load(16 + t)
        back(s, *add(mul(filt, vals), mulc(filt, vals_f)))
        back(8 + s, *add(mulc(filt, grads), mul(filt_f, grads_f)))
        back(16 + s, *add(mulc(vals, grads), mulc(grads, vals_f)))
    result[...] = flat[...].astype(BF16)


def weights_kernel(home, cot_own, cot_other, in_own, in_other, blocks, partial):
    full = home[...].astype(F32).reshape(CHIPS, 2 * ROWS, SIDE)
    sides = []
    for side, cot in ((0, cot_own), (1, cot_other)):
        base = side * ROWS
        mixed = full[:, base:base + 8].reshape(512, SIDE)
        grad = full[:, base + 8:base + 16].reshape(512, SIDE).astype(BF16)
        gated = (mixed * cot[...].astype(F32)).astype(BF16)
        sides.append((grad, gated))
    for a in range(2):
        rows = jnp.concatenate([sides[0][a], sides[1][a]], axis=1)
        rows = dot(blocks[...], rows).astype(BF16)
        total = dot(rows[:, :SIDE], in_own[...]) + dot(rows[:, SIDE:], in_other[...])
        partial[a * 512:(a + 1) * 512, :] = total.astype(BF16)


def inputs_kernel(core, own, other, cot, value_w, gate_w, order, input_grad, filter_part):
    near = own[...].astype(F32).reshape(CHIPS, ROWS, SIDE)
    far = other[...].astype(F32).reshape(CHIPS, ROWS, SIDE)
    natural = 0.0
    for side, full in ((0, near), (1, far)):
        stacked = jnp.concatenate(
            [full[:, a * 8:(a + 1) * 8].reshape(512, SIDE) for a in range(3)], axis=1
        ).astype(BF16)
        natural = natural + dot(stacked, order[core[0] ^ side], 0, 0)
    gated = (natural[:SIDE] * cot[...].astype(F32)).astype(BF16)
    grad = natural[SIDE:2 * SIDE].astype(BF16)
    filter_part[...] = natural[2 * SIDE:].astype(BF16)
    total = dot(grad, value_w[...], 1, 1) + dot(gated, gate_w[...], 1, 1)
    input_grad[...] = total.astype(BF16)


def shape(rows, cols, kind=BF16):
    return jax.ShapeDtypeStruct((rows, cols), kind)


def swap_cores(a):
    return lax.ppermute(a, "c", [(0, 1), (1, 0)])


def local(inputs, cotangent, value_weight, gate_weight, filter_taps):
    core = lax.axis_index("c").astype(jnp.int32).reshape(1)
    order = jnp.asarray(channel_order())
    flat_in = inputs.reshape(SIDE, D)
    cot = cotangent.reshape(SIDE, D)
    scale = float(2 * L) ** (-0.5)

    keep, give, cot_keep, cot_give = pl.pallas_call(
        project_kernel,
        out_shape=[shape(CHIPS * ROWS, SIDE)] * 2 + [shape(512, SIDE)] * 2,
        in_specs=[SMEM] + [VMEM] * 6,
        out_specs=[VMEM] * 4,
        compiler_params=PARAMS,
        name="project",
    )(core, flat_in, cot, filter_taps, value_weight, gate_weight, order)
    got = swap_cores(give)
    message = jnp.concatenate(
        [keep.reshape(CHIPS, ROWS, SIDE), got.reshape(CHIPS, ROWS, SIDE)], axis=1
    )
    spread = lax.all_to_all(message, RING, 0, 0, tiled=True)
    in_other = swap_cores(flat_in)
    cot_other = swap_cores(cot_give)

    result = pl.pallas_call(
        convolve_kernel,
        out_shape=shape(2 * CHIPS * ROWS, SIDE),
        in_specs=[SMEM] + [VMEM] * 7,
        out_specs=VMEM,
        scratch_shapes=[
            pltpu.VMEM((2 * CHIPS * ROWS, SIDE), F32),
            pltpu.VMEM((ROWS, SIDE, 2 * SIDE), F32),
        ],
        compiler_params=PARAMS,
        name="convolve",
    )(core, spread.reshape(2 * CHIPS * ROWS, SIDE), *[jnp.asarray(t) for t in tables()])
    home = lax.all_to_all(result.reshape(CHIPS, 2 * ROWS, SIDE), RING, 0, 0, tiled=True)

    partial = pl.pallas_call(
        weights_kernel,
        out_shape=shape(D, D),
        in_specs=[VMEM] * 6,
        out_specs=VMEM,
        compiler_params=PARAMS,
        name="weights",
    )(home.reshape(2 * CHIPS * ROWS, SIDE), cot_keep, cot_other, flat_in, in_other, jnp.asarray(block_order()))
    far = swap_cores(home[:, ROWS:].reshape(CHIPS * ROWS, SIDE))
    pieces = lax.all_to_all(partial, ("x", "y"), 0, 0, tiled=True)

    input_grad, filter_part = pl.pallas_call(
        inputs_kernel,
        out_shape=[shape(SIDE, D), shape(SIDE, D)],
        in_specs=[SMEM] + [VMEM] * 6,
        out_specs=[VMEM] * 2,
        compiler_params=PARAMS,
        name="input_grad",
    )(core, home[:, :ROWS].reshape(CHIPS * ROWS, SIDE), far, cot, value_weight, gate_weight, order)
    filter_other = lax.ppermute(filter_part, "dp", [(0, 1), (1, 0)])
    filter_grad = (filter_part.astype(F32) + filter_other.astype(F32)) * scale

    sums = jnp.sum(pieces.reshape(16, 64, D).astype(F32), axis=0).astype(BF16)
    sums = sums.reshape(4, 16, 2, 512).transpose(0, 2, 1, 3).reshape(8, 16, 512)
    final = lax.all_to_all(sums, ("z", "dp"), 0, 0, tiled=True)
    rows = jnp.sum(final.astype(F32), axis=0) * scale
    pairs = [(2 * x + c, 2 * x + (c ^ (x & 1))) for x in range(4) for c in range(2)]
    projection_grads = lax.ppermute(rows, ("x", "c"), pairs)
    return (input_grad.reshape(1, SIDE, D), projection_grads, filter_grad)


def solution(mesh):
    fine = Mesh(mesh.devices.reshape(4, 4, 4, 2, 2), ("x", "y", "z", "c", "dp"))
    in_specs = (P("dp", SEQ, None), P("dp", SEQ, None), P(), P(), P(SEQ, None))
    out_specs = (P("dp", SEQ, None), P(SEQ, "dp"), P(SEQ, None))
    return jax.shard_map(local, mesh=fine, in_specs=in_specs, out_specs=out_specs, check_vma=False)
```

time: 1270 us -> 146 us (0.11)
  waiting for transfers between devices: 803 us -> 58.2 us
  local copies, waits for them, and re-layouts: 121 us -> 3.86 us
  matrix products: 97.9 us -> 0 us
  starting transfers between devices: 98.9 us -> 22.2 us
  blocking collectives: 87.9 us -> 34.9 us
  other arithmetic: 32.5 us -> 3.32 us
  Pallas kernels: 0 us -> 21.7 us
  between operations: 16.3 us -> 0.73 us
    reduce_scatter x2 -> x0, waiting for transfers between devices: 588 us -> none  [the longest x1 567 us: local(): lax.psum_scatter(lax.dot_general(joined, flat_in, (((0,), (0,)), ((), ())...]
    all_to_all x10 -> x3, waiting for transfers between devices: 215 us -> 48.4 us  [the longest x1 27.9 us: local(): pieces = lax.all_to_all(partial, ('x', 'y'), 0, 0, tiled=True)]
    dot_general x41 -> x0, matrix products: 97.9 us -> none  [the longest x3 15.8 us: inner_forward(): jnp.einsum('kj,sljc->slkc', inner_im, moved_im, precision=HIGH)]
    all_to_all x10 -> x3, starting transfers between devices: 98.8 us -> 16.5 us  [the longest x1 7.05 us: local(): final = lax.all_to_all(sums, ('z', 'dp'), 0, 0, tiled=True)]
    all_to_all x2 -> x1, blocking collectives: 87.9 us -> 34.9 us  [local(): spread = lax.all_to_all(message, RING, 0, 0, tiled=True)]
    another operation x13 -> x0, local copies, waits for them, and re-layouts: 34.6 us -> none  [the longest x3 12.6 us: inverse_transform(): jnp.stack([turned_re, turned_im])]
    rev x4 -> x0, local copies, waits for them, and re-layouts: 32 us -> none  [the longest x1 9.02 us: local(): prod_im[..., ::-1]]
    unnamed x64 -> x15, local copies, waits for them, and re-layouts: 29.9 us -> 2.28 us
  transfers between devices with their start and end apart: 13 -> 9, of which waited for: 11 -> 5; matrix products, arithmetic and copies ran while one was open for 10% -> 3% of each run, Pallas kernels for 0% -> 4%
where the time goes in v1:
time: 146 us; the launch traced here: 145 us
  waiting for transfers between devices  58.2 us (40%)
  blocking collectives  34.9 us (24%)
  starting transfers between devices  22.2 us (15%)
  Pallas kernels  21.7 us (15%)
  local copies, waits for them, and re-layouts  3.86 us (3%)
  other arithmetic  3.32 us (2%)
    all_to_all x1, blocking collectives, local(): spread = lax.all_to_all(message, RING, 0, 0, tiled=True)  34.9 us
    all_to_all x1, waiting for transfers between devices, local(): pieces = lax.all_to_all(partial, ('x', 'y'), 0, 0, tiled=True)  27.9 us
    all_to_all x1, waiting for transfers between devices, local(): lax.all_to_all(result.reshape(CHIPS, 2 * ROWS, SIDE), RING, 0, 0, tiled=T...  20.5 us
    all_to_all x1, starting transfers between devices, local(): final = lax.all_to_all(sums, ('z', 'dp'), 0, 0, tiled=True)  7.05 us
    ppermute x1, waiting for transfers between devices, local(): filter_other = lax.ppermute(filter_part, 'dp', [(0, 1), (1, 0)])  6.67 us
    pallas_call x1, Pallas kernels, local(): pl.pallas_call(inputs_kernel, out_shape=[shape(SIDE, D), shape(SIDE, D)],...  6.19 us
    pallas_call x1, Pallas kernels, local(): pl.pallas_call(project_kernel, out_shape=[shape(CHIPS * ROWS, SIDE)] * 2...  5.8 us
    all_to_all x1, starting transfers between devices, local(): lax.all_to_all(result.reshape(CHIPS, 2 * ROWS, SIDE), RING, 0, 0, tiled=T...  5.55 us
  transfers between devices with their start and end apart: 9, of which 5 were waited for; matrix products, arithmetic and copies ran while one was open for 3% of the time, Pallas kernels for 4%

profile of v1, /device:TPU:32, one launch (start us, length us, event | category | flops | bytes accessed | tf_op | source)
XLA Modules:
  0.0 144.9 jit_solution(2903012262253607770)
XLA Ops:
  0.6 5.8 %project.1 = (bf16[1536,128]{1,0:T(8,128)(2,1)}, bf16[1536,128]{1,0:T(8,128)(2,1)}, bf16[512,128]{1,0:T(8,128)(2,1)}, bf16[512,128]{1,0:T(8,128)(2,1)}) custom-call(s32[1]{0:T(128)} %bitcast.core, bf16[128,1024]{1,0:T(8,128)(2,1)} %bitcast.19, bf16[128,1024]{1,0:T(8,128)(2,1)} %bitcast.22, bf16[128,1024]{1,0:T(8,128)(2,1)} %taps.1, ...), custom_call_target="tpu_custom_call" | custom-call | tf_op jit(solution)/shard_map/project/pallas_call | solution.py:184
  6.4 1.9 %collective-permute-done = bf16[1536,128]{1,0:T(8,128)(2,1)S(1)} collective-permute-done((bf16[1536,128]{1,0:T(8,128)(2,1)}, bf16[1536,128]{1,0:T(8,128)(2,1)S(1)}, u32[]{:S(2)}, u32[]{:S(2)}) %collective-permute-start) | collective-permute-done | bytes 393248 | tf_op jit(solution)/shard_map/ppermute | solution.py:174
  8.4 1.1 pad_maximum_fusion
  9.5 34.9 %all_to_all.24 = bf16[64,48,128]{2,1,0:T(8,128)(2,1)} all-to-all(bf16[64,48,128]{2,1,0:T(8,128)(2,1)S(1)} %pad_maximum_fusion), channel_id=1, replica_groups=mesh['x'=4,'y'=4,'z'=4,'c'=2,'dp'=2] {'x','y','z'}, dimensions={0} | all-to-all | bytes 1572864 | tf_op jit(solution)/shard_map/all_to_all | solution.py:196
  44.3 5.0 %convolve.1 = bf16[3072,128]{1,0:T(8,128)(2,1)} custom-call(s32[1]{0:T(128)} %bitcast.core, bf16[3072,128]{1,0:T(8,128)(2,1)} %bitcast.17, bf16[2,256,128]{2,1,0:T(8,128)(2,1)} %constant.28.clone.outer, bf16[2,128,256]{2,1,0:T(8,128)(2,1)} %constant.29.clone.outer_t, f32[128,128]{1,0:T(8,128)} %constant.30.clone.tw_re, f32[128,128]{1,0:T(8,128)} %constant.31.clone.tw_im, ...), custom_call_target="tpu_custom_call" | custom-call | tf_op jit(solution)/shard_map/convolve/pallas_call | solution.py:200
  49.4 5.6 %all-to-all-start.1 = ((bf16[64,48,128]{2,1,0:T(8,128)(2,1)}), bf16[64,48,128]{2,1,0:T(8,128)(2,1)S(1)}, u32[]{:S(2)}, u32[]{:S(2)}) async-start(bf16[64,48,128]{2,1,0:T(8,128)(2,1)} %bitcast.16), calls=%async_computation.1 | async-start | bytes 1572864 | tf_op jit(solution)/shard_map/all_to_all | solution.py:212
  55.0 0.5 collective-permute-start.2
  55.5 1.2 collective-permute-done.2.cot_other
  56.7 20.5 %all-to-all-done.1 = bf16[64,48,128]{2,1,0:T(8,128)(2,1)S(1)} async-done(((bf16[64,48,128]{2,1,0:T(8,128)(2,1)}), bf16[64,48,128]{2,1,0:T(8,128)(2,1)S(1)}, u32[]{:S(2)}, u32[]{:S(2)}) %all-to-all-start.1) | async-done | bytes 786464 | tf_op jit(solution)/shard_map/all_to_all | solution.py:212
  77.3 0.9 copy-done
  78.2 4.7 %weights.1 = bf16[1024,1024]{1,0:T(8,128)(2,1)} custom-call(bf16[3072,128]{1,0:T(8,128)(2,1)} %bitcast.15, bf16[512,128]{1,0:T(8,128)(2,1)} %get-tuple-element.12.cot_own, bf16[512,128]{1,0:T(8,128)(2,1)} %copy-done.5, bf16[128,1024]{1,0:T(8,128)(2,1)} %bitcast.20, bf16[128,1024]{1,0:T(8,128)(2,1)} %copy-done.4, bf16[512,512]{1,0:T(8,128)(2,1)} %constant.34.clone.blocks), custom_call_target="tpu_custom_call" | custom-call | tf_op jit(solution)/shard_map/weights/pallas_call | solution.py:214
  82.8 3.8 %all-to-all-start.2 = ((bf16[16,64,1024]{2,1,0:T(8,128)(2,1)}), bf16[16,64,1024]{2,1,0:T(8,128)(2,1)S(1)}, u32[]{:S(2)}, u32[]{:S(2)}) async-start(bf16[16,64,1024]{2,1,0:T(8,128)(2,1)} %bitcast.14), calls=%async_computation.2 | async-start | bytes 4194304 | tf_op jit(solution)/shard_map/all_to_all | solution.py:223
  86.7 0.8 fusion
  87.5 27.9 %all-to-all-done.2 = bf16[16,64,1024]{2,1,0:T(8,128)(2,1)S(1)} async-done(((bf16[16,64,1024]{2,1,0:T(8,128)(2,1)}), bf16[16,64,1024]{2,1,0:T(8,128)(2,1)S(1)}, u32[]{:S(2)}, u32[]{:S(2)}) %all-to-all-start.2) | async-done | bytes 2097184 | tf_op jit(solution)/shard_map/all_to_all | solution.py:223
  115.4 0.4 reduce_sum.21
  115.9 0.7 copy.16
  116.6 7.1 %all-to-all-start.3 = ((bf16[8,16,512]{2,1,0:T(8,128)(2,1)}), bf16[8,16,512]{2,1,0:T(8,128)(2,1)S(1)}, u32[]{:S(2)}, u32[]{:S(2)}) async-start(bf16[8,16,512]{2,1,0:T(8,128)(2,1)} %bitcast.13), calls=%async_computation.3 | async-start | bytes 262144 | tf_op jit(solution)/shard_map/all_to_all | solution.py:238
  123.6 0.8 copy-done.3
  124.4 6.2 %input_grad.1 = (bf16[128,1024]{1,0:T(8,128)(2,1)}, bf16[128,1024]{1,0:T(8,128)(2,1)}) custom-call(s32[1]{0:T(128)} %bitcast.core, bf16[1536,128]{1,0:T(8,128)(2,1)} %bitcast.18, bf16[1536,128]{1,0:T(8,128)(2,1)} %copy-done.3, bf16[128,1024]{1,0:T(8,128)(2,1)} %bitcast.23, bf16[1024,1024]{1,0:T(8,128)(2,1)} %value_w.3, bf16[1024,1024]{1,0:T(8,128)(2,1)} %gate_w.3, ...), custom_call_target="tpu_custom_call" | custom-call | tf_op jit(solution)/shard_map/input_grad/pallas_call | solution.py:225
  130.6 4.5 %collective-permute-start.5 = (bf16[128,1024]{1,0:T(8,128)(2,1)}, bf16[128,1024]{1,0:T(8,128)(2,1)S(1)}, u32[]{:S(2)}, u32[]{:S(2)}) collective-permute-start(bf16[128,1024]{1,0:T(8,128)(2,1)} %get-tuple-element.14), channel_id=1, source_target_pairs={{0,1},{1,0},{2,3},{3,2},{4,5},{5,4},{6,7},{7,6},{8,9},{9,8},{10,11... | collective-permute-start | bytes 786440 | tf_op jit(solution)/shard_map/ppermute | solution.py:233
  135.1 0.7 collective-permute-start.4
  135.7 6.7 %collective-permute-done.5 = bf16[128,1024]{1,0:T(8,128)(2,1)S(1)} collective-permute-done((bf16[128,1024]{1,0:T(8,128)(2,1)}, bf16[128,1024]{1,0:T(8,128)(2,1)S(1)}, u32[]{:S(2)}, u32[]{:S(2)}) %collective-permute-start.5) | collective-permute-done | bytes 262176 | tf_op jit(solution)/shard_map/ppermute | solution.py:233
  142.4 1.8 %add_multiply_fusion = f32[128,1024]{1,0:T(8,128)} fusion(bf16[128,1024]{1,0:T(8,128)(2,1)S(1)} %collective-permute-done.5, bf16[128,1024]{1,0:T(8,128)(2,1)} %get-tuple-element.14), kind=kLoop, calls=%fused_computation.1 | loop fusion | flops 524288 | bytes 1048576 | tf_op jit(solution)/shard_map/mul | solution.py:234
  144.2 0.6 copy.18
  (22 shorter events, 0.2 us)
Async XLA Ops:
  6.4 1.9 %collective-permute-start = (bf16[1536,128]{1,0:T(8,128)(2,1)}, bf16[1536,128]{1,0:T(8,128)(2,1)S(1)}, u32[]{:S(2)}, u32[]{:S(2)}) collective-permute-start(bf16[1536,128]{1,0:T(8,128)(2,1)} %get-tuple-element.10), channel_id=1, source_target_pairs={{0,2},{2,0},{1,3},{3,1},{4,6},{6,4},{5,7},{7,5},{8,10},{10,8},{9,1... | collective-permute-start | bytes 1179656 | tf_op jit(solution)/shard_map/ppermute | solution.py:174
  44.3 10.6 %copy-start.2 = (bf16[1,128,1024]{2,1,0:T(8,128)(2,1)S(1)}, bf16[1,128,1024]{2,1,0:T(8,128)(2,1)}, u32[]{:S(2)}) copy-start(bf16[1,128,1024]{2,1,0:T(8,128)(2,1)} %param.13) | copy-start | bytes 786436
  44.3 10.7 %copy-start.6 = (bf16[512,128]{1,0:T(8,128)(2,1)S(1)}, bf16[512,128]{1,0:T(8,128)(2,1)}, u32[]{:S(2)}) copy-start(bf16[512,128]{1,0:T(8,128)(2,1)} %get-tuple-element.13) | copy-start | bytes 393220
  49.4 27.9 %all-to-all-start.1 = ((bf16[64,48,128]{2,1,0:T(8,128)(2,1)}), bf16[64,48,128]{2,1,0:T(8,128)(2,1)S(1)}, u32[]{:S(2)}, u32[]{:S(2)}) async-start(bf16[64,48,128]{2,1,0:T(8,128)(2,1)} %bitcast.16), calls=%async_computation.1 | async-start | bytes 1572864 | tf_op jit(solution)/shard_map/all_to_all | solution.py:212
  54.9 1.8 %collective-permute-start.3 = (bf16[128,1024]{1,0:T(8,128)(2,1)S(1)}, bf16[128,1024]{1,0:T(8,128)(2,1)S(1)}, u32[]{:S(2)}, u32[]{:S(2)}) collective-permute-start(bf16[128,1024]{1,0:T(8,128)(2,1)S(1)} %bitcast.21), channel_id=1, source_target_pairs={{0,2},{2,0},{1,3},{3,1},{4,6},{6,4},{5,7},{7,5},{8,10},{10,8},{9,1... | collective-permute-start | bytes 786440 | tf_op jit(solution)/shard_map/ppermute | solution.py:174
  55.0 1.7 %collective-permute-start.2 = (bf16[512,128]{1,0:T(8,128)(2,1)S(1)}, bf16[512,128]{1,0:T(8,128)(2,1)S(1)}, u32[]{:S(2)}, u32[]{:S(2)}) collective-permute-start(bf16[512,128]{1,0:T(8,128)(2,1)S(1)} %copy-done.6), channel_id=1, source_target_pairs={{0,2},{2,0},{1,3},{3,1},{4,6},{6,4},{5,7},{7,5},{8,10},{10,8},{9,1... | collective-permute-start | bytes 393224 | tf_op jit(solution)/shard_map/ppermute | solution.py:174
  56.7 20.5 %copy-start.5 = (bf16[512,128]{1,0:T(8,128)(2,1)}, bf16[512,128]{1,0:T(8,128)(2,1)S(1)}, u32[]{:S(2)}) copy-start(bf16[512,128]{1,0:T(8,128)(2,1)S(1)} %collective-permute-done.2.cot_other) | copy-start | bytes 393220
  56.7 20.5 %copy-start.4 = (bf16[128,1024]{1,0:T(8,128)(2,1)}, bf16[128,1024]{1,0:T(8,128)(2,1)S(1)}, u32[]{:S(2)}) copy-start(bf16[128,1024]{1,0:T(8,128)(2,1)S(1)} %collective-permute-done.3.in_other) | copy-start | bytes 786436
  77.3 0.9 copy-start
  82.8 3.9 %copy-start.1 = (bf16[64,48,128]{2,1,0:T(8,128)(2,1)S(1)}, bf16[64,48,128]{2,1,0:T(8,128)(2,1)}, u32[]{:S(2)}) copy-start(bf16[64,48,128]{2,1,0:T(8,128)(2,1)} %copy-done) | copy-start | bytes 2359300
  82.8 32.6 %all-to-all-start.2 = ((bf16[16,64,1024]{2,1,0:T(8,128)(2,1)}), bf16[16,64,1024]{2,1,0:T(8,128)(2,1)S(1)}, u32[]{:S(2)}, u32[]{:S(2)}) async-start(bf16[16,64,1024]{2,1,0:T(8,128)(2,1)} %bitcast.14), calls=%async_computation.2 | async-start | bytes 4194304 | tf_op jit(solution)/shard_map/all_to_all | solution.py:223
  87.5 36.1 %collective-permute-start.1 = (bf16[1536,128]{1,0:T(8,128)(2,1)S(1)}, bf16[1536,128]{1,0:T(8,128)(2,1)S(1)}, u32[]{:S(2)}, u32[]{:S(2)}) collective-permute-start(bf16[1536,128]{1,0:T(8,128)(2,1)S(1)} %bitcast.25), channel_id=1, source_target_pairs={{0,2},{2,0},{1,3},{3,1},{4,6},{6,4},{5,7},{7,5},{8,10},{10,8},{9,1... | collective-permute-start | bytes 1179656 | tf_op jit(solution)/shard_map/ppermute | solution.py:174
  116.6 18.5 %all-to-all-start.3 = ((bf16[8,16,512]{2,1,0:T(8,128)(2,1)}), bf16[8,16,512]{2,1,0:T(8,128)(2,1)S(1)}, u32[]{:S(2)}, u32[]{:S(2)}) async-start(bf16[8,16,512]{2,1,0:T(8,128)(2,1)} %bitcast.13), calls=%async_computation.3 | async-start | bytes 262144 | tf_op jit(solution)/shard_map/all_to_all | solution.py:238
  123.6 0.8 copy-start.3
  130.6 11.9 %collective-permute-start.5 = (bf16[128,1024]{1,0:T(8,128)(2,1)}, bf16[128,1024]{1,0:T(8,128)(2,1)S(1)}, u32[]{:S(2)}, u32[]{:S(2)}) collective-permute-start(bf16[128,1024]{1,0:T(8,128)(2,1)} %get-tuple-element.14), channel_id=1, source_target_pairs={{0,1},{1,0},{2,3},{3,2},{4,5},{5,4},{6,7},{7,6},{8,9},{9,8},{10,11... | collective-permute-start | bytes 786440 | tf_op jit(solution)/shard_map/ppermute | solution.py:233
  135.1 9.2 %collective-permute-start.4 = (f32[16,512]{1,0:T(8,128)S(1)}, f32[16,512]{1,0:T(8,128)S(1)}, u32[]{:S(2)}, u32[]{:S(2)}) collective-permute-start(f32[16,512]{1,0:T(8,128)S(1)} %broadcast_multiply_fusion), channel_id=1, source_target_pairs={{0,0},{2,2},{64,66},{66,64},{128,128},{130,130},{192,194},{194,192... | collective-permute-start | bytes 98312 | tf_op jit(solution)/shard_map/ppermute | solution.py:241

commit v2 on v1

v2 whole, which is shorter than its diff:
```python
import math

import jax
import jax.numpy as jnp
import numpy as np
from jax import lax
from jax.experimental import pallas as pl
from jax.experimental.pallas import tpu as pltpu
from jax.sharding import Mesh, PartitionSpec as P

F32 = jnp.float32
BF16 = jnp.bfloat16
D = 1024
L = 16384
SCALE = float(2 * L) ** (-0.5)
SIDE = 128
CHIPS = 64
ARRS = 3
ROWS = ARRS * 8
SEQ = ("x", "y", "z", "c")
RING = ("x", "y", "z")
VMEM = pl.BlockSpec(memory_space=pltpu.VMEM)
SMEM = pl.BlockSpec(memory_space=pltpu.SMEM)
PARAMS = pltpu.CompilerParams(vmem_limit_bytes=56 * 1024 * 1024)


def owned(z, core):
    chans = np.zeros((16, 8), np.int64)
    q = 4 * np.arange(16)[:, None] + np.arange(4)[None, :]
    chans[:, :4] = 128 * (q // 16) + 32 * z + 16 * core + q % 16
    chans[:, 4:] = D - 1 - chans[:, :4]
    return chans.reshape(-1)


def one_hot_rows(index, width):
    return (index[:, None] == np.arange(width)[None, :]).astype(jnp.bfloat16)


def channel_order():
    return np.stack(
        [
            np.concatenate([one_hot_rows(owned(z, core), D) for z in range(4)])
            for core in range(2)
        ]
    )


def block_order():
    chans = owned(0, 0)
    order = []
    for half in range(2):
        for y in range(4):
            for i in range(16):
                chan = 128 * y + i if half == 0 else 512 + 128 * y + 96 + 16 + i
                order.append(int(np.nonzero(chans == chan)[0][0]))
    return one_hot_rows(np.array(order), SIDE)


def tables():
    k = np.arange(SIDE)
    quarter = k + 0.25
    outer = 2 * math.pi / SIDE * np.outer(quarter, k)
    both = np.concatenate([np.cos(outer), -np.sin(outer)], axis=0)
    there = np.stack([both[:, k ^ core] for core in range(2)])
    back = []
    for z in range(4):
        for core in range(2):
            rows = []
            for xy in range(16):
                for step in range(4):
                    for slot in range(2):
                        rows.append(2 * (4 * xy + (z ^ step)) + (slot ^ core))
            back.append(both.T[np.array(rows)])
    twist = 2 * math.pi / L * np.outer(quarter, k)
    inner = 2 * math.pi / SIDE * np.outer(k, k)
    cos, sin = np.cos(inner), np.sin(inner)
    inner_table = np.block([[cos, -sin], [sin, cos]])
    return (
        there.astype(jnp.bfloat16),
        np.stack(back).astype(jnp.bfloat16),
        np.cos(twist).astype(np.float32),
        np.sin(twist).astype(np.float32),
        inner_table.astype(jnp.bfloat16),
        inner_table.T.astype(jnp.bfloat16),
    )


def dot(a, b, ca=1, cb=0):
    return lax.dot_general(a, b, (((ca,), (cb,)), ((), ())), preferred_element_type=F32)


def project_kernel(where, inputs, cot, taps, value_w, gate_w, order, keep, give, cot_keep, cot_give):
    z, core = where[0], where[1]
    value = dot(inputs[...], value_w[...]).astype(BF16)
    gate = dot(inputs[...], gate_w[...])
    mix = (cot[...].astype(F32) * gate).astype(BF16)
    stacked = jnp.concatenate([value, mix, taps[...], cot[...]], axis=0)
    for side, (out, cot_out) in enumerate(((keep, cot_keep), (give, cot_give))):
        moved = dot(order[core ^ side], stacked, 1, 1)
        lines = []
        for own in range(4):
            line = moved[own * SIDE:(own + 1) * SIDE]
            parts = [line[:, a * SIDE:(a + 1) * SIDE].reshape(16, 8, SIDE) for a in range(3)]
            lines.append(jnp.concatenate(parts, axis=1))
            cot_out[z ^ own] = line[:, 3 * SIDE:].astype(BF16)
        out[...] = jnp.concatenate(lines, axis=1).reshape(CHIPS * ROWS, SIDE).astype(BF16)


def convolve_kernel(where, signal, outer, outer_t, tw_re, tw_im, inner, inner_t, result, flat, spec):
    flat[...] = signal[...].astype(F32)
    outer_m = outer[where[1]]
    outer_tm = outer_t[2 * where[0] + where[1]]
    cos = tw_re[...]
    sin = tw_im[...]
    inner_m = inner[...]
    inner_tm = inner_t[...]

    for j in range(ROWS):
        sig = flat[pl.ds(j, SIDE, stride=ROWS), :].astype(BF16)
        part = dot(outer_m, sig)
        re, im = part[:SIDE], part[SIDE:]
        turned = jnp.concatenate([re * cos + im * sin, im * cos - re * sin], axis=1)
        spec[j] = dot(turned.astype(BF16), inner_m)

    def back(j, re, im):
        both = jnp.concatenate([re, im], axis=1).astype(BF16)
        part = dot(both, inner_tm)
        re, im = part[:, :SIDE], part[:, SIDE:]
        turned = jnp.concatenate([re * cos - im * sin, re * sin + im * cos], axis=0)
        out = dot(outer_tm, turned.astype(BF16))
        flat[pl.ds(j, SIDE, stride=ROWS), :] = out * (1.0 / L)

    def mul(a, b):
        return (a[0] * b[0] - a[1] * b[1], a[0] * b[1] + a[1] * b[0])

    def mulc(a, b):
        return (a[0] * b[0] + a[1] * b[1], a[0] * b[1] - a[1] * b[0])

    def add(a, b):
        return (a[0] + b[0], a[1] + b[1])

    def load(j):
        both = spec[j]
        return (both[:, :SIDE], both[:, SIDE:])

    for s in range(8):
        t = (s + 4) % 8
        vals, grads, filt = load(s), load(8 + s), load(16 + s)
        vals_f, grads_f, filt_f = load(t), load(8 + t), load(16 + t)
        back(s, *add(mul(filt, vals), mulc(filt, vals_f)))
        back(8 + s, *add(mulc(filt, grads), mul(filt_f, grads_f)))
        back(16 + s, *add(mulc(vals, grads), mulc(grads, vals_f)))
    result[...] = flat[...].astype(BF16)


def weights_kernel(home, blocks, *refs):
    cots, ins, partial = refs[:8], refs[8:16], refs[16]
    full = home[...].astype(F32).reshape(16, 8 * ROWS, SIDE)
    grads, gates = [], []
    for p in range(8):
        base = p * ROWS
        mixed = full[:, base:base + 8].reshape(SIDE, SIDE)
        grads.append(full[:, base + 8:base + 16].reshape(SIDE, SIDE).astype(BF16))
        gates.append((mixed * cots[p][...].astype(F32)).astype(BF16))
    joined = []
    for group in (grads, gates):
        joined.append(dot(blocks[...], jnp.concatenate(group, axis=1)).astype(BF16))
    joined = jnp.concatenate(joined, axis=0)
    total = dot(joined[:, :SIDE], ins[0][...])
    for p in range(1, 8):
        total = total + dot(joined[:, p * SIDE:(p + 1) * SIDE], ins[p][...])
    partial[...] = total.astype(BF16)


def inputs_kernel(where, cot, value_w, gate_w, order, far, *refs):
    lines, cross = refs[:4], refs[4:8]
    input_grad, filter_grad, stack = refs[8:]
    z, core = where[0], where[1]
    other = far[...].astype(F32).reshape(4, 16, ROWS + 8, SIDE)
    for k in range(4):
        near = lines[k][...].astype(F32).reshape(16, 2 * ROWS, SIDE)
        extra = cross[k][...].astype(F32).reshape(16, 16, SIDE)
        for side in range(2):
            if side == 0:
                parts = [near[:, a * 8:(a + 1) * 8] for a in range(3)] + [extra[:, :8]]
            else:
                parts = [other[k, :, a * 8:(a + 1) * 8] for a in range(4)]
            parts = [part.reshape(SIDE, SIDE) for part in parts]
            stack[core ^ side, z ^ k] = jnp.concatenate(parts, axis=1).astype(BF16)
    natural = dot(stack[...].reshape(D, 4 * SIDE), order[...].reshape(D, D), 0, 0)
    gated = (natural[:SIDE] * cot[...].astype(F32)).astype(BF16)
    grad = natural[SIDE:2 * SIDE].astype(BF16)
    filter_grad[...] = (natural[2 * SIDE:3 * SIDE] + natural[3 * SIDE:]) * SCALE
    total = dot(grad, value_w[...], 1, 1) + dot(gated, gate_w[...], 1, 1)
    input_grad[...] = total.astype(BF16)


def shape(*dims, kind=BF16):
    return jax.ShapeDtypeStruct(dims, kind)


def swap_cores(a):
    return lax.ppermute(a, "c", [(0, 1), (1, 0)])


def along(a, k):
    return lax.ppermute(a, "z", [(z, z ^ k) for z in range(4)])


def across(a, k):
    pairs = [(2 * z + dp, 2 * (z ^ k) + 1 - dp) for z in range(4) for dp in range(2)]
    return lax.ppermute(a, ("z", "dp"), pairs)


def final_pairs(other):
    pairs = []
    for x in range(4):
        for z in range(4):
            for c in range(2):
                flip = x & 1
                z_to, c_to = (3 - z, 1 - c) if flip else (z, c)
                if other is None:
                    pairs.append(((x * 4 + z) * 2 + c, (x * 4 + z_to) * 2 + c_to))
                else:
                    for dp in range(2):
                        start = ((x * 4 + z) * 2 + c) * 2 + dp
                        pairs.append((start, ((x * 4 + z_to) * 2 + c_to) * 2 + 1 - dp))
    return pairs


def local(inputs, cotangent, value_weight, gate_weight, filter_taps):
    z = lax.axis_index("z").astype(jnp.int32)
    core = lax.axis_index("c").astype(jnp.int32)
    dp = lax.axis_index("dp")
    where = jnp.stack([z, core])
    order = jnp.asarray(channel_order())
    flat_in = inputs.reshape(SIDE, D)
    cot = cotangent.reshape(SIDE, D)

    keep, give, cot_keep, cot_give = pl.pallas_call(
        project_kernel,
        out_shape=[shape(CHIPS * ROWS, SIDE)] * 2 + [shape(4, SIDE, SIDE)] * 2,
        in_specs=[SMEM] + [VMEM] * 6,
        out_specs=[VMEM] * 4,
        compiler_params=PARAMS,
        name="project",
    )(where, flat_in, cot, filter_taps, value_weight, gate_weight, order)
    got = swap_cores(give)
    message = jnp.concatenate(
        [keep.reshape(CHIPS, ROWS, SIDE), got.reshape(CHIPS, ROWS, SIDE)], axis=1
    )
    spread = lax.all_to_all(message, RING, 0, 0, tiled=True)

    cot_other = swap_cores(cot_give)
    cots = [cot_keep[0], cot_other[0]]
    ins = [flat_in, swap_cores(flat_in)]
    for k in range(1, 4):
        pair = along(jnp.stack([cot_keep[k], cot_other[k]]), k)
        moved = along(flat_in, k)
        cots += [pair[0], pair[1]]
        ins += [moved, swap_cores(moved)]

    result = pl.pallas_call(
        convolve_kernel,
        out_shape=shape(2 * CHIPS * ROWS, SIDE),
        in_specs=[SMEM] + [VMEM] * 7,
        out_specs=VMEM,
        scratch_shapes=[
            pltpu.VMEM((2 * CHIPS * ROWS, SIDE), F32),
            pltpu.VMEM((ROWS, SIDE, 2 * SIDE), F32),
        ],
        compiler_params=PARAMS,
        name="convolve",
    )(where, spread.reshape(2 * CHIPS * ROWS, SIDE), *[jnp.asarray(t) for t in tables()])
    home = lax.all_to_all(result.reshape(16, 8 * ROWS, SIDE), ("x", "y"), 0, 0, tiled=True)

    by_step = home.reshape(16, 4, 2 * ROWS, SIDE)
    lines, cross = [], []
    for k in range(4):
        line = by_step[:, k]
        parts = jnp.concatenate([line[:, 16:24], line[:, 40:48]], axis=1)
        lines.append(line if k == 0 else along(line, k))
        cross.append(across(parts, k))

    partial = pl.pallas_call(
        weights_kernel,
        out_shape=shape(256, D),
        in_specs=[VMEM] * 18,
        out_specs=VMEM,
        compiler_params=PARAMS,
        name="weights",
    )(home.reshape(2 * CHIPS * ROWS, SIDE), jnp.asarray(block_order()), *cots, *ins)
    pieces = lax.all_to_all(partial, ("x", "y"), 0, 0, tiled=True)

    far = swap_cores(
        jnp.stack(
            [jnp.concatenate([lines[k][:, ROWS:], cross[k][:, 8:]], axis=1) for k in range(4)]
        )
    )
    input_grad, filter_grad = pl.pallas_call(
        inputs_kernel,
        out_shape=[shape(SIDE, D), shape(SIDE, D, kind=F32)],
        in_specs=[SMEM] + [VMEM] * 13,
        out_specs=[VMEM] * 2,
        scratch_shapes=[pltpu.VMEM((2, 4, SIDE, 4 * SIDE), BF16)],
        compiler_params=PARAMS,
        name="input_grad",
    )(
        where,
        cot,
        value_weight,
        gate_weight,
        order.reshape(2, 4, SIDE, D),
        far.reshape(4 * 16 * 32, SIDE),
        *[line.reshape(16 * 48, SIDE) for line in lines],
        *[part.reshape(16 * 16, SIDE) for part in cross],
    )

    sums = jnp.sum(pieces.reshape(16, 16, D).astype(F32), axis=0)
    mine = lax.dynamic_slice_in_dim(sums, dp * 512, 512, 1)
    theirs = lax.dynamic_slice_in_dim(sums, (1 - dp) * 512, 512, 1)
    mine = lax.ppermute(mine, ("x", "z", "c"), final_pairs(None))
    theirs = lax.ppermute(theirs, ("x", "z", "c", "dp"), final_pairs(1))
    projection_grads = (mine + theirs) * SCALE
    return (input_grad.reshape(1, SIDE, D), projection_grads, filter_grad)


def solution(mesh):
    fine = Mesh(mesh.devices.reshape(4, 4, 4, 2, 2), ("x", "y", "z", "c", "dp"))
    in_specs = (P("dp", SEQ, None), P("dp", SEQ, None), P(), P(), P(SEQ, None))
    out_specs = (P("dp", SEQ, None), P(SEQ, "dp"), P(SEQ, None))
    return jax.shard_map(local, mesh=fine, in_specs=in_specs, out_specs=out_specs, check_vma=False)
```

time: 146 us -> 135 us (0.925)
  the two profiles are of different devices: /device:TPU:32 before, /device:TPU:15 now
where the time goes in v2:
time: 135 us; the launch traced here: 134 us
  starting transfers between devices  70.9 us (53%)
  waiting for transfers between devices  30.1 us (22%)
  Pallas kernels  21.7 us (16%)
  local copies, waits for them, and re-layouts  7.06 us (5%)
  other arithmetic  3.48 us (3%)
    ppermute x9, starting transfers between devices, along(): return lax.ppermute(a, 'z', [(z, z ^ k) for z in range(4)])  23.7 us
    all_to_all x1, starting transfers between devices, local(): spread = lax.all_to_all(message, RING, 0, 0, tiled=True)  11.6 us
    ppermute x7, starting transfers between devices, swap_cores(): return lax.ppermute(a, 'c', [(0, 1), (1, 0)])  10.2 us
    all_to_all x1, waiting for transfers between devices, local(): spread = lax.all_to_all(message, RING, 0, 0, tiled=True)  9.91 us
    ppermute x4, waiting for transfers between devices, across(): return lax.ppermute(a, ('z', 'dp'), pairs)  9.71 us
    ppermute x4, starting transfers between devices, across(): return lax.ppermute(a, ('z', 'dp'), pairs)  8.43 us
    pallas_call x1, Pallas kernels, local(): pl.pallas_call(inputs_kernel, out_shape=[shape(SIDE, D), shape(SIDE, D, k...  6.67 us
    all_to_all x1, starting transfers between devices, local(): pieces = lax.all_to_all(partial, ('x', 'y'), 0, 0, tiled=True)  6.58 us
  transfers between devices with their start and end apart: 25, of which 11 were waited for; matrix products, arithmetic and copies ran while one was open for 5% of the time, Pallas kernels for 7%

profile of v2, /device:TPU:15, one launch (start us, length us, event | category | flops | bytes accessed | tf_op | source)
XLA Modules:
  0.0 134.2 jit_solution(8471163114731386589)
XLA Ops:
  1.2 5.8 %project.1 = (bf16[1536,128]{1,0:T(8,128)(2,1)}, bf16[1536,128]{1,0:T(8,128)(2,1)}, bf16[4,128,128]{2,1,0:T(8,128)(2,1)}, bf16[4,128,128]{2,1,0:T(8,128)(2,1)}) custom-call(s32[2]{0:T(128)} %pad_add_fusion.where, bf16[128,1024]{1,0:T(8,128)(2,1)} %bitcast.67, bf16[128,1024]{1,0:T(8,128)(2,1)} %bitcast.73, bf16[128,1024]{1,0:T(8,128)(2,1)} %taps.1, ...), custom_call_target="tpu_custom_call" | custom-call | tf_op jit(solution)/shard_map/project/pallas_call | solution.py:240
  9.4 2.0 %pad_maximum_fusion = bf16[64,48,128]{2,1,0:T(8,128)(2,1)} fusion(bf16[64,24,128]{2,1,0:T(8,128)(2,1)S(1)} %bitcast.81, bf16[64,24,128]{2,1,0:T(8,128)(2,1)} %bitcast.80), kind=kLoop, calls=%fused_computation.1 | loop fusion | flops 1572864 | bytes 1572864 | tf_op jit(solution)/shard_map/concatenate | solution.py:249
  11.4 11.6 %all-to-all-start = ((bf16[64,48,128]{2,1,0:T(8,128)(2,1)}), bf16[64,48,128]{2,1,0:T(8,128)(2,1)S(1)}, u32[]{:S(2)}, u32[]{:S(2)}) async-start(bf16[64,48,128]{2,1,0:T(8,128)(2,1)} %pad_maximum_fusion), calls=%async_computation | async-start | bytes 1572864 | tf_op jit(solution)/shard_map/all_to_all | solution.py:252
  24.2 2.1 %collective-permute-start.16 = (bf16[128,1024]{1,0:T(8,128)(2,1)S(1)}, bf16[128,1024]{1,0:T(8,128)(2,1)S(1)}, u32[]{:S(2)}, u32[]{:S(2)}) collective-permute-start(bf16[128,1024]{1,0:T(8,128)(2,1)S(1)} %bitcast.70), channel_id=1, source_target_pairs={{0,8},{4,12},{8,0},{12,4},{1,9},{5,13},{9,1},{13,5},{2,10},{6,14},... | collective-permute-start | bytes 786440 | tf_op jit(solution)/shard_map/ppermute | solution.py:207
  30.3 3.1 %collective-permute-start.12 = (bf16[2,128,128]{2,1,0:T(8,128)(2,1)S(1)}, bf16[2,128,128]{2,1,0:T(8,128)(2,1)S(1)}, u32[]{:S(2)}, u32[]{:S(2)}) collective-permute-start(bf16[2,128,128]{2,1,0:T(8,128)(2,1)S(1)} %pad_maximum_fusion.8), channel_id=1, source_target_pairs={{0,12},{4,8},{8,4},{12,0},{1,13},{5,9},{9,5},{13,1},{2,14},{6,10},... | collective-permute-start | bytes 196616 | tf_op jit(solution)/shard_map/ppermute | solution.py:207
  33.4 9.9 %all-to-all-done = bf16[64,48,128]{2,1,0:T(8,128)(2,1)S(1)} async-done(((bf16[64,48,128]{2,1,0:T(8,128)(2,1)}), bf16[64,48,128]{2,1,0:T(8,128)(2,1)S(1)}, u32[]{:S(2)}, u32[]{:S(2)}) %all-to-all-start) | async-done | bytes 786464 | tf_op jit(solution)/shard_map/all_to_all | solution.py:252
  44.2 5.1 %convolve.1 = bf16[3072,128]{1,0:T(8,128)(2,1)} custom-call(s32[2]{0:T(128)} %pad_add_fusion.where, bf16[3072,128]{1,0:T(8,128)(2,1)} %bitcast.65, bf16[2,256,128]{2,1,0:T(8,128)(2,1)} %constant.40.clone.outer, bf16[8,128,256]{2,1,0:T(8,128)(2,1)} %constant.41.clone.outer_t, f32[128,128]{1,0:T(8,128)} %constant.42.clone.tw_re, ...), custom_call_target="tpu_custom_call" | custom-call | tf_op jit(solution)/shard_map/convolve/pallas_call | solution.py:263
  49.3 6.3 %all-to-all-start.1 = ((bf16[16,192,128]{2,1,0:T(8,128)(2,1)}), bf16[16,192,128]{2,1,0:T(8,128)(2,1)S(1)}, u32[]{:S(2)}, u32[]{:S(2)}) async-start(bf16[16,192,128]{2,1,0:T(8,128)(2,1)} %bitcast.64), calls=%async_computation.1 | async-start | bytes 1572864 | tf_op jit(solution)/shard_map/all_to_all | solution.py:275
  56.9 11.2 %collective-permute-start.11 = (bf16[2,128,128]{2,1,0:T(8,128)(2,1)S(1)}, bf16[2,128,128]{2,1,0:T(8,128)(2,1)S(1)}, u32[]{:S(2)}, u32[]{:S(2)}) collective-permute-start(bf16[2,128,128]{2,1,0:T(8,128)(2,1)S(1)} %pad_maximum_fusion.7), channel_id=1, source_target_pairs={{0,8},{4,12},{8,0},{12,4},{1,9},{5,13},{9,1},{13,5},{2,10},{6,14},... | collective-permute-start | bytes 196616 | tf_op jit(solution)/shard_map/ppermute | solution.py:207
  69.7 1.8 %collective-permute-start.10 = (bf16[2,128,128]{2,1,0:T(8,128)(2,1)S(1)}, bf16[2,128,128]{2,1,0:T(8,128)(2,1)S(1)}, u32[]{:S(2)}, u32[]{:S(2)}) collective-permute-start(bf16[2,128,128]{2,1,0:T(8,128)(2,1)S(1)} %pad_maximum_fusion.6), channel_id=1, source_target_pairs={{0,4},{4,0},{8,12},{12,8},{1,5},{5,1},{9,13},{13,9},{2,6},{6,2},{1... | collective-permute-start | bytes 196616 | tf_op jit(solution)/shard_map/ppermute | solution.py:207
  73.8 3.4 %collective-permute-start.15 = (bf16[128,1024]{1,0:T(8,128)(2,1)S(1)}, bf16[128,1024]{1,0:T(8,128)(2,1)}, u32[]{:S(2)}, u32[]{:S(2)}) collective-permute-start(bf16[128,1024]{1,0:T(8,128)(2,1)S(1)} %collective-permute-done.14.refs_10_), channel_id=1, source_target_pairs={{0,2},{2,0},{1,3},{3,1},{4,6},{6,4},{5,7},{7,5},{8,10},{10,8},{9,1... | collective-permute-start | bytes 786440 | tf_op jit(solution)/shard_map/ppermute | solution.py:203
  79.3 1.8 %collective-permute-start.2 = (bf16[16,48,128]{2,1,0:T(8,128)(2,1)S(1)}, bf16[16,48,128]{2,1,0:T(8,128)(2,1)S(1)}, u32[]{:S(2)}, u32[]{:S(2)}) collective-permute-start(bf16[16,48,128]{2,1,0:T(8,128)(2,1)S(1)} %get-tuple-element.18), channel_id=1, source_target_pairs={{0,4},{4,0},{8,12},{12,8},{1,5},{5,1},{9,13},{13,9},{2,6},{6,2},{1... | collective-permute-start | bytes 589832 | tf_op jit(solution)/shard_map/ppermute | solution.py:207
  84.0 4.1 %weights.1 = bf16[256,1024]{1,0:T(8,128)(2,1)} custom-call(bf16[3072,128]{1,0:T(8,128)(2,1)} %bitcast.63, bf16[128,128]{1,0:T(8,128)(2,1)} %constant.46.clone.blocks, bf16[128,128]{1,0:T(8,128)(2,1)} %get-tuple-element.31.refs_0_, bf16[128,128]{1,0:T(8,128)(2,1)} %get-tuple-element.35.refs_1_, bf16[128,128]{1,0:T(8,128)(2,1)} %get-tuple-element.43.refs_2_, ...), custom_call_target="tpu_custom_call" | custom-call | tf_op jit(solution)/shard_map/weights/pallas_call | solution.py:285
  88.1 6.6 %all-to-all-start.2 = ((bf16[16,16,1024]{2,1,0:T(8,128)(2,1)}), bf16[16,16,1024]{2,1,0:T(8,128)(2,1)S(1)}, u32[]{:S(2)}, u32[]{:S(2)}) async-start(bf16[16,16,1024]{2,1,0:T(8,128)(2,1)} %bitcast.66), calls=%async_computation.2 | async-start | bytes 1048576 | tf_op jit(solution)/shard_map/all_to_all | solution.py:293
  94.7 4.3 %collective-permute-start.1 = (bf16[16,16,128]{2,1,0:T(8,128)(2,1)S(1)}, bf16[16,16,128]{2,1,0:T(8,128)(2,1)S(1)}, u32[]{:S(2)}, u32[]{:S(2)}) collective-permute-start(bf16[16,16,128]{2,1,0:T(8,128)(2,1)S(1)} %pad_maximum_fusion.2), channel_id=1, source_target_pairs={{0,1},{1,0},{4,5},{5,4},{8,9},{9,8},{12,13},{13,12},{2,3},{3,2},{6... | collective-permute-start | bytes 196616 | tf_op jit(solution)/shard_map/ppermute | solution.py:212
  99.7 2.3 %collective-permute-done.1 = bf16[16,16,128]{2,1,0:T(8,128)(2,1)S(1)} collective-permute-done((bf16[16,16,128]{2,1,0:T(8,128)(2,1)S(1)}, bf16[16,16,128]{2,1,0:T(8,128)(2,1)S(1)}, u32[]{:S(2)}, u32[]{:S(2)}) %collective-permute-start.1) | collective-permute-done | bytes 65568 | tf_op jit(solution)/shard_map/ppermute | solution.py:212
  101.9 2.8 %collective-permute-start.5 = (bf16[16,16,128]{2,1,0:T(8,128)(2,1)S(1)}, bf16[16,16,128]{2,1,0:T(8,128)(2,1)S(1)}, u32[]{:S(2)}, u32[]{:S(2)}) collective-permute-start(bf16[16,16,128]{2,1,0:T(8,128)(2,1)S(1)} %pad_maximum_fusion.4), channel_id=1, source_target_pairs={{0,9},{1,8},{4,13},{5,12},{8,1},{9,0},{12,5},{13,4},{2,11},{3,10},... | collective-permute-start | bytes 196616 | tf_op jit(solution)/shard_map/ppermute | solution.py:212
  104.7 3.8 %collective-permute-done.3 = bf16[16,16,128]{2,1,0:T(8,128)(2,1)S(1)} collective-permute-done((bf16[16,16,128]{2,1,0:T(8,128)(2,1)S(1)}, bf16[16,16,128]{2,1,0:T(8,128)(2,1)S(1)}, u32[]{:S(2)}, u32[]{:S(2)}) %collective-permute-start.3) | collective-permute-done | bytes 65568 | tf_op jit(solution)/shard_map/ppermute | solution.py:212
  109.3 3.7 %collective-permute-done.7 = bf16[16,16,128]{2,1,0:T(8,128)(2,1)S(1)} collective-permute-done((bf16[16,16,128]{2,1,0:T(8,128)(2,1)S(1)}, bf16[16,16,128]{2,1,0:T(8,128)(2,1)S(1)}, u32[]{:S(2)}, u32[]{:S(2)}) %collective-permute-start.7) | collective-permute-done | bytes 65568 | tf_op jit(solution)/shard_map/ppermute | solution.py:212
  113.3 3.7 %collective-permute-start.8 = (bf16[4,16,32,128]{3,2,1,0:T(8,128)(2,1)S(1)}, bf16[4,16,32,128]{3,2,1,0:T(8,128)(2,1)S(1)}, u32[]{:S(2)}, u32[]{:S(2)}) collective-permute-start(bf16[4,16,32,128]{3,2,1,0:T(8,128)(2,1)S(1)} %pad_maximum_fusion.1), channel_id=1, source_target_pairs={{0,2},{2,0},{1,3},{3,1},{4,6},{6,4},{5,7},{7,5},{8,10},{10,8},{9,1... | collective-permute-start | bytes 1572872 | tf_op jit(solution)/shard_map/ppermute | solution.py:203
  117.1 3.3 %collective-permute-start.20 = (f32[16,512]{1,0:T(8,128)S(1)}, f32[16,512]{1,0:T(8,128)S(1)}, u32[]{:S(2)}, u32[]{:S(2)}) collective-permute-start(f32[16,512]{1,0:T(8,128)S(1)} %get-tuple-element.37), channel_id=1, source_target_pairs={{0,0},{2,2},{4,4},{6,6},{8,8},{10,10},{12,12},{14,14},{64,78},{66,... | collective-permute-start | bytes 98312 | tf_op jit(solution)/shard_map/ppermute | solution.py:322
  121.3 2.9 %collective-permute-done.20 = f32[16,512]{1,0:T(8,128)S(1)} collective-permute-done((f32[16,512]{1,0:T(8,128)S(1)}, f32[16,512]{1,0:T(8,128)S(1)}, u32[]{:S(2)}, u32[]{:S(2)}) %collective-permute-start.20) | collective-permute-done | bytes 32800 | tf_op jit(solution)/shard_map/ppermute | solution.py:322
  124.1 2.0 %collective-permute-done.21 = f32[16,512]{1,0:T(8,128)S(1)} collective-permute-done((f32[16,512]{1,0:T(8,128)S(1)}, f32[16,512]{1,0:T(8,128)S(1)}, u32[]{:S(2)}, u32[]{:S(2)}) %collective-permute-start.21) | collective-permute-done | bytes 32800 | tf_op jit(solution)/shard_map/ppermute | solution.py:323
  127.5 6.7 %input_grad.1 = (bf16[128,1024]{1,0:T(8,128)(2,1)}, f32[128,1024]{1,0:T(8,128)}) custom-call(s32[2]{0:T(128)} %pad_add_fusion.where, bf16[128,1024]{1,0:T(8,128)(2,1)} %bitcast.74, bf16[1024,1024]{1,0:T(8,128)(2,1)} %value_w.3, bf16[1024,1024]{1,0:T(8,128)(2,1)} %gate_w.3, bf16[2,4,128,1024]{3,2,1,0:T(8,128)(2,1)} %constant.49.order, ...), custom_call_target="tpu_custom_call" | custom-call | tf_op jit(solution)/shard_map/input_grad/pallas_call | solution.py:300
  (103 shorter events, 23.1 us)
Async XLA Ops:
  7.1 2.3 %collective-permute-start = (bf16[1536,128]{1,0:T(8,128)(2,1)}, bf16[1536,128]{1,0:T(8,128)(2,1)S(1)}, u32[]{:S(2)}, u32[]{:S(2)}) collective-permute-start(bf16[1536,128]{1,0:T(8,128)(2,1)} %get-tuple-element.10), channel_id=1, source_target_pairs={{0,2},{2,0},{1,3},{3,1},{4,6},{6,4},{5,7},{7,5},{8,10},{10,8},{9,1... | collective-permute-start | bytes 1179656 | tf_op jit(solution)/shard_map/ppermute | solution.py:203
  11.4 32.0 %all-to-all-start = ((bf16[64,48,128]{2,1,0:T(8,128)(2,1)}), bf16[64,48,128]{2,1,0:T(8,128)(2,1)S(1)}, u32[]{:S(2)}, u32[]{:S(2)}) async-start(bf16[64,48,128]{2,1,0:T(8,128)(2,1)} %pad_maximum_fusion), calls=%async_computation | async-start | bytes 1572864 | tf_op jit(solution)/shard_map/all_to_all | solution.py:252
  23.0 50.9 %collective-permute-start.14 = (bf16[128,1024]{1,0:T(8,128)(2,1)S(1)}, bf16[128,1024]{1,0:T(8,128)(2,1)S(1)}, u32[]{:S(2)}, u32[]{:S(2)}) collective-permute-start(bf16[128,1024]{1,0:T(8,128)(2,1)S(1)} %bitcast.69), channel_id=1, source_target_pairs={{0,4},{4,0},{8,12},{12,8},{1,5},{5,1},{9,13},{13,9},{2,6},{6,2},{1... | collective-permute-start | bytes 786440 | tf_op jit(solution)/shard_map/ppermute | solution.py:207
  24.2 53.0 %collective-permute-start.16 = (bf16[128,1024]{1,0:T(8,128)(2,1)S(1)}, bf16[128,1024]{1,0:T(8,128)(2,1)S(1)}, u32[]{:S(2)}, u32[]{:S(2)}) collective-permute-start(bf16[128,1024]{1,0:T(8,128)(2,1)S(1)} %bitcast.70), channel_id=1, source_target_pairs={{0,8},{4,12},{8,0},{12,4},{1,9},{5,13},{9,1},{13,5},{2,10},{6,14},... | collective-permute-start | bytes 786440 | tf_op jit(solution)/shard_map/ppermute | solution.py:207
  26.3 51.1 %collective-permute-start.18 = (bf16[128,1024]{1,0:T(8,128)(2,1)S(1)}, bf16[128,1024]{1,0:T(8,128)(2,1)S(1)}, u32[]{:S(2)}, u32[]{:S(2)}) collective-permute-start(bf16[128,1024]{1,0:T(8,128)(2,1)S(1)} %bitcast.71), channel_id=1, source_target_pairs={{0,12},{4,8},{8,4},{12,0},{1,13},{5,9},{9,5},{13,1},{2,14},{6,10},... | collective-permute-start | bytes 786440 | tf_op jit(solution)/shard_map/ppermute | solution.py:207
  26.6 55.2 %collective-permute-start.13 = (bf16[128,1024]{1,0:T(8,128)(2,1)S(1)}, bf16[128,1024]{1,0:T(8,128)(2,1)S(1)}, u32[]{:S(2)}, u32[]{:S(2)}) collective-permute-start(bf16[128,1024]{1,0:T(8,128)(2,1)S(1)} %bitcast.72), channel_id=1, source_target_pairs={{0,2},{2,0},{1,3},{3,1},{4,6},{6,4},{5,7},{7,5},{8,10},{10,8},{9,1... | collective-permute-start | bytes 786440 | tf_op jit(solution)/shard_map/ppermute | solution.py:203
  30.3 26.5 %collective-permute-start.12 = (bf16[2,128,128]{2,1,0:T(8,128)(2,1)S(1)}, bf16[2,128,128]{2,1,0:T(8,128)(2,1)S(1)}, u32[]{:S(2)}, u32[]{:S(2)}) collective-permute-start(bf16[2,128,128]{2,1,0:T(8,128)(2,1)S(1)} %pad_maximum_fusion.8), channel_id=1, source_target_pairs={{0,12},{4,8},{8,4},{12,0},{1,13},{5,9},{9,5},{13,1},{2,14},{6,10},... | collective-permute-start | bytes 196616 | tf_op jit(solution)/shard_map/ppermute | solution.py:207
  49.3 28.5 %all-to-all-start.1 = ((bf16[16,192,128]{2,1,0:T(8,128)(2,1)}), bf16[16,192,128]{2,1,0:T(8,128)(2,1)S(1)}, u32[]{:S(2)}, u32[]{:S(2)}) async-start(bf16[16,192,128]{2,1,0:T(8,128)(2,1)} %bitcast.64), calls=%async_computation.1 | async-start | bytes 1572864 | tf_op jit(solution)/shard_map/all_to_all | solution.py:275
  56.9 12.9 %collective-permute-start.11 = (bf16[2,128,128]{2,1,0:T(8,128)(2,1)S(1)}, bf16[2,128,128]{2,1,0:T(8,128)(2,1)S(1)}, u32[]{:S(2)}, u32[]{:S(2)}) collective-permute-start(bf16[2,128,128]{2,1,0:T(8,128)(2,1)S(1)} %pad_maximum_fusion.7), channel_id=1, source_target_pairs={{0,8},{4,12},{8,0},{12,4},{1,9},{5,13},{9,1},{13,5},{2,10},{6,14},... | collective-permute-start | bytes 196616 | tf_op jit(solution)/shard_map/ppermute | solution.py:207
  69.7 3.5 %collective-permute-start.10 = (bf16[2,128,128]{2,1,0:T(8,128)(2,1)S(1)}, bf16[2,128,128]{2,1,0:T(8,128)(2,1)S(1)}, u32[]{:S(2)}, u32[]{:S(2)}) collective-permute-start(bf16[2,128,128]{2,1,0:T(8,128)(2,1)S(1)} %pad_maximum_fusion.6), channel_id=1, source_target_pairs={{0,4},{4,0},{8,12},{12,8},{1,5},{5,1},{9,13},{13,9},{2,6},{6,2},{1... | collective-permute-start | bytes 196616 | tf_op jit(solution)/shard_map/ppermute | solution.py:207
  73.8 8.4 %collective-permute-start.15 = (bf16[128,1024]{1,0:T(8,128)(2,1)S(1)}, bf16[128,1024]{1,0:T(8,128)(2,1)}, u32[]{:S(2)}, u32[]{:S(2)}) collective-permute-start(bf16[128,1024]{1,0:T(8,128)(2,1)S(1)} %collective-permute-done.14.refs_10_), channel_id=1, source_target_pairs={{0,2},{2,0},{1,3},{3,1},{4,6},{6,4},{5,7},{7,5},{8,10},{10,8},{9,1... | collective-permute-start | bytes 786440 | tf_op jit(solution)/shard_map/ppermute | solution.py:203
  77.3 6.6 %collective-permute-start.17 = (bf16[128,1024]{1,0:T(8,128)(2,1)S(1)}, bf16[128,1024]{1,0:T(8,128)(2,1)}, u32[]{:S(2)}, u32[]{:S(2)}) collective-permute-start(bf16[128,1024]{1,0:T(8,128)(2,1)S(1)} %collective-permute-done.16.refs_12_), channel_id=1, source_target_pairs={{0,2},{2,0},{1,3},{3,1},{4,6},{6,4},{5,7},{7,5},{8,10},{10,8},{9,1... | collective-permute-start | bytes 786440 | tf_op jit(solution)/shard_map/ppermute | solution.py:203
  77.4 6.5 %collective-permute-start.19 = (bf16[128,1024]{1,0:T(8,128)(2,1)S(1)}, bf16[128,1024]{1,0:T(8,128)(2,1)}, u32[]{:S(2)}, u32[]{:S(2)}) collective-permute-start(bf16[128,1024]{1,0:T(8,128)(2,1)S(1)} %collective-permute-done.18.refs_14_), channel_id=1, source_target_pairs={{0,2},{2,0},{1,3},{3,1},{4,6},{6,4},{5,7},{7,5},{8,10},{10,8},{9,1... | collective-permute-start | bytes 786440 | tf_op jit(solution)/shard_map/ppermute | solution.py:203
  79.3 33.7 %collective-permute-start.2 = (bf16[16,48,128]{2,1,0:T(8,128)(2,1)S(1)}, bf16[16,48,128]{2,1,0:T(8,128)(2,1)S(1)}, u32[]{:S(2)}, u32[]{:S(2)}) collective-permute-start(bf16[16,48,128]{2,1,0:T(8,128)(2,1)S(1)} %get-tuple-element.18), channel_id=1, source_target_pairs={{0,4},{4,0},{8,12},{12,8},{1,5},{5,1},{9,13},{13,9},{2,6},{6,2},{1... | collective-permute-start | bytes 589832 | tf_op jit(solution)/shard_map/ppermute | solution.py:207
  81.8 31.2 %collective-permute-start.4 = (bf16[16,48,128]{2,1,0:T(8,128)(2,1)S(1)}, bf16[16,48,128]{2,1,0:T(8,128)(2,1)S(1)}, u32[]{:S(2)}, u32[]{:S(2)}) collective-permute-start(bf16[16,48,128]{2,1,0:T(8,128)(2,1)S(1)} %get-tuple-element.17), channel_id=1, source_target_pairs={{0,8},{4,12},{8,0},{12,4},{1,9},{5,13},{9,1},{13,5},{2,10},{6,14},... | collective-permute-start | bytes 589832 | tf_op jit(solution)/shard_map/ppermute | solution.py:207
  82.2 30.8 %collective-permute-start.6 = (bf16[16,48,128]{2,1,0:T(8,128)(2,1)S(1)}, bf16[16,48,128]{2,1,0:T(8,128)(2,1)S(1)}, u32[]{:S(2)}, u32[]{:S(2)}) collective-permute-start(bf16[16,48,128]{2,1,0:T(8,128)(2,1)S(1)} %get-tuple-element.19), channel_id=1, source_target_pairs={{0,12},{4,8},{8,4},{12,0},{1,13},{5,9},{9,5},{13,1},{2,14},{6,10},... | collective-permute-start | bytes 589832 | tf_op jit(solution)/shard_map/ppermute | solution.py:207
  88.1 28.9 %all-to-all-start.2 = ((bf16[16,16,1024]{2,1,0:T(8,128)(2,1)}), bf16[16,16,1024]{2,1,0:T(8,128)(2,1)S(1)}, u32[]{:S(2)}, u32[]{:S(2)}) async-start(bf16[16,16,1024]{2,1,0:T(8,128)(2,1)} %bitcast.66), calls=%async_computation.2 | async-start | bytes 1048576 | tf_op jit(solution)/shard_map/all_to_all | solution.py:293
  94.7 7.2 %collective-permute-start.1 = (bf16[16,16,128]{2,1,0:T(8,128)(2,1)S(1)}, bf16[16,16,128]{2,1,0:T(8,128)(2,1)S(1)}, u32[]{:S(2)}, u32[]{:S(2)}) collective-permute-start(bf16[16,16,128]{2,1,0:T(8,128)(2,1)S(1)} %pad_maximum_fusion.2), channel_id=1, source_target_pairs={{0,1},{1,0},{4,5},{5,4},{8,9},{9,8},{12,13},{13,12},{2,3},{3,2},{6... | collective-permute-start | bytes 196616 | tf_op jit(solution)/shard_map/ppermute | solution.py:212
  99.0 9.5 %collective-permute-start.3 = (bf16[16,16,128]{2,1,0:T(8,128)(2,1)S(1)}, bf16[16,16,128]{2,1,0:T(8,128)(2,1)S(1)}, u32[]{:S(2)}, u32[]{:S(2)}) collective-permute-start(bf16[16,16,128]{2,1,0:T(8,128)(2,1)S(1)} %pad_maximum_fusion.3), channel_id=1, source_target_pairs={{0,5},{1,4},{4,1},{5,0},{8,13},{9,12},{12,9},{13,8},{2,7},{3,6},{6... | collective-permute-start | bytes 196616 | tf_op jit(solution)/shard_map/ppermute | solution.py:212
  101.9 7.3 %collective-permute-start.5 = (bf16[16,16,128]{2,1,0:T(8,128)(2,1)S(1)}, bf16[16,16,128]{2,1,0:T(8,128)(2,1)S(1)}, u32[]{:S(2)}, u32[]{:S(2)}) collective-permute-start(bf16[16,16,128]{2,1,0:T(8,128)(2,1)S(1)} %pad_maximum_fusion.4), channel_id=1, source_target_pairs={{0,9},{1,8},{4,13},{5,12},{8,1},{9,0},{12,5},{13,4},{2,11},{3,10},... | collective-permute-start | bytes 196616 | tf_op jit(solution)/shard_map/ppermute | solution.py:212
  108.5 4.5 %collective-permute-start.7 = (bf16[16,16,128]{2,1,0:T(8,128)(2,1)S(1)}, bf16[16,16,128]{2,1,0:T(8,128)(2,1)S(1)}, u32[]{:S(2)}, u32[]{:S(2)}) collective-permute-start(bf16[16,16,128]{2,1,0:T(8,128)(2,1)S(1)} %pad_maximum_fusion.5), channel_id=1, source_target_pairs={{0,13},{1,12},{4,9},{5,8},{8,5},{9,4},{12,1},{13,0},{2,15},{3,14},... | collective-permute-start | bytes 196616 | tf_op jit(solution)/shard_map/ppermute | solution.py:212
  113.3 13.5 %collective-permute-start.8 = (bf16[4,16,32,128]{3,2,1,0:T(8,128)(2,1)S(1)}, bf16[4,16,32,128]{3,2,1,0:T(8,128)(2,1)S(1)}, u32[]{:S(2)}, u32[]{:S(2)}) collective-permute-start(bf16[4,16,32,128]{3,2,1,0:T(8,128)(2,1)S(1)} %pad_maximum_fusion.1), channel_id=1, source_target_pairs={{0,2},{2,0},{1,3},{3,1},{4,6},{6,4},{5,7},{7,5},{8,10},{10,8},{9,1... | collective-permute-start | bytes 1572872 | tf_op jit(solution)/shard_map/ppermute | solution.py:203
  117.1 7.0 %collective-permute-start.20 = (f32[16,512]{1,0:T(8,128)S(1)}, f32[16,512]{1,0:T(8,128)S(1)}, u32[]{:S(2)}, u32[]{:S(2)}) collective-permute-start(f32[16,512]{1,0:T(8,128)S(1)} %get-tuple-element.37), channel_id=1, source_target_pairs={{0,0},{2,2},{4,4},{6,6},{8,8},{10,10},{12,12},{14,14},{64,78},{66,... | collective-permute-start | bytes 98312 | tf_op jit(solution)/shard_map/ppermute | solution.py:322
  120.4 5.7 %collective-permute-start.21 = (f32[16,512]{1,0:T(8,128)S(1)}, f32[16,512]{1,0:T(8,128)S(1)}, u32[]{:S(2)}, u32[]{:S(2)}) collective-permute-start(f32[16,512]{1,0:T(8,128)S(1)} %get-tuple-element.36), channel_id=1, source_target_pairs={{0,1},{1,0},{2,3},{3,2},{4,5},{5,4},{6,7},{7,6},{8,9},{9,8},{10,11... | collective-permute-start | bytes 98312 | tf_op jit(solution)/shard_map/ppermute | solution.py:323
  (21 other events, 245.7 us)

commit v3 on v1

v3 whole, which is shorter than its diff:
```python
import math

import jax
import jax.numpy as jnp
import numpy as np
from jax import lax
from jax.experimental import pallas as pl
from jax.experimental.pallas import tpu as pltpu
from jax.sharding import Mesh, PartitionSpec as P

F32 = jnp.float32
BF16 = jnp.bfloat16
D = 1024
L = 16384
SCALE = float(2 * L) ** (-0.5)
SIDE = 128
CHIPS = 64
ARRS = 3
ROWS = ARRS * 8
SEQ = ("x", "y", "z", "c")
VMEM = pl.BlockSpec(memory_space=pltpu.VMEM)
SMEM = pl.BlockSpec(memory_space=pltpu.SMEM)


def one_hot_rows(index, width):
    return (index[:, None] == np.arange(width)[None, :]).astype(jnp.bfloat16)


def spread_order():
    orders = []
    for parity in range(2):
        index = []
        for y in range(4):
            for z in range(4):
                for core in range(2):
                    low = [32 * z + 16 * (core ^ parity) + 4 * y + s for s in range(4)]
                    index += low + [2 * SIDE - 1 - d for d in low]
        orders.append(one_hot_rows(np.array(index), 2 * SIDE))
    return np.stack(orders)


def classes(with_z):
    groups = []
    for dp in range(2):
        for core in range(2):
            members = [
                [((16 * x + 4 * y + z) * 2 + (core ^ (x & 1))) * 2 + dp for z in range(4)]
                for x in range(4)
                for y in range(4)
            ]
            if with_z:
                groups.append([member for row in members for member in row])
            else:
                groups += [[row[z] for row in members] for z in range(4)]
    return groups


def by_class(a, with_z):
    return lax.all_to_all(a, SEQ + ("dp",), 0, 0, axis_index_groups=classes(with_z), tiled=True)


def block_order():
    index = []
    for half in range(2):
        for y in range(4):
            for zz in range(4):
                for i in range(16):
                    x, z, q = (y, zz, i) if half == 0 else (3 - y, 3 - zz, 15 - i)
                    index.append((16 * x + 4 * (q // 4) + z) * 8 + 4 * half + q % 4)
    return one_hot_rows(np.array(index), 512)


def tables():
    k = np.arange(SIDE)
    quarter = k + 0.25
    outer = 2 * math.pi / SIDE * np.outer(quarter, k)
    both = np.concatenate([np.cos(outer), -np.sin(outer)], axis=0)
    back = []
    for core in range(2):
        rows = [2 * g + (slot ^ core ^ (g >> 4 & 1)) for g in range(CHIPS) for slot in range(2)]
        back.append(both.T[np.array(rows)])
    twist = 2 * math.pi / L * np.outer(quarter, k)
    inner = 2 * math.pi / SIDE * np.outer(k, k)
    cos, sin = np.cos(inner), np.sin(inner)
    inner_table = np.block([[cos, -sin], [sin, cos]])
    return (
        both.astype(jnp.bfloat16),
        np.stack(back).astype(jnp.bfloat16),
        np.cos(twist).astype(np.float32),
        np.sin(twist).astype(np.float32),
        inner_table.astype(jnp.bfloat16),
        inner_table.T.astype(jnp.bfloat16),
    )


def dot(a, b, ca=1, cb=0):
    return lax.dot_general(a, b, (((ca,), (cb,)), ((), ())), preferred_element_type=F32)


def project_kernel(core, inputs, cot, taps, order, value_w, gate_w, message, give, cot_own, w_buf, cot_buf, sems):
    fetch = [
        pltpu.make_async_copy(w, w_buf.at[i], sems.at[i]) for i, w in enumerate((value_w, gate_w))
    ]
    for copy in fetch:
        copy.start()
    for j in range(8):
        give[j * SIDE:(j + 1) * SIDE, :] = inputs[:, j * SIDE:(j + 1) * SIDE]
    fetch[0].wait()
    value = dot(inputs[...], w_buf[0]).astype(BF16)
    fetch[1].wait()
    gate = dot(inputs[...], w_buf[1])
    mix = (cot[...].astype(F32) * gate).astype(BF16)
    stacked = jnp.concatenate([value, mix, taps[...], cot[...]], axis=0)
    for b in range(4):
        low = stacked[:, b * SIDE:(b + 1) * SIDE]
        high = stacked[:, (7 - b) * SIDE:(8 - b) * SIDE]
        moved = dot(order[b & 1], jnp.concatenate([low, high], axis=1), 1, 1)
        parts = [moved[:, a * SIDE:(a + 1) * SIDE].reshape(32, 8, SIDE) for a in range(4)]
        block = jnp.concatenate(parts[:3], axis=1).reshape(32 * ROWS, SIDE).astype(BF16)
        message[b * 32 * ROWS:(b + 1) * 32 * ROWS, :] = block
        line = parts[3].reshape(16, 2, 8, SIDE)
        for c in range(2):
            rows = line[:, c ^ (b & 1)].reshape(SIDE, SIDE).astype(BF16)
            cot_buf[c ^ core[0], b * SIDE:(b + 1) * SIDE, :] = rows
    cot_own[...] = cot_buf[0]
    give[D:, :] = cot_buf[1]


def inverse(both, outer_tm, cos, sin, inner_tm):
    part = dot(both, inner_tm)
    re, im = part[:, :SIDE], part[:, SIDE:]
    turned = jnp.concatenate([re * cos - im * sin, re * sin + im * cos], axis=0)
    return dot(outer_tm, turned.astype(BF16)) * (1.0 / L)


def convolve_kernel(core, signal, outer, outer_t, tw_re, tw_im, inner, inner_t, result, flat, spec):
    flat[...] = signal[...].astype(F32)
    outer_m = outer[...]
    outer_tm = outer_t[core[0]]
    cos = tw_re[...]
    sin = tw_im[...]
    inner_m = inner[...]
    inner_tm = inner_t[...]

    for j in range(ROWS):
        sig = flat[pl.ds(j, SIDE, stride=ROWS), :].astype(BF16)
        part = dot(outer_m, sig)
        re, im = part[:SIDE], part[SIDE:]
        turned = jnp.concatenate([re * cos + im * sin, im * cos - re * sin], axis=1)
        spec[j] = dot(turned.astype(BF16), inner_m)

    def back(re, im):
        both = jnp.concatenate([re, im], axis=1).astype(BF16)
        return inverse(both, outer_tm, cos, sin, inner_tm)

    def mul(a, b):
        return (a[0] * b[0] - a[1] * b[1], a[0] * b[1] + a[1] * b[0])

    def mulc(a, b):
        return (a[0] * b[0] + a[1] * b[1], a[0] * b[1] - a[1] * b[0])

    def add(a, b):
        return (a[0] + b[0], a[1] + b[1])

    def load(j):
        both = spec[j]
        return (both[:, :SIDE], both[:, SIDE:])

    for s in range(8):
        t = (s + 4) % 8
        vals, grads, filt = load(s), load(8 + s), load(16 + s)
        vals_f, grads_f, filt_f = load(t), load(8 + t), load(16 + t)
        mixed = back(*add(mul(filt, vals), mulc(filt, vals_f)))
        flat[pl.ds(s, SIDE, stride=ROWS), :] = mixed
        grad = back(*add(mulc(filt, grads), mul(filt_f, grads_f)))
        flat[pl.ds(8 + s, SIDE, stride=ROWS), :] = grad
        part = add(mulc(vals, grads), mulc(grads, vals_f))
        flat[pl.ds(16 + s, SIDE, stride=ROWS), :] = back(*part)
    result[...] = flat[...].astype(BF16)


def weights_kernel(home, blocks, inputs, cot_own, got, partial):
    full = home[...].astype(F32).reshape(CHIPS, 2 * ROWS, SIDE)
    grads, gates = [], []
    for slot, cot in enumerate((cot_own[...], got[D:, :])):
        base = slot * ROWS
        mixed = full[:, base:base + 8].reshape(512, SIDE)
        grads.append(full[:, base + 8:base + 16].reshape(512, SIDE).astype(BF16))
        gates.append((mixed * cot.astype(F32)).astype(BF16))
    for a, group in enumerate((grads, gates)):
        rows = dot(blocks[...], jnp.concatenate(group, axis=1)).astype(BF16)
        for j in range(8):
            cols = slice(j * SIDE, (j + 1) * SIDE)
            pair = jnp.concatenate([inputs[:, cols], got[cols, :]], axis=0)
            partial[a * 512:(a + 1) * 512, cols] = dot(rows, pair).astype(BF16)


def natural_order(stack, order):
    width = stack.shape[3]
    low, high = [], []
    for b in range(4):
        rows = stack[16 * b:16 * b + 16].reshape(2 * SIDE, width).astype(BF16)
        both = dot(rows, order[0], 0, 0)
        low.append(both[:, :SIDE])
        high.insert(0, both[:, SIDE:])
    return jnp.concatenate(low + high, axis=1)


def inputs_kernel(core, cot, order, own, far, value_w, gate_w, input_grad, w_buf, stack, sems):
    fetch = [
        pltpu.make_async_copy(w, w_buf.at[i], sems.at[i]) for i, w in enumerate((value_w, gate_w))
    ]
    for copy in fetch:
        copy.start()
    for side, ref in ((0, own), (1, far)):
        full = ref[...].astype(F32).reshape(CHIPS, ROWS, SIDE)
        stack[:, core[0] ^ side] = jnp.concatenate([full[:, :8], full[:, 8:16]], axis=2)
    natural = natural_order(stack, order)
    gated = (natural[:SIDE] * cot[...].astype(F32)).astype(BF16)
    grad = natural[SIDE:].astype(BF16)
    fetch[0].wait()
    total = dot(grad, w_buf[0], 1, 1)
    fetch[1].wait()
    input_grad[...] = (total + dot(gated, w_buf[1], 1, 1)).astype(BF16)


def filter_kernel(core, order, mine, theirs, filter_grad, stack):
    total = (mine[...].astype(F32) + theirs[...].astype(F32)).reshape(2, CHIPS, 8, SIDE)
    for side in range(2):
        rounded = total[side].astype(BF16).astype(F32)
        stack[:, core[0] ^ side] = jnp.concatenate([rounded, total[side] - rounded], axis=2)
    both = natural_order(stack, order)
    filter_grad[...] = (both[:SIDE] + both[SIDE:]) * SCALE


def shape(*dims, kind=BF16):
    return jax.ShapeDtypeStruct(dims, kind)


def swap_cores(a):
    return lax.ppermute(a, "c", [(0, 1), (1, 0)])


def kernel(name, body, outs, ins, anys=0, scratch=(), gflop=0.1, mbyte=4.0, limit=24):
    return pl.pallas_call(
        body,
        out_shape=outs,
        in_specs=ins + [pl.BlockSpec(memory_space=pl.ANY)] * anys,
        out_specs=[VMEM] * len(outs),
        scratch_shapes=scratch,
        compiler_params=pltpu.CompilerParams(vmem_limit_bytes=limit * 2**20),
        cost_estimate=pl.CostEstimate(
            flops=int(gflop * 1e9), bytes_accessed=int(mbyte * 2**20), transcendentals=0
        ),
        name=name,
    )


def local(inputs, cotangent, value_weight, gate_weight, filter_taps):
    odd = lax.axis_index("x").astype(jnp.int32) & 1
    core = (lax.axis_index("c").astype(jnp.int32) ^ odd).reshape(1)
    order = jnp.asarray(spread_order())
    flat_in = inputs.reshape(SIDE, D)
    cot = cotangent.reshape(SIDE, D)
    w_scratch = pltpu.VMEM((2, D, D), BF16)
    sems = pltpu.SemaphoreType.DMA((2,))

    message, give, cot_own = kernel(
        "project",
        project_kernel,
        [shape(2 * CHIPS * ROWS, SIDE), shape(1536, SIDE), shape(512, SIDE)],
        [SMEM] + [VMEM] * 4,
        2,
        [w_scratch, pltpu.VMEM((2, 512, SIDE), BF16), sems],
        0.8,
        8.0,
        56,
    )(core, flat_in, cot, filter_taps, order, value_weight, gate_weight)
    spread = lax.all_to_all(message.reshape(2 * CHIPS, ROWS, SIDE), SEQ, 0, 0, tiled=True)
    got = swap_cores(give)

    (result,) = kernel(
        "convolve",
        convolve_kernel,
        [shape(2 * CHIPS * ROWS, SIDE)],
        [SMEM] + [VMEM] * 7,
        0,
        [
            pltpu.VMEM((2 * CHIPS * ROWS, SIDE), F32),
            pltpu.VMEM((ROWS, SIDE, 2 * SIDE), F32),
        ],
        1.2,
        4.0,
    )(core, spread.reshape(2 * CHIPS * ROWS, SIDE), *[jnp.asarray(t) for t in tables()])
    home = by_class(result.reshape(CHIPS, 2 * ROWS, SIDE), True)

    (partial,) = kernel(
        "weights", weights_kernel, [shape(D, D)], [VMEM] * 5, gflop=0.6, mbyte=4.0, limit=56
    )(home.reshape(2 * CHIPS * ROWS, SIDE), jnp.asarray(block_order()), flat_in, cot_own, got)
    parts = by_class(partial, False)

    own = home[:, :ROWS]
    far = swap_cores(home[:, ROWS:])
    filter_part = jnp.stack([own[:, 16:], far[:, 16:]]).reshape(1024, SIDE)
    filter_other = lax.ppermute(filter_part, "dp", [(0, 1), (1, 0)])
    (input_grad,) = kernel(
        "input_grad",
        inputs_kernel,
        [shape(SIDE, D)],
        [SMEM] + [VMEM] * 4,
        2,
        [w_scratch, pltpu.VMEM((CHIPS, 2, 8, 2 * SIDE), F32), sems],
        0.7,
        8.0,
        56,
    )(core, cot, order, own.reshape(1536, SIDE), far.reshape(1536, SIDE), value_weight, gate_weight)
    (filter_grad,) = kernel(
        "filter_grad",
        filter_kernel,
        [shape(SIDE, D, kind=F32)],
        [SMEM] + [VMEM] * 3,
        0,
        [pltpu.VMEM((CHIPS, 2, 8, 2 * SIDE), F32)],
        0.1,
        2.0,
    )(core, order, filter_part, filter_other)

    parts, input_grad, filter_grad = lax.optimization_barrier((parts, input_grad, filter_grad))
    sums = jnp.sum(parts.reshape(16, 64, D).astype(F32), axis=0).astype(BF16)
    sums = sums.reshape(4, 16, 2, 512).transpose(0, 2, 1, 3).reshape(8, 16, 512)
    final = lax.all_to_all(sums, ("z", "dp"), 0, 0, tiled=True)
    projection_grads = jnp.sum(final.astype(F32), axis=0) * SCALE
    return (input_grad.reshape(1, SIDE, D), projection_grads, filter_grad)


def solution(mesh):
    fine = Mesh(mesh.devices.reshape(4, 4, 4, 2, 2), SEQ + ("dp",))
    in_specs = (P("dp", SEQ, None), P("dp", SEQ, None), P(), P(), P(SEQ, None))
    out_specs = (P("dp", SEQ, None), P(SEQ, "dp"), P(SEQ, None))
    return jax.shard_map(local, mesh=fine, in_specs=in_specs, out_specs=out_specs, check_vma=False)
```

time: 146 us -> 131 us (0.90)
  waiting for transfers between devices: 58.2 us -> 40.2 us
  blocking collectives: 34.9 us -> 50.4 us
  starting transfers between devices: 22.2 us -> 15.9 us
  other arithmetic: 3.32 us -> 1.07 us
  local copies, waits for them, and re-layouts: 3.86 us -> 1.89 us
    all_to_all x3 -> x2, waiting for transfers between devices: 48.4 us -> 29 us  [by_class(): lax.all_to_all(a, SEQ + ('dp',), 0, 0, axis_index_groups=classes(with_z),...]
    all_to_all x1 -> x2, blocking collectives: 34.9 us -> 50.4 us  [the longest x1 35 us: local(): lax.all_to_all(message.reshape(2 * CHIPS, ROWS, SIDE), SEQ, 0, 0, tiled=T...]
    all_to_all x3 -> x2, starting transfers between devices: 16.5 us -> 11 us  [by_class(): lax.all_to_all(a, SEQ + ('dp',), 0, 0, axis_index_groups=classes(with_z),...]
    pallas_call x4 -> x5, Pallas kernels: 21.7 us -> 20.8 us  [the longest x1 5.75 us: local(): kernel('input_grad', inputs_kernel, [shape(SIDE, D)], [SMEM] + [VMEM] * 4...]
    ppermute x4 -> x2, waiting for transfers between devices: 3.15 us -> 3.42 us  [swap_cores(): return lax.ppermute(a, 'c', [(0, 1), (1, 0)])]
  transfers between devices with their start and end apart: 9 -> 5, of which waited for: 5 -> 5; matrix products, arithmetic and copies ran while one was open for 3% -> 1% of each run, Pallas kernels for 4% -> 5%
where the time goes in v3:
time: 131 us
  blocking collectives  50.4 us (38%)
  waiting for transfers between devices  40.2 us (31%)
  Pallas kernels  20.8 us (16%)
  starting transfers between devices  15.9 us (12%)
  local copies, waits for them, and re-layouts  1.89 us (1%)
    all_to_all x1, blocking collectives, local(): lax.all_to_all(message.reshape(2 * CHIPS, ROWS, SIDE), SEQ, 0, 0, tiled=T...  35 us
    all_to_all x2, waiting for transfers between devices, by_class(): lax.all_to_all(a, SEQ + ('dp',), 0, 0, axis_index_groups=classes(with_z),...  29 us
    all_to_all x1, blocking collectives, local(): final = lax.all_to_all(sums, ('z', 'dp'), 0, 0, tiled=True)  15.4 us
    all_to_all x2, starting transfers between devices, by_class(): lax.all_to_all(a, SEQ + ('dp',), 0, 0, axis_index_groups=classes(with_z),...  11 us
    ppermute x1, waiting for transfers between devices, local(): filter_other = lax.ppermute(filter_part, 'dp', [(0, 1), (1, 0)])  7.71 us
    pallas_call x1, Pallas kernels, local(): kernel('input_grad', inputs_kernel, [shape(SIDE, D)], [SMEM] + [VMEM] * 4...  5.75 us
    pallas_call x1, Pallas kernels, local(): kernel('project', project_kernel, [shape(2 * CHIPS * ROWS, SIDE), shape(1...  5.4 us
    ppermute x1, starting transfers between devices, local(): filter_other = lax.ppermute(filter_part, 'dp', [(0, 1), (1, 0)])  4.76 us
  transfers between devices with their start and end apart: 5, of which 5 were waited for; matrix products, arithmetic and copies ran while one was open for 1% of the time, Pallas kernels for 5%

profile of v3, /device:TPU:32, one launch (start us, length us, event | category | flops | bytes accessed | tf_op | source)
XLA Modules:
  0.0 131.1 jit_solution(5036762967457509975)
XLA Ops:
  0.6 0.0 copy-start.1
  0.6 0.0 copy-start.2
  0.7 0.0 copy-start.3
  0.7 5.4 %project.1 = (bf16[3072,128]{1,0:T(8,128)(2,1)}, bf16[1536,128]{1,0:T(8,128)(2,1)}, bf16[512,128]{1,0:T(8,128)(2,1)}) custom-call(s32[1]{0:T(128)} %bitcast.core, bf16[128,1024]{1,0:T(8,128)(2,1)} %bitcast.26, bf16[128,1024]{1,0:T(8,128)(2,1)} %bitcast.28, bf16[128,1024]{1,0:T(8,128)(2,1)} %taps.1, bf16[2,256,256]{2,1,0:T(8,128)(2,1)} %constant.34.clone.order, ...), custom_call_target="tpu_custom_call" | custom-call | flops 800000000 | bytes 8388608 | tf_op jit(solution)/shard_map/project/pallas_call | solution.py:268
  6.1 35.0 %all_to_all.27 = bf16[128,24,128]{2,1,0:T(8,128)(2,1)S(1)} all-to-all(bf16[128,24,128]{2,1,0:T(8,128)(2,1)} %bitcast.30), channel_id=1, replica_groups=mesh['x'=4,'y'=4,'z'=4,'c'=2,'dp'=2] {'x','y','z','c'}, dimensions={0} | all-to-all | bytes 1572864 | tf_op jit(solution)/shard_map/all_to_all | solution.py:279
  41.2 3.6 %convolve.1 = bf16[3072,128]{1,0:T(8,128)(2,1)} custom-call(s32[1]{0:T(128)} %bitcast.core, bf16[3072,128]{1,0:T(8,128)(2,1)S(1)} %bitcast.22, bf16[256,128]{1,0:T(8,128)(2,1)S(1)} %copy-done.6, bf16[2,128,256]{2,1,0:T(8,128)(2,1)S(1)} %copy-done.3, f32[128,128]{1,0:T(8,128)S(1)} %copy-done.5, f32[128,128]{1,0:T(8,128)S(1)} %copy-done.4, ...), custom_call_target="tpu_custom_call" | custom-call | flops 1200000000 | bytes 4194304 | tf_op jit(solution)/shard_map/convolve/pallas_call | solution.py:282
  44.9 7.2 %all-to-all-start.1 = ((bf16[64,48,128]{2,1,0:T(8,128)(2,1)}), bf16[64,48,128]{2,1,0:T(8,128)(2,1)S(1)}, u32[]{:S(2)}, u32[]{:S(2)}) async-start(bf16[64,48,128]{2,1,0:T(8,128)(2,1)} %bitcast.5), calls=%async_computation.1 | async-start | bytes 1572864 | tf_op jit(solution)/shard_map/all_to_all | solution.py:59
  52.1 0.1 collective-permute-start
  52.2 1.7 %collective-permute-done.got = bf16[1536,128]{1,0:T(8,128)(2,1)S(1)} collective-permute-done((bf16[1536,128]{1,0:T(8,128)(2,1)S(1)}, bf16[1536,128]{1,0:T(8,128)(2,1)S(1)}, u32[]{:S(2)}, u32[]{:S(2)}) %collective-permute-start) | collective-permute-done | bytes 393248 | tf_op jit(solution)/shard_map/ppermute | solution.py:241
  53.9 20.8 %all-to-all-done.1 = bf16[64,48,128]{2,1,0:T(8,128)(2,1)S(1)} async-done(((bf16[64,48,128]{2,1,0:T(8,128)(2,1)}), bf16[64,48,128]{2,1,0:T(8,128)(2,1)S(1)}, u32[]{:S(2)}, u32[]{:S(2)}) %all-to-all-start.1) | async-done | bytes 786464 | tf_op jit(solution)/shard_map/all_to_all | solution.py:59
  74.7 0.9 copy-done.7
  75.6 4.6 %weights.1 = bf16[1024,1024]{1,0:T(8,128)(2,1)} custom-call(bf16[3072,128]{1,0:T(8,128)(2,1)} %bitcast.24, bf16[512,512]{1,0:T(8,128)(2,1)} %constant.41.clone.blocks, bf16[128,1024]{1,0:T(8,128)(2,1)} %bitcast.27, bf16[512,128]{1,0:T(8,128)(2,1)} %get-tuple-element.10.cot_own, bf16[1536,128]{1,0:T(8,128)(2,1)} %copy-done.10), custom_call_target="tpu_custom_call" | custom-call | flops 600000000 | bytes 4194304 | tf_op jit(solution)/shard_map/weights/pallas_call | solution.py:297
  80.2 3.8 %all-to-all-start.2 = ((bf16[16,64,1024]{2,1,0:T(8,128)(2,1)}), bf16[16,64,1024]{2,1,0:T(8,128)(2,1)S(1)}, u32[]{:S(2)}, u32[]{:S(2)}) async-start(bf16[16,64,1024]{2,1,0:T(8,128)(2,1)} %bitcast.23), calls=%async_computation.2 | async-start | bytes 4194304 | tf_op jit(solution)/shard_map/all_to_all | solution.py:59
  84.0 0.8 fusion
  84.9 1.7 %collective-permute-done.1 = bf16[64,24,128]{2,1,0:T(8,128)(2,1)S(1)} collective-permute-done((bf16[64,24,128]{2,1,0:T(8,128)(2,1)S(1)}, bf16[64,24,128]{2,1,0:T(8,128)(2,1)S(1)}, u32[]{:S(2)}, u32[]{:S(2)}) %collective-permute-start.1) | collective-permute-done | bytes 393248 | tf_op jit(solution)/shard_map/ppermute | solution.py:241
  86.6 4.8 %collective-permute-start.2 = (bf16[1024,128]{1,0:T(8,128)(2,1)S(1)}, bf16[1024,128]{1,0:T(8,128)(2,1)S(1)}, u32[]{:S(2)}, u32[]{:S(2)}) collective-permute-start(bf16[1024,128]{1,0:T(8,128)(2,1)S(1)} %bitcast.20), channel_id=1, source_target_pairs={{0,1},{1,0},{2,3},{3,2},{4,5},{5,4},{6,7},{7,6},{8,9},{9,8},{10,11... | collective-permute-start | bytes 786440 | tf_op jit(solution)/shard_map/ppermute | solution.py:305
  91.4 5.8 %input_grad.1 = bf16[128,1024]{1,0:T(8,128)(2,1)} custom-call(s32[1]{0:T(128)} %bitcast.core, bf16[128,1024]{1,0:T(8,128)(2,1)} %bitcast.29, bf16[2,256,256]{2,1,0:T(8,128)(2,1)} %constant.34.clone.order, bf16[1536,128]{1,0:T(8,128)(2,1)} %bitcast.25, bf16[1536,128]{1,0:T(8,128)(2,1)} %bitcast.31, bf16[1024,1024]{1,0:T(8,128)(2,1)} %value_w.3, ...), custom_call_target="tpu_custom_call" | custom-call | flops 700000000 | bytes 8388608 | tf_op jit(solution)/shard_map/input_grad/pallas_call | solution.py:306
  97.2 7.7 %collective-permute-done.2.theirs = bf16[1024,128]{1,0:T(8,128)(2,1)S(1)} collective-permute-done((bf16[1024,128]{1,0:T(8,128)(2,1)S(1)}, bf16[1024,128]{1,0:T(8,128)(2,1)S(1)}, u32[]{:S(2)}, u32[]{:S(2)}) %collective-permute-start.2) | collective-permute-done | bytes 262176 | tf_op jit(solution)/shard_map/ppermute | solution.py:305
  104.9 1.4 %filter_grad.1 = f32[128,1024]{1,0:T(8,128)} custom-call(s32[1]{0:T(128)} %bitcast.core, bf16[2,256,256]{2,1,0:T(8,128)(2,1)S(1)} %copy-done, bf16[1024,128]{1,0:T(8,128)(2,1)S(1)} %bitcast.21, bf16[1024,128]{1,0:T(8,128)(2,1)S(1)} %collective-permute-done.2.theirs), custom_call_target="tpu_custom_call" | custom-call | flops 100000000 | bytes 2097152 | tf_op jit(solution)/shard_map/filter_grad/pallas_call | solution.py:317
  106.3 8.3 %all-to-all-done.2 = bf16[16,64,1024]{2,1,0:T(8,128)(2,1)S(1)} async-done(((bf16[16,64,1024]{2,1,0:T(8,128)(2,1)}), bf16[16,64,1024]{2,1,0:T(8,128)(2,1)S(1)}, u32[]{:S(2)}, u32[]{:S(2)}) %all-to-all-start.2) | async-done | bytes 2097184 | tf_op jit(solution)/shard_map/all_to_all | solution.py:59
  114.5 0.4 reduce_sum.21
  114.9 0.1 reshape.62
  115.0 15.4 %all_to_all.28 = bf16[8,16,512]{2,1,0:T(8,128)(2,1)S(1)} all-to-all(bf16[8,16,512]{2,1,0:T(8,128)(2,1)S(1)} %bitcast.33), channel_id=1, replica_groups=mesh['x'=4,'y'=4,'z'=4,'c'=2,'dp'=2] {'z','dp'}, dimensions={0} | all-to-all | bytes 262144 | tf_op jit(solution)/shard_map/all_to_all | solution.py:331
  130.4 0.6 broadcast_multiply_fusion
  (26 shorter events, 0.1 us)
Async XLA Ops:
  0.6 40.5 %copy-start.1 = (bf16[256,256]{1,0:T(8,128)(2,1)S(1)}, bf16[256,256]{1,0:T(8,128)(2,1)}, u32[]{:S(2)}) copy-start(bf16[256,256]{1,0:T(8,128)(2,1)} %constant.40.clone.inner_t) | copy-start | bytes 393220
  0.6 40.5 %copy-start.2 = (bf16[256,256]{1,0:T(8,128)(2,1)S(1)}, bf16[256,256]{1,0:T(8,128)(2,1)}, u32[]{:S(2)}) copy-start(bf16[256,256]{1,0:T(8,128)(2,1)} %constant.39.clone.inner) | copy-start | bytes 393220
  0.7 40.5 %copy-start.3 = (bf16[2,128,256]{2,1,0:T(8,128)(2,1)S(1)}, bf16[2,128,256]{2,1,0:T(8,128)(2,1)}, u32[]{:S(2)}) copy-start(bf16[2,128,256]{2,1,0:T(8,128)(2,1)} %constant.36.clone.outer_t) | copy-start | bytes 393220
  0.7 40.5 %copy-start.4 = (f32[128,128]{1,0:T(8,128)S(1)}, f32[128,128]{1,0:T(8,128)}, u32[]{:S(2)}) copy-start(f32[128,128]{1,0:T(8,128)} %constant.38.clone.tw_im) | copy-start | bytes 196612
  0.7 40.5 %copy-start.5 = (f32[128,128]{1,0:T(8,128)S(1)}, f32[128,128]{1,0:T(8,128)}, u32[]{:S(2)}) copy-start(f32[128,128]{1,0:T(8,128)} %constant.37.clone.tw_re) | copy-start | bytes 196612
  0.7 40.5 %copy-start.6 = (bf16[256,128]{1,0:T(8,128)(2,1)S(1)}, bf16[256,128]{1,0:T(8,128)(2,1)}, u32[]{:S(2)}) copy-start(bf16[256,128]{1,0:T(8,128)(2,1)} %constant.35.clone.outer) | copy-start | bytes 196612
  41.2 10.8 %copy-start.11 = (bf16[1536,128]{1,0:T(8,128)(2,1)S(1)}, bf16[1536,128]{1,0:T(8,128)(2,1)}, u32[]{:S(2)}) copy-start(bf16[1536,128]{1,0:T(8,128)(2,1)} %get-tuple-element.11) | copy-start | bytes 1179652
  44.9 29.8 %all-to-all-start.1 = ((bf16[64,48,128]{2,1,0:T(8,128)(2,1)}), bf16[64,48,128]{2,1,0:T(8,128)(2,1)S(1)}, u32[]{:S(2)}, u32[]{:S(2)}) async-start(bf16[64,48,128]{2,1,0:T(8,128)(2,1)} %bitcast.5), calls=%async_computation.1 | async-start | bytes 1572864 | tf_op jit(solution)/shard_map/all_to_all | solution.py:59
  52.1 1.8 %collective-permute-start = (bf16[1536,128]{1,0:T(8,128)(2,1)S(1)}, bf16[1536,128]{1,0:T(8,128)(2,1)S(1)}, u32[]{:S(2)}, u32[]{:S(2)}) collective-permute-start(bf16[1536,128]{1,0:T(8,128)(2,1)S(1)} %copy-done.11), channel_id=1, source_target_pairs={{0,2},{2,0},{1,3},{3,1},{4,6},{6,4},{5,7},{7,5},{8,10},{10,8},{9,1... | collective-permute-start | bytes 1179656 | tf_op jit(solution)/shard_map/ppermute | solution.py:241
  53.9 20.8 %copy-start.10 = (bf16[1536,128]{1,0:T(8,128)(2,1)}, bf16[1536,128]{1,0:T(8,128)(2,1)S(1)}, u32[]{:S(2)}) copy-start(bf16[1536,128]{1,0:T(8,128)(2,1)S(1)} %collective-permute-done.got) | copy-start | bytes 1179652
  74.7 0.9 copy-start.7
  80.2 3.9 %copy-start.8 = (bf16[64,48,128]{2,1,0:T(8,128)(2,1)S(1)}, bf16[64,48,128]{2,1,0:T(8,128)(2,1)}, u32[]{:S(2)}) copy-start(bf16[64,48,128]{2,1,0:T(8,128)(2,1)} %copy-done.7) | copy-start | bytes 2359300
  80.2 34.3 %all-to-all-start.2 = ((bf16[16,64,1024]{2,1,0:T(8,128)(2,1)}), bf16[16,64,1024]{2,1,0:T(8,128)(2,1)S(1)}, u32[]{:S(2)}, u32[]{:S(2)}) async-start(bf16[16,64,1024]{2,1,0:T(8,128)(2,1)} %bitcast.23), calls=%async_computation.2 | async-start | bytes 4194304 | tf_op jit(solution)/shard_map/all_to_all | solution.py:59
  84.9 1.7 %collective-permute-start.1 = (bf16[64,24,128]{2,1,0:T(8,128)(2,1)S(1)}, bf16[64,24,128]{2,1,0:T(8,128)(2,1)S(1)}, u32[]{:S(2)}, u32[]{:S(2)}) collective-permute-start(bf16[64,24,128]{2,1,0:T(8,128)(2,1)S(1)} %get-tuple-element.15), channel_id=1, source_target_pairs={{0,2},{2,0},{1,3},{3,1},{4,6},{6,4},{5,7},{7,5},{8,10},{10,8},{9,1... | collective-permute-start | bytes 1179656 | tf_op jit(solution)/shard_map/ppermute | solution.py:241
  86.6 4.8 %copy-start.9 = (bf16[64,24,128]{2,1,0:T(8,128)(2,1)}, bf16[64,24,128]{2,1,0:T(8,128)(2,1)S(1)}, u32[]{:S(2)}) copy-start(bf16[64,24,128]{2,1,0:T(8,128)(2,1)S(1)} %collective-permute-done.1) | copy-start | bytes 1179652
  86.6 18.2 %collective-permute-start.2 = (bf16[1024,128]{1,0:T(8,128)(2,1)S(1)}, bf16[1024,128]{1,0:T(8,128)(2,1)S(1)}, u32[]{:S(2)}, u32[]{:S(2)}) collective-permute-start(bf16[1024,128]{1,0:T(8,128)(2,1)S(1)} %bitcast.20), channel_id=1, source_target_pairs={{0,1},{1,0},{2,3},{3,2},{4,5},{5,4},{6,7},{7,6},{8,9},{9,8},{10,11... | collective-permute-start | bytes 786440 | tf_op jit(solution)/shard_map/ppermute | solution.py:305
  91.4 13.5 %copy-start = (bf16[2,256,256]{2,1,0:T(8,128)(2,1)S(1)}, bf16[2,256,256]{2,1,0:T(8,128)(2,1)}, u32[]{:S(2)}) copy-start(bf16[2,256,256]{2,1,0:T(8,128)(2,1)} %constant.34.clone.order) | copy-start | bytes 786436

commit v4 on v3

--- a/solution.py
+++ b/solution.py
@@ -17,7 +17,7 @@
 CHIPS = 64
 ARRS = 3
 ROWS = ARRS * 8
-SEQ = ("x", "y", "z", "c")
+SEQ = ("x1", "x0", "y", "z", "c")
 VMEM = pl.BlockSpec(memory_space=pltpu.VMEM)
 SMEM = pl.BlockSpec(memory_space=pltpu.SMEM)
 
@@ -27,36 +27,13 @@
 
 
 def spread_order():
-    orders = []
-    for parity in range(2):
-        index = []
-        for y in range(4):
-            for z in range(4):
-                for core in range(2):
-                    low = [32 * z + 16 * (core ^ parity) + 4 * y + s for s in range(4)]
-                    index += low + [2 * SIDE - 1 - d for d in low]
-        orders.append(one_hot_rows(np.array(index), 2 * SIDE))
-    return np.stack(orders)
-
-
-def classes(with_z):
-    groups = []
-    for dp in range(2):
-        for core in range(2):
-            members = [
-                [((16 * x + 4 * y + z) * 2 + (core ^ (x & 1))) * 2 + dp for z in range(4)]
-                for x in range(4)
-                for y in range(4)
-            ]
-            if with_z:
-                groups.append([member for row in members for member in row])
-            else:
-                groups += [[row[z] for row in members] for z in range(4)]
-    return groups
-
-
-def by_class(a, with_z):
-    return lax.all_to_all(a, SEQ + ("dp",), 0, 0, axis_index_groups=classes(with_z), tiled=True)
+    index = []
+    for y in range(4):
+        for z in range(4):
+            for core in range(2):
+                low = [32 * z + 16 * core + 4 * y + s for s in range(4)]
+                index += low + [2 * SIDE - 1 - d for d in low]
+    return one_hot_rows(np.array(index), 2 * SIDE)
 
 
 def block_order():
@@ -77,7 +54,7 @@
     both = np.concatenate([np.cos(outer), -np.sin(outer)], axis=0)
     back = []
     for core in range(2):
-        rows = [2 * g + (slot ^ core ^ (g >> 4 & 1)) for g in range(CHIPS) for slot in range(2)]
+        rows = [2 * g + (slot ^ core) for g in range(CHIPS) for slot in range(2)]
         back.append(both.T[np.array(rows)])
     twist = 2 * math.pi / L * np.outer(quarter, k)
     inner = 2 * math.pi / SIDE * np.outer(k, k)
@@ -97,14 +74,12 @@
     return lax.dot_general(a, b, (((ca,), (cb,)), ((), ())), preferred_element_type=F32)
 
 
-def project_kernel(core, inputs, cot, taps, order, value_w, gate_w, message, give, cot_own, w_buf, cot_buf, sems):
+def project_kernel(core, inputs, cot, taps, order, value_w, gate_w, message, cot_own, cot_give, w_buf, cot_buf, sems):
     fetch = [
         pltpu.make_async_copy(w, w_buf.at[i], sems.at[i]) for i, w in enumerate((value_w, gate_w))
     ]
     for copy in fetch:
         copy.start()
-    for j in range(8):
-        give[j * SIDE:(j + 1) * SIDE, :] = inputs[:, j * SIDE:(j + 1) * SIDE]
     fetch[0].wait()
     value = dot(inputs[...], w_buf[0]).astype(BF16)
     fetch[1].wait()
@@ -114,16 +89,16 @@
     for b in range(4):
         low = stacked[:, b * SIDE:(b + 1) * SIDE]
         high = stacked[:, (7 - b) * SIDE:(8 - b) * SIDE]
-        moved = dot(order[b & 1], jnp.concatenate([low, high], axis=1), 1, 1)
+        moved = dot(order[...], jnp.concatenate([low, high], axis=1), 1, 1)
         parts = [moved[:, a * SIDE:(a + 1) * SIDE].reshape(32, 8, SIDE) for a in range(4)]
         block = jnp.concatenate(parts[:3], axis=1).reshape(32 * ROWS, SIDE).astype(BF16)
         message[b * 32 * ROWS:(b + 1) * 32 * ROWS, :] = block
         line = parts[3].reshape(16, 2, 8, SIDE)
         for c in range(2):
-            rows = line[:, c ^ (b & 1)].reshape(SIDE, SIDE).astype(BF16)
+            rows = line[:, c].reshape(SIDE, SIDE).astype(BF16)
             cot_buf[c ^ core[0], b * SIDE:(b + 1) * SIDE, :] = rows
     cot_own[...] = cot_buf[0]
-    give[D:, :] = cot_buf[1]
+    cot_give[...] = cot_buf[1]
 
 
 def inverse(both, outer_tm, cos, sin, inner_tm):
@@ -179,20 +154,28 @@
     result[...] = flat[...].astype(BF16)
 
 
-def weights_kernel(home, blocks, inputs, cot_own, got, partial):
+def gate_kernel(odd, home, blocks, cot_own, cot_other, keep, send):
     full = home[...].astype(F32).reshape(CHIPS, 2 * ROWS, SIDE)
     grads, gates = [], []
-    for slot, cot in enumerate((cot_own[...], got[D:, :])):
+    for slot, cot in enumerate((cot_own, cot_other)):
         base = slot * ROWS
         mixed = full[:, base:base + 8].reshape(512, SIDE)
         grads.append(full[:, base + 8:base + 16].reshape(512, SIDE).astype(BF16))
-        gates.append((mixed * cot.astype(F32)).astype(BF16))
+        gates.append((mixed * cot[...].astype(F32)).astype(BF16))
     for a, group in enumerate((grads, gates)):
-        rows = dot(blocks[...], jnp.concatenate(group, axis=1)).astype(BF16)
-        for j in range(8):
-            cols = slice(j * SIDE, (j + 1) * SIDE)
-            pair = jnp.concatenate([inputs[:, cols], got[cols, :]], axis=0)
-            partial[a * 512:(a + 1) * 512, cols] = dot(rows, pair).astype(BF16)
+        rows = dot(blocks[...], jnp.concatenate(group, axis=1))
+        low, high = rows[:256], rows[256:]
+        keep[a * 256:(a + 1) * 256, :] = jnp.where(odd[0] == 1, high, low).astype(BF16)
+        send[a * 256:(a + 1) * 256, :] = jnp.where(odd[0] == 1, low, high).astype(BF16)
+
+
+def weights_kernel(odd, mine, theirs, inputs, in_other, next_in, next_other, partial):
+    total = 0.0
+    for rows, one, two in ((mine, inputs, in_other), (theirs, next_in, next_other)):
+        first = jnp.where(odd[0] == 1, two[...], one[...])
+        second = jnp.where(odd[0] == 1, one[...], two[...])
+        total = total + dot(rows[...], jnp.concatenate([first, second], axis=0))
+    partial[...] = total.astype(BF16)
 
 
 def natural_order(stack, order):
@@ -200,7 +183,7 @@
     low, high = [], []
     for b in range(4):
         rows = stack[16 * b:16 * b + 16].reshape(2 * SIDE, width).astype(BF16)
-        both = dot(rows, order[0], 0, 0)
+        both = dot(rows, order[...], 0, 0)
         low.append(both[:, :SIDE])
         high.insert(0, both[:, SIDE:])
     return jnp.concatenate(low + high, axis=1)
@@ -256,19 +239,30 @@
     )
 
 
+def pair_rows(a, cross):
+    pairs = []
+    for x1 in range(2):
+        for x0 in range(2):
+            for c in range(2):
+                x_to = x0 ^ 1 if cross else x0
+                c_to = c ^ x_to
+                pairs.append(((2 * x1 + x0) * 2 + c, (2 * x1 + x_to) * 2 + c_to))
+    return lax.ppermute(a, ("x1", "x0", "c"), pairs)
+
+
 def local(inputs, cotangent, value_weight, gate_weight, filter_taps):
-    odd = lax.axis_index("x").astype(jnp.int32) & 1
-    core = (lax.axis_index("c").astype(jnp.int32) ^ odd).reshape(1)
+    core = lax.axis_index("c").astype(jnp.int32).reshape(1)
+    odd = lax.axis_index("x0").astype(jnp.int32).reshape(1)
     order = jnp.asarray(spread_order())
     flat_in = inputs.reshape(SIDE, D)
     cot = cotangent.reshape(SIDE, D)
     w_scratch = pltpu.VMEM((2, D, D), BF16)
     sems = pltpu.SemaphoreType.DMA((2,))
 
-    message, give, cot_own = kernel(
+    message, cot_own, cot_give = kernel(
         "project",
         project_kernel,
-        [shape(2 * CHIPS * ROWS, SIDE), shape(1536, SIDE), shape(512, SIDE)],
+        [shape(2 * CHIPS * ROWS, SIDE), shape(512, SIDE), shape(512, SIDE)],
         [SMEM] + [VMEM] * 4,
         2,
         [w_scratch, pltpu.VMEM((2, 512, SIDE), BF16), sems],
@@ -277,7 +271,10 @@
         56,
     )(core, flat_in, cot, filter_taps, order, value_weight, gate_weight)
     spread = lax.all_to_all(message.reshape(2 * CHIPS, ROWS, SIDE), SEQ, 0, 0, tiled=True)
-    got = swap_cores(give)
+    cot_other = swap_cores(cot_give)
+    in_other = swap_cores(flat_in)
+    next_in = lax.ppermute(flat_in, "x0", [(0, 1), (1, 0)])
+    next_other = swap_cores(next_in)
 
     (result,) = kernel(
         "convolve",
@@ -292,12 +289,17 @@
         1.2,
         4.0,
     )(core, spread.reshape(2 * CHIPS * ROWS, SIDE), *[jnp.asarray(t) for t in tables()])
-    home = by_class(result.reshape(CHIPS, 2 * ROWS, SIDE), True)
-
+    home = lax.all_to_all(result.reshape(CHIPS, 2 * ROWS, SIDE), SEQ[:4], 0, 0, tiled=True)
+
+    keep, send = kernel("gate", gate_kernel, [shape(512, 256)] * 2, [SMEM] + [VMEM] * 4, gflop=0.3, mbyte=2.0)(
+        odd, home.reshape(2 * CHIPS * ROWS, SIDE), jnp.asarray(block_order()), cot_own, cot_other
+    )
+    mine = pair_rows(keep, False)
+    theirs = pair_rows(send, True)
     (partial,) = kernel(
-        "weights", weights_kernel, [shape(D, D)], [VMEM] * 5, gflop=0.6, mbyte=4.0, limit=56
-    )(home.reshape(2 * CHIPS * ROWS, SIDE), jnp.asarray(block_order()), flat_in, cot_own, got)
-    parts = by_class(partial, False)
+        "weights", weights_kernel, [shape(512, D)], [SMEM] + [VMEM] * 6, gflop=0.6, mbyte=4.0, limit=56
+    )(odd, mine, theirs, flat_in, in_other, next_in, next_other)
+    parts = lax.all_to_all(partial, ("x1", "y"), 0, 0, tiled=True)
 
     own = home[:, :ROWS]
     far = swap_cores(home[:, ROWS:])
@@ -325,8 +327,7 @@
         2.0,
     )(core, order, filter_part, filter_other)
 
-    parts, input_grad, filter_grad = lax.optimization_barrier((parts, input_grad, filter_grad))
-    sums = jnp.sum(parts.reshape(16, 64, D).astype(F32), axis=0).astype(BF16)
+    sums = jnp.sum(parts.reshape(8, 64, D).astype(F32), axis=0).astype(BF16)
     sums = sums.reshape(4, 16, 2, 512).transpose(0, 2, 1, 3).reshape(8, 16, 512)
     final = lax.all_to_all(sums, ("z", "dp"), 0, 0, tiled=True)
     projection_grads = jnp.sum(final.astype(F32), axis=0) * SCALE
@@ -334,7 +335,7 @@
 
 
 def solution(mesh):
-    fine = Mesh(mesh.devices.reshape(4, 4, 4, 2, 2), SEQ + ("dp",))
+    fine = Mesh(mesh.devices.reshape(2, 2, 4, 4, 2, 2), SEQ + ("dp",))
     in_specs = (P("dp", SEQ, None), P("dp", SEQ, None), P(), P(), P(SEQ, None))
     out_specs = (P("dp", SEQ, None), P(SEQ, "dp"), P(SEQ, None))
     return jax.shard_map(local, mesh=fine, in_specs=in_specs, out_specs=out_specs, check_vma=False)

time: 131 us -> 125 us (0.954)
  blocking collectives: 50.4 us -> 35 us
  starting transfers between devices: 15.9 us -> 27.3 us
  waiting for transfers between devices: 40.2 us -> 37.8 us
    ppermute x0 -> x3, waiting for transfers between devices: none -> 18.3 us  [the longest x1 11.4 us: local(): next_in = lax.ppermute(flat_in, 'x0', [(0, 1), (1, 0)])]
    all_to_all x1 -> x0, blocking collectives: 15.4 us -> none  [local(): final = lax.all_to_all(sums, ('z', 'dp'), 0, 0, tiled=True)]
    all_to_all x2 -> x3, waiting for transfers between devices: 29 us -> 17.8 us  [the longest x1 9.07 us: local(): lax.all_to_all(result.reshape(CHIPS, 2 * ROWS, SIDE), SEQ[:4], 0, 0, tile...]
    ppermute x1, waiting for transfers between devices: 7.71 us -> 0.01 us  [local(): filter_other = lax.ppermute(filter_part, 'dp', [(0, 1), (1, 0)])]
    all_to_all x2 -> x3, starting transfers between devices: 11 us -> 17.7 us  [the longest x1 7.19 us: local(): lax.all_to_all(result.reshape(CHIPS, 2 * ROWS, SIDE), SEQ[:4], 0, 0, tile...]
    ppermute x0 -> x3, starting transfers between devices: none -> 4.33 us  [the longest x2 2.77 us: pair_rows(): return lax.ppermute(a, ('x1', 'x0', 'c'), pairs)]
    ppermute x2 -> x4, waiting for transfers between devices: 3.42 us -> 1.71 us  [swap_cores(): return lax.ppermute(a, 'c', [(0, 1), (1, 0)])]
    pallas_call x2 -> x3, Pallas kernels: 10 us -> 8.78 us  [the longest x1 5.26 us: local(): kernel('project', project_kernel, [shape(2 * CHIPS * ROWS, SIDE), shape(5...]
  transfers between devices with their start and end apart: 5 -> 11, of which waited for: 5 -> 6; matrix products, arithmetic and copies ran while one was open for 1% -> 1% of each run, Pallas kernels for 5% -> 6%
where the time goes in v4:
time: 125 us; the launch traced here: 124 us
  waiting for transfers between devices  37.8 us (30%)
  blocking collectives  35 us (28%)
  starting transfers between devices  27.3 us (22%)
  Pallas kernels  19.5 us (16%)
  local copies, waits for them, and re-layouts  2.39 us (2%)
    all_to_all x1, blocking collectives, local(): lax.all_to_all(message.reshape(2 * CHIPS, ROWS, SIDE), SEQ, 0, 0, tiled=T...  35 us
    ppermute x1, waiting for transfers between devices, local(): next_in = lax.ppermute(flat_in, 'x0', [(0, 1), (1, 0)])  11.4 us
    all_to_all x1, waiting for transfers between devices, local(): lax.all_to_all(result.reshape(CHIPS, 2 * ROWS, SIDE), SEQ[:4], 0, 0, tile...  9.07 us
    all_to_all x1, waiting for transfers between devices, local(): parts = lax.all_to_all(partial, ('x1', 'y'), 0, 0, tiled=True)  8.44 us
    all_to_all x1, starting transfers between devices, local(): lax.all_to_all(result.reshape(CHIPS, 2 * ROWS, SIDE), SEQ[:4], 0, 0, tile...  7.19 us
    all_to_all x1, starting transfers between devices, local(): final = lax.all_to_all(sums, ('z', 'dp'), 0, 0, tiled=True)  6.91 us
    ppermute x2, waiting for transfers between devices, pair_rows(): return lax.ppermute(a, ('x1', 'x0', 'c'), pairs)  6.82 us
    pallas_call x1, Pallas kernels, local(): kernel('input_grad', inputs_kernel, [shape(SIDE, D)], [SMEM] + [VMEM] * 4...  5.73 us
  transfers between devices with their start and end apart: 11, of which 6 were waited for; matrix products, arithmetic and copies ran while one was open for 1% of the time, Pallas kernels for 6%

profile of v4, /device:TPU:32, one launch (start us, length us, event | category | flops | bytes accessed | tf_op | source)
XLA Modules:
  0.0 123.8 jit_solution(15512677748654321798)
XLA Ops:
  0.7 5.3 %project.1 = (bf16[3072,128]{1,0:T(8,128)(2,1)}, bf16[512,128]{1,0:T(8,128)(2,1)}, bf16[512,128]{1,0:T(8,128)(2,1)}) custom-call(s32[1]{0:T(128)} %bitcast.core, bf16[128,1024]{1,0:T(8,128)(2,1)} %bitcast.27, bf16[128,1024]{1,0:T(8,128)(2,1)} %bitcast.25, bf16[128,1024]{1,0:T(8,128)(2,1)} %taps.1, bf16[256,256]{1,0:T(8,128)(2,1)} %constant.30.clone.order, ...), custom_call_target="tpu_custom_call" | custom-call | flops 800000000 | bytes 8388608 | tf_op jit(solution)/shard_map/project/pallas_call | solution.py:262
  6.0 35.0 %all_to_all.24 = bf16[128,24,128]{2,1,0:T(8,128)(2,1)S(1)} all-to-all(bf16[128,24,128]{2,1,0:T(8,128)(2,1)} %bitcast.31), channel_id=1, replica_groups=mesh['x1'=2,'x0'=2,'y'=4,'z'=4,'c'=2,'dp'=2] {'x1','x0','y','z','c'}, dimensions={0} | all-to-all | bytes 1572864 | tf_op jit(solution)/shard_map/all_to_all | solution.py:273
  41.1 3.6 %convolve.1 = bf16[3072,128]{1,0:T(8,128)(2,1)} custom-call(s32[1]{0:T(128)} %bitcast.core, bf16[3072,128]{1,0:T(8,128)(2,1)S(1)} %bitcast.22, bf16[256,128]{1,0:T(8,128)(2,1)S(1)} %copy-done.6, bf16[2,128,256]{2,1,0:T(8,128)(2,1)S(1)} %copy-done.3, f32[128,128]{1,0:T(8,128)S(1)} %copy-done.7, f32[128,128]{1,0:T(8,128)S(1)} %copy-done.8, ...), custom_call_target="tpu_custom_call" | custom-call | flops 1200000000 | bytes 4194304 | tf_op jit(solution)/shard_map/convolve/pallas_call | solution.py:279
  44.7 7.2 %all-to-all-start.1 = ((bf16[64,48,128]{2,1,0:T(8,128)(2,1)}), bf16[64,48,128]{2,1,0:T(8,128)(2,1)S(1)}, u32[]{:S(2)}, u32[]{:S(2)}) async-start(bf16[64,48,128]{2,1,0:T(8,128)(2,1)} %bitcast.5), calls=%async_computation.1 | async-start | bytes 1572864 | tf_op jit(solution)/shard_map/all_to_all | solution.py:292
  52.0 1.6 %collective-permute-start.5 = (bf16[128,1024]{1,0:T(8,128)(2,1)S(1)}, bf16[128,1024]{1,0:T(8,128)(2,1)S(1)}, u32[]{:S(2)}, u32[]{:S(2)}) collective-permute-start(bf16[128,1024]{1,0:T(8,128)(2,1)S(1)} %bitcast.29), channel_id=1, source_target_pairs={{0,64},{64,0},{1,65},{65,1},{2,66},{66,2},{3,67},{67,3},{4,68},{68... | collective-permute-start | bytes 786440 | tf_op jit(solution)/shard_map/ppermute | solution.py:276
  53.5 0.5 collective-permute-start.4
  54.0 11.4 %collective-permute-done.5.next_in = bf16[128,1024]{1,0:T(8,128)(2,1)S(1)} collective-permute-done((bf16[128,1024]{1,0:T(8,128)(2,1)S(1)}, bf16[128,1024]{1,0:T(8,128)(2,1)S(1)}, u32[]{:S(2)}, u32[]{:S(2)}) %collective-permute-start.5) | collective-permute-done | bytes 262176 | tf_op jit(solution)/shard_map/ppermute | solution.py:276
  65.5 9.1 %all-to-all-done.1 = bf16[64,48,128]{2,1,0:T(8,128)(2,1)S(1)} async-done(((bf16[64,48,128]{2,1,0:T(8,128)(2,1)}), bf16[64,48,128]{2,1,0:T(8,128)(2,1)S(1)}, u32[]{:S(2)}, u32[]{:S(2)}) %all-to-all-start.1) | async-done | bytes 786464 | tf_op jit(solution)/shard_map/all_to_all | solution.py:292
  74.5 0.4 gate.1
  75.0 0.7 collective-permute-start.2
  75.7 2.1 %collective-permute-start.3 = (bf16[512,256]{1,0:T(8,128)(2,1)S(1)}, bf16[512,256]{1,0:T(8,128)(2,1)S(1)}, u32[]{:S(2)}, u32[]{:S(2)}) collective-permute-start(bf16[512,256]{1,0:T(8,128)(2,1)S(1)} %get-tuple-element.12), channel_id=1, source_target_pairs={{0,66},{2,64},{64,0},{66,2},{128,194},{130,192},{192,128},{194,130... | collective-permute-start | bytes 786440 | tf_op jit(solution)/shard_map/ppermute | solution.py:250
  77.8 6.8 %collective-permute-done.3.theirs = bf16[512,256]{1,0:T(8,128)(2,1)S(1)} collective-permute-done((bf16[512,256]{1,0:T(8,128)(2,1)S(1)}, bf16[512,256]{1,0:T(8,128)(2,1)S(1)}, u32[]{:S(2)}, u32[]{:S(2)}) %collective-permute-start.3) | collective-permute-done | bytes 262176 | tf_op jit(solution)/shard_map/ppermute | solution.py:250
  84.7 0.7 copy-done.15
  85.4 3.1 %weights.1 = bf16[512,1024]{1,0:T(8,128)(2,1)} custom-call(s32[1]{0:T(128)} %bitcast.9.odd, bf16[512,256]{1,0:T(8,128)(2,1)} %copy-done.14, bf16[512,256]{1,0:T(8,128)(2,1)} %copy-done.15, bf16[128,1024]{1,0:T(8,128)(2,1)} %bitcast.28, bf16[128,1024]{1,0:T(8,128)(2,1)} %copy-done.12, bf16[128,1024]{1,0:T(8,128)(2,1)} %copy-done.11, bf16[128,1024]{1,0:T(8,128)(2,1)} %copy-done.13), custom_call_target="tpu_custom_call" | custom-call | flops 600000000 | bytes 4194304 | tf_op jit(solution)/shard_map/weights/pallas_call | solution.py:299
  88.5 3.6 %all-to-all-start.2 = ((bf16[8,64,1024]{2,1,0:T(8,128)(2,1)}), bf16[8,64,1024]{2,1,0:T(8,128)(2,1)S(1)}, u32[]{:S(2)}, u32[]{:S(2)}) async-start(bf16[8,64,1024]{2,1,0:T(8,128)(2,1)} %bitcast.23), calls=%async_computation.2 | async-start | bytes 2097152 | tf_op jit(solution)/shard_map/all_to_all | solution.py:302
  92.0 0.8 fusion
  92.9 1.7 %collective-permute-done = bf16[64,24,128]{2,1,0:T(8,128)(2,1)S(1)} collective-permute-done((bf16[64,24,128]{2,1,0:T(8,128)(2,1)S(1)}, bf16[64,24,128]{2,1,0:T(8,128)(2,1)S(1)}, u32[]{:S(2)}, u32[]{:S(2)}) %collective-permute-start) | collective-permute-done | bytes 393248 | tf_op jit(solution)/shard_map/ppermute | solution.py:224
  94.6 4.8 %collective-permute-start.7 = (bf16[1024,128]{1,0:T(8,128)(2,1)S(1)}, bf16[1024,128]{1,0:T(8,128)(2,1)S(1)}, u32[]{:S(2)}, u32[]{:S(2)}) collective-permute-start(bf16[1024,128]{1,0:T(8,128)(2,1)S(1)} %bitcast.20), channel_id=1, source_target_pairs={{0,1},{1,0},{2,3},{3,2},{4,5},{5,4},{6,7},{7,6},{8,9},{9,8},{10,11... | collective-permute-start | bytes 786440 | tf_op jit(solution)/shard_map/ppermute | solution.py:307
  99.4 8.4 %all-to-all-done.2 = bf16[8,64,1024]{2,1,0:T(8,128)(2,1)S(1)} async-done(((bf16[8,64,1024]{2,1,0:T(8,128)(2,1)}), bf16[8,64,1024]{2,1,0:T(8,128)(2,1)S(1)}, u32[]{:S(2)}, u32[]{:S(2)}) %all-to-all-start.2) | async-done | bytes 1048608 | tf_op jit(solution)/shard_map/all_to_all | solution.py:302
  108.1 0.7 copy.16
  108.8 6.9 %all-to-all-start.3 = ((bf16[8,16,512]{2,1,0:T(8,128)(2,1)}), bf16[8,16,512]{2,1,0:T(8,128)(2,1)S(1)}, u32[]{:S(2)}, u32[]{:S(2)}) async-start(bf16[8,16,512]{2,1,0:T(8,128)(2,1)} %bitcast.13), calls=%async_computation.3 | async-start | bytes 262144 | tf_op jit(solution)/shard_map/all_to_all | solution.py:332
  115.7 5.7 %input_grad.1 = bf16[128,1024]{1,0:T(8,128)(2,1)} custom-call(s32[1]{0:T(128)} %bitcast.core, bf16[128,1024]{1,0:T(8,128)(2,1)} %bitcast.26, bf16[256,256]{1,0:T(8,128)(2,1)} %constant.30.clone.order, bf16[1536,128]{1,0:T(8,128)(2,1)} %bitcast.24, bf16[1536,128]{1,0:T(8,128)(2,1)} %bitcast.32, bf16[1024,1024]{1,0:T(8,128)(2,1)} %value_w.3, ...), custom_call_target="tpu_custom_call" | custom-call | flops 700000000 | bytes 8388608 | tf_op jit(solution)/shard_map/input_grad/pallas_call | solution.py:308
  121.4 1.4 %filter_grad.1 = f32[128,1024]{1,0:T(8,128)} custom-call(s32[1]{0:T(128)} %bitcast.core, bf16[256,256]{1,0:T(8,128)(2,1)S(1)} %copy-done, bf16[1024,128]{1,0:T(8,128)(2,1)S(1)} %bitcast.21, bf16[1024,128]{1,0:T(8,128)(2,1)S(1)} %collective-permute-done.7.theirs), custom_call_target="tpu_custom_call" | custom-call | flops 100000000 | bytes 2097152 | tf_op jit(solution)/shard_map/filter_grad/pallas_call | solution.py:319
  123.1 0.6 broadcast_multiply_fusion
  (48 shorter events, 0.7 us)
Async XLA Ops:
  0.6 40.4 %copy-start.3 = (bf16[2,128,256]{2,1,0:T(8,128)(2,1)S(1)}, bf16[2,128,256]{2,1,0:T(8,128)(2,1)}, u32[]{:S(2)}) copy-start(bf16[2,128,256]{2,1,0:T(8,128)(2,1)} %constant.32.clone.outer_t) | copy-start | bytes 393220
  0.6 40.4 %copy-start.4 = (bf16[256,256]{1,0:T(8,128)(2,1)S(1)}, bf16[256,256]{1,0:T(8,128)(2,1)}, u32[]{:S(2)}) copy-start(bf16[256,256]{1,0:T(8,128)(2,1)} %constant.35.clone.inner) | copy-start | bytes 393220
  0.7 40.4 %copy-start.5 = (bf16[256,256]{1,0:T(8,128)(2,1)S(1)}, bf16[256,256]{1,0:T(8,128)(2,1)}, u32[]{:S(2)}) copy-start(bf16[256,256]{1,0:T(8,128)(2,1)} %constant.36.clone.inner_t) | copy-start | bytes 393220
  0.7 40.4 %copy-start.6 = (bf16[256,128]{1,0:T(8,128)(2,1)S(1)}, bf16[256,128]{1,0:T(8,128)(2,1)}, u32[]{:S(2)}) copy-start(bf16[256,128]{1,0:T(8,128)(2,1)} %constant.31.clone.outer) | copy-start | bytes 196612
  0.7 40.4 %copy-start.7 = (f32[128,128]{1,0:T(8,128)S(1)}, f32[128,128]{1,0:T(8,128)}, u32[]{:S(2)}) copy-start(f32[128,128]{1,0:T(8,128)} %constant.33.clone.tw_re) | copy-start | bytes 196612
  0.7 40.4 %copy-start.8 = (f32[128,128]{1,0:T(8,128)S(1)}, f32[128,128]{1,0:T(8,128)}, u32[]{:S(2)}) copy-start(f32[128,128]{1,0:T(8,128)} %constant.34.clone.tw_im) | copy-start | bytes 196612
  41.1 10.9 %copy-start.9 = (bf16[1,128,1024]{2,1,0:T(8,128)(2,1)S(1)}, bf16[1,128,1024]{2,1,0:T(8,128)(2,1)}, u32[]{:S(2)}) copy-start(bf16[1,128,1024]{2,1,0:T(8,128)(2,1)} %param.13) | copy-start | bytes 786436
  41.1 12.4 %copy-start.16 = (bf16[512,128]{1,0:T(8,128)(2,1)S(1)}, bf16[512,128]{1,0:T(8,128)(2,1)}, u32[]{:S(2)}) copy-start(bf16[512,128]{1,0:T(8,128)(2,1)} %get-tuple-element.10) | copy-start | bytes 393220
  41.1 33.5 %copy-start.1 = (bf16[512,512]{1,0:T(8,128)(2,1)S(1)}, bf16[512,512]{1,0:T(8,128)(2,1)}, u32[]{:S(2)}) copy-start(bf16[512,512]{1,0:T(8,128)(2,1)} %constant.37.clone.blocks) | copy-start | bytes 1572868
  41.1 33.4 %copy-start.2 = (bf16[512,128]{1,0:T(8,128)(2,1)S(1)}, bf16[512,128]{1,0:T(8,128)(2,1)}, u32[]{:S(2)}) copy-start(bf16[512,128]{1,0:T(8,128)(2,1)} %get-tuple-element.9.cot_own) | copy-start | bytes 393220
  44.7 29.8 %all-to-all-start.1 = ((bf16[64,48,128]{2,1,0:T(8,128)(2,1)}), bf16[64,48,128]{2,1,0:T(8,128)(2,1)S(1)}, u32[]{:S(2)}, u32[]{:S(2)}) async-start(bf16[64,48,128]{2,1,0:T(8,128)(2,1)} %bitcast.5), calls=%async_computation.1 | async-start | bytes 1572864 | tf_op jit(solution)/shard_map/all_to_all | solution.py:292
  52.0 13.5 %collective-permute-start.5 = (bf16[128,1024]{1,0:T(8,128)(2,1)S(1)}, bf16[128,1024]{1,0:T(8,128)(2,1)S(1)}, u32[]{:S(2)}, u32[]{:S(2)}) collective-permute-start(bf16[128,1024]{1,0:T(8,128)(2,1)S(1)} %bitcast.29), channel_id=1, source_target_pairs={{0,64},{64,0},{1,65},{65,1},{2,66},{66,2},{3,67},{67,3},{4,68},{68... | collective-permute-start | bytes 786440 | tf_op jit(solution)/shard_map/ppermute | solution.py:276
  53.5 12.0 %collective-permute-start.1 = (bf16[512,128]{1,0:T(8,128)(2,1)S(1)}, bf16[512,128]{1,0:T(8,128)(2,1)S(1)}, u32[]{:S(2)}, u32[]{:S(2)}) collective-permute-start(bf16[512,128]{1,0:T(8,128)(2,1)S(1)} %copy-done.16), channel_id=1, source_target_pairs={{0,2},{2,0},{1,3},{3,1},{4,6},{6,4},{5,7},{7,5},{8,10},{10,8},{9,1... | collective-permute-start | bytes 393224 | tf_op jit(solution)/shard_map/ppermute | solution.py:224
  53.5 24.3 %collective-permute-start.4 = (bf16[128,1024]{1,0:T(8,128)(2,1)S(1)}, bf16[128,1024]{1,0:T(8,128)(2,1)S(1)}, u32[]{:S(2)}, u32[]{:S(2)}) collective-permute-start(bf16[128,1024]{1,0:T(8,128)(2,1)S(1)} %bitcast.30), channel_id=1, source_target_pairs={{0,2},{2,0},{1,3},{3,1},{4,6},{6,4},{5,7},{7,5},{8,10},{10,8},{9,1... | collective-permute-start | bytes 786440 | tf_op jit(solution)/shard_map/ppermute | solution.py:224
  65.5 19.2 %copy-start.11 = (bf16[128,1024]{1,0:T(8,128)(2,1)}, bf16[128,1024]{1,0:T(8,128)(2,1)S(1)}, u32[]{:S(2)}) copy-start(bf16[128,1024]{1,0:T(8,128)(2,1)S(1)} %collective-permute-done.5.next_in) | copy-start | bytes 786436
  65.5 12.3 %collective-permute-start.6 = (bf16[128,1024]{1,0:T(8,128)(2,1)S(1)}, bf16[128,1024]{1,0:T(8,128)(2,1)S(1)}, u32[]{:S(2)}, u32[]{:S(2)}) collective-permute-start(bf16[128,1024]{1,0:T(8,128)(2,1)S(1)} %collective-permute-done.5.next_in), channel_id=1, source_target_pairs={{0,2},{2,0},{1,3},{3,1},{4,6},{6,4},{5,7},{7,5},{8,10},{10,8},{9,1... | collective-permute-start | bytes 786440 | tf_op jit(solution)/shard_map/ppermute | solution.py:224
  75.0 2.8 %collective-permute-start.2 = (bf16[512,256]{1,0:T(8,128)(2,1)S(1)}, bf16[512,256]{1,0:T(8,128)(2,1)S(1)}, u32[]{:S(2)}, u32[]{:S(2)}) collective-permute-start(bf16[512,256]{1,0:T(8,128)(2,1)S(1)} %get-tuple-element.11), channel_id=1, source_target_pairs={{0,0},{2,2},{64,66},{66,64},{128,128},{130,130},{192,194},{194,192... | collective-permute-start | bytes 786440 | tf_op jit(solution)/shard_map/ppermute | solution.py:250
  75.7 9.0 %collective-permute-start.3 = (bf16[512,256]{1,0:T(8,128)(2,1)S(1)}, bf16[512,256]{1,0:T(8,128)(2,1)S(1)}, u32[]{:S(2)}, u32[]{:S(2)}) collective-permute-start(bf16[512,256]{1,0:T(8,128)(2,1)S(1)} %get-tuple-element.12), channel_id=1, source_target_pairs={{0,66},{2,64},{64,0},{66,2},{128,194},{130,192},{192,128},{194,130... | collective-permute-start | bytes 786440 | tf_op jit(solution)/shard_map/ppermute | solution.py:250
  77.8 6.9 %copy-start.12 = (bf16[128,1024]{1,0:T(8,128)(2,1)}, bf16[128,1024]{1,0:T(8,128)(2,1)S(1)}, u32[]{:S(2)}) copy-start(bf16[128,1024]{1,0:T(8,128)(2,1)S(1)} %collective-permute-done.4.in_other) | copy-start | bytes 786436
  88.5 19.4 %all-to-all-start.2 = ((bf16[8,64,1024]{2,1,0:T(8,128)(2,1)}), bf16[8,64,1024]{2,1,0:T(8,128)(2,1)S(1)}, u32[]{:S(2)}, u32[]{:S(2)}) async-start(bf16[8,64,1024]{2,1,0:T(8,128)(2,1)} %bitcast.23), calls=%async_computation.2 | async-start | bytes 2097152 | tf_op jit(solution)/shard_map/all_to_all | solution.py:302
  92.8 1.7 %collective-permute-start = (bf16[64,24,128]{2,1,0:T(8,128)(2,1)S(1)}, bf16[64,24,128]{2,1,0:T(8,128)(2,1)S(1)}, u32[]{:S(2)}, u32[]{:S(2)}) collective-permute-start(bf16[64,24,128]{2,1,0:T(8,128)(2,1)S(1)} %get-tuple-element.13), channel_id=1, source_target_pairs={{0,2},{2,0},{1,3},{3,1},{4,6},{6,4},{5,7},{7,5},{8,10},{10,8},{9,1... | collective-permute-start | bytes 1179656 | tf_op jit(solution)/shard_map/ppermute | solution.py:224
  94.6 21.1 %copy-start.10 = (bf16[64,24,128]{2,1,0:T(8,128)(2,1)}, bf16[64,24,128]{2,1,0:T(8,128)(2,1)S(1)}, u32[]{:S(2)}) copy-start(bf16[64,24,128]{2,1,0:T(8,128)(2,1)S(1)} %collective-permute-done) | copy-start | bytes 1179652
  94.6 26.8 %collective-permute-start.7 = (bf16[1024,128]{1,0:T(8,128)(2,1)S(1)}, bf16[1024,128]{1,0:T(8,128)(2,1)S(1)}, u32[]{:S(2)}, u32[]{:S(2)}) collective-permute-start(bf16[1024,128]{1,0:T(8,128)(2,1)S(1)} %bitcast.20), channel_id=1, source_target_pairs={{0,1},{1,0},{2,3},{3,2},{4,5},{5,4},{6,7},{7,6},{8,9},{9,8},{10,11... | collective-permute-start | bytes 786440 | tf_op jit(solution)/shard_map/ppermute | solution.py:307
  108.8 14.4 %all-to-all-start.3 = ((bf16[8,16,512]{2,1,0:T(8,128)(2,1)}), bf16[8,16,512]{2,1,0:T(8,128)(2,1)S(1)}, u32[]{:S(2)}, u32[]{:S(2)}) async-start(bf16[8,16,512]{2,1,0:T(8,128)(2,1)} %bitcast.13), calls=%async_computation.3 | async-start | bytes 262144 | tf_op jit(solution)/shard_map/all_to_all | solution.py:332
  (4 other events, 20.2 us)

commit v5 on v4

--- a/solution.py
+++ b/solution.py
@@ -17,7 +17,7 @@
 CHIPS = 64
 ARRS = 3
 ROWS = ARRS * 8
-SEQ = ("x1", "x0", "y", "z", "c")
+SEQ = ("x1", "x0", "y1", "y0", "z", "c")
 VMEM = pl.BlockSpec(memory_space=pltpu.VMEM)
 SMEM = pl.BlockSpec(memory_space=pltpu.SMEM)
 
@@ -39,11 +39,13 @@
 def block_order():
     index = []
     for half in range(2):
-        for y in range(4):
-            for zz in range(4):
-                for i in range(16):
-                    x, z, q = (y, zz, i) if half == 0 else (3 - y, 3 - zz, 15 - i)
-                    index.append((16 * x + 4 * (q // 4) + z) * 8 + 4 * half + q % 4)
+        for y0 in range(2):
+            for y1 in range(2):
+                for zz in range(4):
+                    for i in range(16):
+                        y = 2 * y1 + y0
+                        x, z, q = (y, zz, i) if half == 0 else (3 - y, 3 - zz, 15 - i)
+                        index.append((16 * x + 4 * (q // 4) + z) * 8 + 4 * half + q % 4)
     return one_hot_rows(np.array(index), 512)
 
 
@@ -74,29 +76,34 @@
     return lax.dot_general(a, b, (((ca,), (cb,)), ((), ())), preferred_element_type=F32)
 
 
-def project_kernel(core, inputs, cot, taps, order, value_w, gate_w, message, cot_own, cot_give, w_buf, cot_buf, sems):
+def project_kernel(core, inputs, cot, taps, order, value_w, gate_w, message, cot_own, cot_give, w_buf, cot_buf, taps_buf, sems):
     fetch = [
         pltpu.make_async_copy(w, w_buf.at[i], sems.at[i]) for i, w in enumerate((value_w, gate_w))
     ]
     for copy in fetch:
         copy.start()
+    def blocks_of(arrays):
+        stacked = jnp.concatenate(arrays, axis=0)
+        for b in range(4):
+            low = stacked[:, b * SIDE:(b + 1) * SIDE]
+            high = stacked[:, (7 - b) * SIDE:(8 - b) * SIDE]
+            moved = dot(order[...], jnp.concatenate([low, high], axis=1), 1, 1)
+            yield b, [moved[:, a * SIDE:(a + 1) * SIDE].reshape(32, 8, SIDE) for a in range(2)]
+
+    for b, (tap, line) in blocks_of([taps[...], cot[...]]):
+        taps_buf[b] = tap
+        line = line.reshape(16, 2, 8, SIDE)
+        for c in range(2):
+            rows = line[:, c].reshape(SIDE, SIDE).astype(BF16)
+            cot_buf[c ^ core[0], b * SIDE:(b + 1) * SIDE, :] = rows
     fetch[0].wait()
     value = dot(inputs[...], w_buf[0]).astype(BF16)
     fetch[1].wait()
     gate = dot(inputs[...], w_buf[1])
     mix = (cot[...].astype(F32) * gate).astype(BF16)
-    stacked = jnp.concatenate([value, mix, taps[...], cot[...]], axis=0)
-    for b in range(4):
-        low = stacked[:, b * SIDE:(b + 1) * SIDE]
-        high = stacked[:, (7 - b) * SIDE:(8 - b) * SIDE]
-        moved = dot(order[...], jnp.concatenate([low, high], axis=1), 1, 1)
-        parts = [moved[:, a * SIDE:(a + 1) * SIDE].reshape(32, 8, SIDE) for a in range(4)]
-        block = jnp.concatenate(parts[:3], axis=1).reshape(32 * ROWS, SIDE).astype(BF16)
+    for b, parts in blocks_of([value, mix]):
+        block = jnp.concatenate(parts + [taps_buf[b]], axis=1).reshape(32 * ROWS, SIDE).astype(BF16)
         message[b * 32 * ROWS:(b + 1) * 32 * ROWS, :] = block
-        line = parts[3].reshape(16, 2, 8, SIDE)
-        for c in range(2):
-            rows = line[:, c].reshape(SIDE, SIDE).astype(BF16)
-            cot_buf[c ^ core[0], b * SIDE:(b + 1) * SIDE, :] = rows
     cot_own[...] = cot_buf[0]
     cot_give[...] = cot_buf[1]
 
@@ -154,7 +161,7 @@
     result[...] = flat[...].astype(BF16)
 
 
-def gate_kernel(odd, home, blocks, cot_own, cot_other, keep, send):
+def gate_kernel(odd, home, blocks, cot_own, cot_other, *outs):
     full = home[...].astype(F32).reshape(CHIPS, 2 * ROWS, SIDE)
     grads, gates = [], []
     for slot, cot in enumerate((cot_own, cot_other)):
@@ -164,18 +171,25 @@
         gates.append((mixed * cot[...].astype(F32)).astype(BF16))
     for a, group in enumerate((grads, gates)):
         rows = dot(blocks[...], jnp.concatenate(group, axis=1))
-        low, high = rows[:256], rows[256:]
-        keep[a * 256:(a + 1) * 256, :] = jnp.where(odd[0] == 1, high, low).astype(BF16)
-        send[a * 256:(a + 1) * 256, :] = jnp.where(odd[0] == 1, low, high).astype(BF16)
-
-
-def weights_kernel(odd, mine, theirs, inputs, in_other, next_in, next_other, partial):
+        parts = [[rows[(2 * h + q) * SIDE:(2 * h + q + 1) * SIDE] for q in range(2)] for h in range(2)]
+        for dx in range(2):
+            line = [jnp.where(odd[0] == 1, parts[1 - dx][q], parts[dx][q]) for q in range(2)]
+            for dy in range(2):
+                part = jnp.where(odd[1] == 1, line[1 - dy], line[dy])
+                outs[2 * dx + dy][a * SIDE:(a + 1) * SIDE, :] = part.astype(BF16)
+
+
+def weights_kernel(odd, *refs):
+    rows, ins, partial = refs[:4], refs[4:12], refs[12]
     total = 0.0
-    for rows, one, two in ((mine, inputs, in_other), (theirs, next_in, next_other)):
-        first = jnp.where(odd[0] == 1, two[...], one[...])
-        second = jnp.where(odd[0] == 1, one[...], two[...])
-        total = total + dot(rows[...], jnp.concatenate([first, second], axis=0))
-    partial[...] = total.astype(BF16)
+    for k in range(4):
+        one, two = ins[2 * k][...], ins[2 * k + 1][...]
+        first = jnp.where(odd[0] == 1, two, one)
+        second = jnp.where(odd[0] == 1, one, two)
+        total = total + dot(rows[k][...], jnp.concatenate([first, second], axis=0))
+    for half in range(2):
+        cols = total[:, half * 512:(half + 1) * 512].astype(BF16)
+        partial[:, half] = cols.reshape(16, 16, 512)
 
 
 def natural_order(stack, order):
@@ -189,14 +203,15 @@
     return jnp.concatenate(low + high, axis=1)
 
 
-def inputs_kernel(core, cot, order, own, far, value_w, gate_w, input_grad, w_buf, stack, sems):
+def inputs_kernel(core, cot, order, home, far, value_w, gate_w, input_grad, w_buf, stack, sems):
     fetch = [
         pltpu.make_async_copy(w, w_buf.at[i], sems.at[i]) for i, w in enumerate((value_w, gate_w))
     ]
     for copy in fetch:
         copy.start()
-    for side, ref in ((0, own), (1, far)):
-        full = ref[...].astype(F32).reshape(CHIPS, ROWS, SIDE)
+    near = home[...].astype(F32).reshape(CHIPS, 2 * ROWS, SIDE)
+    other = far[...].astype(F32).reshape(CHIPS, 16, SIDE)
+    for side, full in ((0, near), (1, other)):
         stack[:, core[0] ^ side] = jnp.concatenate([full[:, :8], full[:, 8:16]], axis=2)
     natural = natural_order(stack, order)
     gated = (natural[:SIDE] * cot[...].astype(F32)).astype(BF16)
@@ -207,13 +222,10 @@
     input_grad[...] = (total + dot(gated, w_buf[1], 1, 1)).astype(BF16)
 
 
-def filter_kernel(core, order, mine, theirs, filter_grad, stack):
-    total = (mine[...].astype(F32) + theirs[...].astype(F32)).reshape(2, CHIPS, 8, SIDE)
-    for side in range(2):
-        rounded = total[side].astype(BF16).astype(F32)
-        stack[:, core[0] ^ side] = jnp.concatenate([rounded, total[side] - rounded], axis=2)
-    both = natural_order(stack, order)
-    filter_grad[...] = (both[:SIDE] + both[SIDE:]) * SCALE
+def filter_kernel(core, order, own, far, filter_grad, stack):
+    for side, ref in ((0, own), (1, far)):
+        stack[:, core[0] ^ side] = ref[...].astype(F32).reshape(CHIPS, 8, SIDE)
+    filter_grad[...] = natural_order(stack, order) * SCALE
 
 
 def shape(*dims, kind=BF16):
@@ -239,20 +251,23 @@
     )
 
 
-def pair_rows(a, cross):
+def near(a, dx, dy, cross=False):
     pairs = []
-    for x1 in range(2):
-        for x0 in range(2):
-            for c in range(2):
-                x_to = x0 ^ 1 if cross else x0
-                c_to = c ^ x_to
-                pairs.append(((2 * x1 + x0) * 2 + c, (2 * x1 + x_to) * 2 + c_to))
-    return lax.ppermute(a, ("x1", "x0", "c"), pairs)
+    for x0 in range(2):
+        for y1 in range(2):
+            for y0 in range(2):
+                for z in range(4):
+                    for c in range(2):
+                        x_to = x0 ^ dx
+                        c_to = c ^ x_to if cross else c
+                        start = (((2 * x0 + y1) * 2 + y0) * 4 + z) * 2 + c
+                        pairs.append((start, (((2 * x_to + y1) * 2 + (y0 ^ dy)) * 4 + z) * 2 + c_to))
+    return lax.ppermute(a, ("x0", "y1", "y0", "z", "c"), pairs)
 
 
 def local(inputs, cotangent, value_weight, gate_weight, filter_taps):
     core = lax.axis_index("c").astype(jnp.int32).reshape(1)
-    odd = lax.axis_index("x0").astype(jnp.int32).reshape(1)
+    odd = jnp.stack([lax.axis_index(name).astype(jnp.int32) for name in ("x0", "y0")])
     order = jnp.asarray(spread_order())
     flat_in = inputs.reshape(SIDE, D)
     cot = cotangent.reshape(SIDE, D)
@@ -265,16 +280,18 @@
         [shape(2 * CHIPS * ROWS, SIDE), shape(512, SIDE), shape(512, SIDE)],
         [SMEM] + [VMEM] * 4,
         2,
-        [w_scratch, pltpu.VMEM((2, 512, SIDE), BF16), sems],
+        [w_scratch, pltpu.VMEM((2, 512, SIDE), BF16), pltpu.VMEM((4, 32, 8, SIDE), F32), sems],
         0.8,
         8.0,
         56,
     )(core, flat_in, cot, filter_taps, order, value_weight, gate_weight)
     spread = lax.all_to_all(message.reshape(2 * CHIPS, ROWS, SIDE), SEQ, 0, 0, tiled=True)
     cot_other = swap_cores(cot_give)
-    in_other = swap_cores(flat_in)
-    next_in = lax.ppermute(flat_in, "x0", [(0, 1), (1, 0)])
-    next_other = swap_cores(next_in)
+    ins = []
+    for dx in range(2):
+        for dy in range(2):
+            block = near(flat_in, dx, dy) if dx + dy else flat_in
+            ins += [block, swap_cores(block)]
 
     (result,) = kernel(
         "convolve",
@@ -289,22 +306,27 @@
         1.2,
         4.0,
     )(core, spread.reshape(2 * CHIPS * ROWS, SIDE), *[jnp.asarray(t) for t in tables()])
-    home = lax.all_to_all(result.reshape(CHIPS, 2 * ROWS, SIDE), SEQ[:4], 0, 0, tiled=True)
-
-    keep, send = kernel("gate", gate_kernel, [shape(512, 256)] * 2, [SMEM] + [VMEM] * 4, gflop=0.3, mbyte=2.0)(
+    home = lax.all_to_all(result.reshape(CHIPS, 2 * ROWS, SIDE), SEQ[:5], 0, 0, tiled=True)
+
+    rows = kernel("gate", gate_kernel, [shape(256, 256)] * 4, [SMEM] + [VMEM] * 4, gflop=0.3, mbyte=2.0)(
         odd, home.reshape(2 * CHIPS * ROWS, SIDE), jnp.asarray(block_order()), cot_own, cot_other
     )
-    mine = pair_rows(keep, False)
-    theirs = pair_rows(send, True)
+    shaped = home.reshape(CHIPS, 2, ROWS, SIDE)
+    filter_part = jnp.stack([shaped[:, slot, 16:] for slot in range(2)])
+    cuts = filter_part.reshape(2, 64, 8, SIDE)
+    cuts = [cuts[i] for i in range(2)]
+    cuts, rows = lax.optimization_barrier((cuts, rows))
+    others = [lax.ppermute(cut, "dp", [(0, 1), (1, 0)]) for cut in cuts]
+    sums = [(cut.astype(F32) + other.astype(F32)).astype(BF16) for cut, other in zip(cuts, others)]
+    filter_sum = jnp.concatenate(sums, axis=0).reshape(2, CHIPS, 8, SIDE)
+    rows = [near(rows[2 * dx + dy], dx, dy, True) for dx in range(2) for dy in range(2)]
     (partial,) = kernel(
-        "weights", weights_kernel, [shape(512, D)], [SMEM] + [VMEM] * 6, gflop=0.6, mbyte=4.0, limit=56
-    )(odd, mine, theirs, flat_in, in_other, next_in, next_other)
-    parts = lax.all_to_all(partial, ("x1", "y"), 0, 0, tiled=True)
-
-    own = home[:, :ROWS]
-    far = swap_cores(home[:, ROWS:])
-    filter_part = jnp.stack([own[:, 16:], far[:, 16:]]).reshape(1024, SIDE)
-    filter_other = lax.ppermute(filter_part, "dp", [(0, 1), (1, 0)])
+        "weights", weights_kernel, [shape(16, 2, 16, 512)], [SMEM] + [VMEM] * 12, gflop=0.6, mbyte=4.0, limit=56
+    )(odd, *rows, *ins)
+    parts = lax.all_to_all(partial.reshape(4, SIDE, 512), ("x1", "y1"), 0, 0, tiled=True)
+
+    far = swap_cores(shaped[:, 1, :16])
+    filter_far = swap_cores(filter_sum[1])
     (input_grad,) = kernel(
         "input_grad",
         inputs_kernel,
@@ -315,27 +337,26 @@
         0.7,
         8.0,
         56,
-    )(core, cot, order, own.reshape(1536, SIDE), far.reshape(1536, SIDE), value_weight, gate_weight)
+    )(core, cot, order, home.reshape(3072, SIDE), far.reshape(1024, SIDE), value_weight, gate_weight)
     (filter_grad,) = kernel(
         "filter_grad",
         filter_kernel,
         [shape(SIDE, D, kind=F32)],
         [SMEM] + [VMEM] * 3,
         0,
-        [pltpu.VMEM((CHIPS, 2, 8, 2 * SIDE), F32)],
+        [pltpu.VMEM((CHIPS, 2, 8, SIDE), F32)],
         0.1,
         2.0,
-    )(core, order, filter_part, filter_other)
-
-    sums = jnp.sum(parts.reshape(8, 64, D).astype(F32), axis=0).astype(BF16)
-    sums = sums.reshape(4, 16, 2, 512).transpose(0, 2, 1, 3).reshape(8, 16, 512)
-    final = lax.all_to_all(sums, ("z", "dp"), 0, 0, tiled=True)
+    )(core, order, filter_sum[0].reshape(512, SIDE), filter_far.reshape(512, SIDE))
+
+    rows = jnp.sum(parts.astype(F32), axis=0).astype(BF16).reshape(8, 16, 512)
+    final = lax.all_to_all(rows, ("z", "dp"), 0, 0, tiled=True)
     projection_grads = jnp.sum(final.astype(F32), axis=0) * SCALE
     return (input_grad.reshape(1, SIDE, D), projection_grads, filter_grad)
 
 
 def solution(mesh):
-    fine = Mesh(mesh.devices.reshape(2, 2, 4, 4, 2, 2), SEQ + ("dp",))
+    fine = Mesh(mesh.devices.reshape(2, 2, 2, 2, 4, 2, 2), SEQ + ("dp",))
     in_specs = (P("dp", SEQ, None), P("dp", SEQ, None), P(), P(), P(SEQ, None))
     out_specs = (P("dp", SEQ, None), P(SEQ, "dp"), P(SEQ, None))
     return jax.shard_map(local, mesh=fine, in_specs=in_specs, out_specs=out_specs, check_vma=False)

time: 125 us -> 123 us (0.984)
  waiting for transfers between devices: 37.8 us -> 26.2 us
  starting transfers between devices: 27.3 us -> 37.7 us
    all_to_all x3, waiting for transfers between devices: 17.8 us -> 6.38 us  [the longest x1 5.54 us: local(): lax.all_to_all(partial.reshape(4, SIDE, 512), ('x1', 'y1'), 0, 0, tiled=T...]
    ppermute x4 -> x9, starting transfers between devices: 9.09 us -> 16.8 us  [the longest x2 9.07 us: local(): others = [lax.ppermute(cut, 'dp', [(0, 1), (1, 0)]) for cut in cuts]]
    all_to_all x3, starting transfers between devices: 17.7 us -> 20 us  [the longest x1 7.32 us: local(): lax.all_to_all(result.reshape(CHIPS, 2 * ROWS, SIDE), SEQ[:5], 0, 0, tile...]
    ppermute x4 -> x7, waiting for transfers between devices: 1.71 us -> 0.02 us  [swap_cores(): return lax.ppermute(a, 'c', [(0, 1), (1, 0)])]
    ppermute x4 -> x9, waiting for transfers between devices: 18.3 us -> 19.8 us  [the longest x7 19.8 us: near(): return lax.ppermute(a, ('x0', 'y1', 'y0', 'z', 'c'), pairs)]
  transfers between devices with their start and end apart: 11 -> 19, of which waited for: 6 -> 6; matrix products, arithmetic and copies ran while one was open for 1% -> 1% of each run, Pallas kernels for 6% -> 9%
where the time goes in v5:
time: 123 us
  starting transfers between devices  37.7 us (31%)
  blocking collectives  35 us (28%)
  waiting for transfers between devices  26.2 us (21%)
  Pallas kernels  19.9 us (16%)
  other arithmetic  1.54 us (1%)
  local copies, waits for them, and re-layouts  1.51 us (1%)
    all_to_all x1, blocking collectives, local(): lax.all_to_all(message.reshape(2 * CHIPS, ROWS, SIDE), SEQ, 0, 0, tiled=T...  35 us
    ppermute x7, waiting for transfers between devices, near(): return lax.ppermute(a, ('x0', 'y1', 'y0', 'z', 'c'), pairs)  19.8 us
    ppermute x2, starting transfers between devices, local(): others = [lax.ppermute(cut, 'dp', [(0, 1), (1, 0)]) for cut in cuts]  9.07 us
    ppermute x7, starting transfers between devices, near(): return lax.ppermute(a, ('x0', 'y1', 'y0', 'z', 'c'), pairs)  7.75 us
    all_to_all x1, starting transfers between devices, local(): lax.all_to_all(result.reshape(CHIPS, 2 * ROWS, SIDE), SEQ[:5], 0, 0, tile...  7.32 us
    all_to_all x1, starting transfers between devices, local(): final = lax.all_to_all(rows, ('z', 'dp'), 0, 0, tiled=True)  6.49 us
    all_to_all x1, starting transfers between devices, local(): lax.all_to_all(partial.reshape(4, SIDE, 512), ('x1', 'y1'), 0, 0, tiled=T...  6.22 us
    pallas_call x1, Pallas kernels, local(): kernel('input_grad', inputs_kernel, [shape(SIDE, D)], [SMEM] + [VMEM] * 4...  5.78 us
  transfers between devices with their start and end apart: 19, of which 6 were waited for; matrix products, arithmetic and copies ran while one was open for 1% of the time, Pallas kernels for 9%

profile of v5, /device:TPU:32, one launch (start us, length us, event | category | flops | bytes accessed | tf_op | source)
XLA Modules:
  0.0 122.9 jit_solution(4503140508941823964)
XLA Ops:
  0.7 5.1 %project.1 = (bf16[3072,128]{1,0:T(8,128)(2,1)}, bf16[512,128]{1,0:T(8,128)(2,1)}, bf16[512,128]{1,0:T(8,128)(2,1)}) custom-call(s32[1]{0:T(128)} %bitcast.core, bf16[128,1024]{1,0:T(8,128)(2,1)} %bitcast.32, bf16[128,1024]{1,0:T(8,128)(2,1)} %bitcast.30, bf16[128,1024]{1,0:T(8,128)(2,1)} %taps.1, bf16[256,256]{1,0:T(8,128)(2,1)} %constant.34.clone.order, ...), custom_call_target="tpu_custom_call" | custom-call | flops 800000000 | bytes 8388608 | tf_op jit(solution)/shard_map/project/pallas_call | solution.py:277
  5.9 35.0 %all_to_all.20 = bf16[128,24,128]{2,1,0:T(8,128)(2,1)S(1)} all-to-all(bf16[128,24,128]{2,1,0:T(8,128)(2,1)} %bitcast.38), channel_id=1, replica_groups=mesh['x1'=2,'x0'=2,'y1'=2,'y0'=2,'z'=4,'c'=2,'dp'=2] {'x1','x0','y1','y0..., dimensions={0} | all-to-all | bytes 1572864 | tf_op jit(solution)/shard_map/all_to_all | solution.py:288
  41.0 3.6 %convolve.1 = bf16[3072,128]{1,0:T(8,128)(2,1)} custom-call(s32[1]{0:T(128)} %bitcast.core, bf16[3072,128]{1,0:T(8,128)(2,1)S(1)} %bitcast.27, bf16[256,128]{1,0:T(8,128)(2,1)S(1)} %copy-done.8, bf16[2,128,256]{2,1,0:T(8,128)(2,1)S(1)} %copy-done.5, f32[128,128]{1,0:T(8,128)S(1)} %copy-done.9, f32[128,128]{1,0:T(8,128)S(1)} %copy-done.10, ...), custom_call_target="tpu_custom_call" | custom-call | flops 1200000000 | bytes 4194304 | tf_op jit(solution)/shard_map/convolve/pallas_call | solution.py:296
  44.6 7.3 %all-to-all-start.1 = ((bf16[64,48,128]{2,1,0:T(8,128)(2,1)}), bf16[64,48,128]{2,1,0:T(8,128)(2,1)S(1)}, u32[]{:S(2)}, u32[]{:S(2)}) async-start(bf16[64,48,128]{2,1,0:T(8,128)(2,1)} %bitcast.5), calls=%async_computation.1 | async-start | bytes 1572864 | tf_op jit(solution)/shard_map/all_to_all | solution.py:309
  52.0 1.6 %collective-permute-start.7 = (bf16[128,1024]{1,0:T(8,128)(2,1)S(1)}, bf16[128,1024]{1,0:T(8,128)(2,1)S(1)}, u32[]{:S(2)}, u32[]{:S(2)}) collective-permute-start(bf16[128,1024]{1,0:T(8,128)(2,1)S(1)} %bitcast.34), channel_id=1, source_target_pairs={{0,16},{2,18},{4,20},{6,22},{8,24},{10,26},{12,28},{14,30},{16,0},... | collective-permute-start | bytes 786440 | tf_op jit(solution)/shard_map/ppermute | solution.py:265
  53.5 1.5 %collective-permute-start.9 = (bf16[128,1024]{1,0:T(8,128)(2,1)S(1)}, bf16[128,1024]{1,0:T(8,128)(2,1)S(1)}, u32[]{:S(2)}, u32[]{:S(2)}) collective-permute-start(bf16[128,1024]{1,0:T(8,128)(2,1)S(1)} %bitcast.35), channel_id=1, source_target_pairs={{0,64},{2,66},{4,68},{6,70},{8,72},{10,74},{12,76},{14,78},{16,80}... | collective-permute-start | bytes 786440 | tf_op jit(solution)/shard_map/ppermute | solution.py:265
  56.1 9.7 %collective-permute-done.7.refs_6_ = bf16[128,1024]{1,0:T(8,128)(2,1)S(1)} collective-permute-done((bf16[128,1024]{1,0:T(8,128)(2,1)S(1)}, bf16[128,1024]{1,0:T(8,128)(2,1)S(1)}, u32[]{:S(2)}, u32[]{:S(2)}) %collective-permute-start.7) | collective-permute-done | bytes 262176 | tf_op jit(solution)/shard_map/ppermute | solution.py:265
  65.8 1.4 %collective-permute-done.9.refs_8_ = bf16[128,1024]{1,0:T(8,128)(2,1)S(1)} collective-permute-done((bf16[128,1024]{1,0:T(8,128)(2,1)S(1)}, bf16[128,1024]{1,0:T(8,128)(2,1)S(1)}, u32[]{:S(2)}, u32[]{:S(2)}) %collective-permute-start.9) | collective-permute-done | bytes 262176 | tf_op jit(solution)/shard_map/ppermute | solution.py:265
  67.3 6.4 %collective-permute-done.11.refs_10_ = bf16[128,1024]{1,0:T(8,128)(2,1)S(1)} collective-permute-done((bf16[128,1024]{1,0:T(8,128)(2,1)S(1)}, bf16[128,1024]{1,0:T(8,128)(2,1)S(1)}, u32[]{:S(2)}, u32[]{:S(2)}) %collective-permute-start.11) | collective-permute-done | bytes 262176 | tf_op jit(solution)/shard_map/ppermute | solution.py:265
  73.7 0.8 all-to-all-done.1
  74.6 1.0 gate.1
  76.7 2.1 %collective-permute-start.4 = (bf16[256,256]{1,0:T(8,128)(2,1)S(1)}, bf16[256,256]{1,0:T(8,128)(2,1)S(1)}, u32[]{:S(2)}, u32[]{:S(2)}) collective-permute-start(bf16[256,256]{1,0:T(8,128)(2,1)S(1)} %get-tuple-element.25), channel_id=1, source_target_pairs={{0,66},{2,64},{4,70},{6,68},{8,74},{10,72},{12,78},{14,76},{16,82}... | collective-permute-start | bytes 393224 | tf_op jit(solution)/shard_map/ppermute | solution.py:265
  78.8 1.1 collective-permute-start.5
  79.9 4.5 %collective-permute-start.14 = (bf16[64,8,128]{2,1,0:T(8,128)(2,1)S(1)}, bf16[64,8,128]{2,1,0:T(8,128)(2,1)S(1)}, u32[]{:S(2)}, u32[]{:S(2)}) collective-permute-start(bf16[64,8,128]{2,1,0:T(8,128)(2,1)S(1)} %get-tuple-element.28), channel_id=1, source_target_pairs={{0,1},{1,0},{2,3},{3,2},{4,5},{5,4},{6,7},{7,6},{8,9},{9,8},{10,11... | collective-permute-start | bytes 393224 | tf_op jit(solution)/shard_map/ppermute | solution.py:319
  84.4 2.2 %collective-permute-done.5.refs_3_ = bf16[256,256]{1,0:T(8,128)(2,1)S(1)} collective-permute-done((bf16[256,256]{1,0:T(8,128)(2,1)S(1)}, bf16[256,256]{1,0:T(8,128)(2,1)S(1)}, u32[]{:S(2)}, u32[]{:S(2)}) %collective-permute-start.5) | collective-permute-done | bytes 131104 | tf_op jit(solution)/shard_map/ppermute | solution.py:265
  87.4 3.2 %weights.1 = bf16[16,2,16,512]{3,2,1,0:T(8,128)(2,1)} custom-call(s32[2]{0:T(128)} %copy-done.4, bf16[256,256]{1,0:T(8,128)(2,1)} %copy-done.18, bf16[256,256]{1,0:T(8,128)(2,1)} %copy-done.19, bf16[256,256]{1,0:T(8,128)(2,1)} %copy-done.20, bf16[256,256]{1,0:T(8,128)(2,1)} %copy-done.21, bf16[128,1024]{1,0:T(8,128)(2,1)} %bitcast.33, ...), custom_call_target="tpu_custom_call" | custom-call | flops 600000000 | bytes 4194304 | tf_op jit(solution)/shard_map/weights/pallas_call | solution.py:323
  90.6 6.2 %all-to-all-start.2 = ((bf16[4,128,512]{2,1,0:T(8,128)(2,1)}), bf16[4,128,512]{2,1,0:T(8,128)(2,1)S(1)}, u32[]{:S(2)}, u32[]{:S(2)}) async-start(bf16[4,128,512]{2,1,0:T(8,128)(2,1)} %bitcast.29), calls=%async_computation.2 | async-start | bytes 1048576 | tf_op jit(solution)/shard_map/all_to_all | solution.py:326
  97.0 4.6 %collective-permute-start.13 = (bf16[64,8,128]{2,1,0:T(8,128)(2,1)S(1)}, bf16[64,8,128]{2,1,0:T(8,128)(2,1)S(1)}, u32[]{:S(2)}, u32[]{:S(2)}) collective-permute-start(bf16[64,8,128]{2,1,0:T(8,128)(2,1)S(1)} %get-tuple-element.27), channel_id=1, source_target_pairs={{0,1},{1,0},{2,3},{3,2},{4,5},{5,4},{6,7},{7,6},{8,9},{9,8},{10,11... | collective-permute-start | bytes 393224 | tf_op jit(solution)/shard_map/ppermute | solution.py:319
  101.8 5.5 %all-to-all-done.2 = bf16[4,128,512]{2,1,0:T(8,128)(2,1)S(1)} async-done(((bf16[4,128,512]{2,1,0:T(8,128)(2,1)}), bf16[4,128,512]{2,1,0:T(8,128)(2,1)S(1)}, u32[]{:S(2)}, u32[]{:S(2)}) %all-to-all-start.2) | async-done | bytes 524320 | tf_op jit(solution)/shard_map/all_to_all | solution.py:326
  107.4 0.7 reduce_sum.21
  108.1 6.5 %all-to-all-start.3 = ((bf16[8,16,512]{2,1,0:T(8,128)(2,1)}), bf16[8,16,512]{2,1,0:T(8,128)(2,1)S(1)}, u32[]{:S(2)}, u32[]{:S(2)}) async-start(bf16[8,16,512]{2,1,0:T(8,128)(2,1)} %bitcast.16), calls=%async_computation.3 | async-start | bytes 262144 | tf_op jit(solution)/shard_map/all_to_all | solution.py:353
  114.7 1.1 filter_grad.1
  115.8 0.7 copy-done.12
  116.5 5.8 %input_grad.1 = bf16[128,1024]{1,0:T(8,128)(2,1)} custom-call(s32[1]{0:T(128)} %bitcast.core, bf16[128,1024]{1,0:T(8,128)(2,1)} %bitcast.31, bf16[256,256]{1,0:T(8,128)(2,1)} %constant.34.clone.order, bf16[3072,128]{1,0:T(8,128)(2,1)} %bitcast.26, bf16[1024,128]{1,0:T(8,128)(2,1)} %bitcast.39, bf16[1024,1024]{1,0:T(8,128)(2,1)} %value_w.3, ...), custom_call_target="tpu_custom_call" | custom-call | flops 700000000 | bytes 8388608 | tf_op jit(solution)/shard_map/input_grad/pallas_call | solution.py:330
  (75 shorter events, 4.0 us)
Async XLA Ops:
  0.6 40.3 %copy-start.5 = (bf16[2,128,256]{2,1,0:T(8,128)(2,1)S(1)}, bf16[2,128,256]{2,1,0:T(8,128)(2,1)}, u32[]{:S(2)}) copy-start(bf16[2,128,256]{2,1,0:T(8,128)(2,1)} %constant.36.clone.outer_t) | copy-start | bytes 393220
  0.6 40.3 %copy-start.6 = (bf16[256,256]{1,0:T(8,128)(2,1)S(1)}, bf16[256,256]{1,0:T(8,128)(2,1)}, u32[]{:S(2)}) copy-start(bf16[256,256]{1,0:T(8,128)(2,1)} %constant.39.clone.inner) | copy-start | bytes 393220
  0.7 40.3 %copy-start.7 = (bf16[256,256]{1,0:T(8,128)(2,1)S(1)}, bf16[256,256]{1,0:T(8,128)(2,1)}, u32[]{:S(2)}) copy-start(bf16[256,256]{1,0:T(8,128)(2,1)} %constant.40.clone.inner_t) | copy-start | bytes 393220
  0.7 40.3 %copy-start.8 = (bf16[256,128]{1,0:T(8,128)(2,1)S(1)}, bf16[256,128]{1,0:T(8,128)(2,1)}, u32[]{:S(2)}) copy-start(bf16[256,128]{1,0:T(8,128)(2,1)} %constant.35.clone.outer) | copy-start | bytes 196612
  0.7 40.2 %copy-start.9 = (f32[128,128]{1,0:T(8,128)S(1)}, f32[128,128]{1,0:T(8,128)}, u32[]{:S(2)}) copy-start(f32[128,128]{1,0:T(8,128)} %constant.37.clone.tw_re) | copy-start | bytes 196612
  44.6 29.9 %all-to-all-start.1 = ((bf16[64,48,128]{2,1,0:T(8,128)(2,1)}), bf16[64,48,128]{2,1,0:T(8,128)(2,1)S(1)}, u32[]{:S(2)}, u32[]{:S(2)}) async-start(bf16[64,48,128]{2,1,0:T(8,128)(2,1)} %bitcast.5), calls=%async_computation.1 | async-start | bytes 1572864 | tf_op jit(solution)/shard_map/all_to_all | solution.py:309
  52.0 13.9 %collective-permute-start.7 = (bf16[128,1024]{1,0:T(8,128)(2,1)S(1)}, bf16[128,1024]{1,0:T(8,128)(2,1)S(1)}, u32[]{:S(2)}, u32[]{:S(2)}) collective-permute-start(bf16[128,1024]{1,0:T(8,128)(2,1)S(1)} %bitcast.34), channel_id=1, source_target_pairs={{0,16},{2,18},{4,20},{6,22},{8,24},{10,26},{12,28},{14,30},{16,0},... | collective-permute-start | bytes 786440 | tf_op jit(solution)/shard_map/ppermute | solution.py:265
  53.5 13.8 %collective-permute-start.9 = (bf16[128,1024]{1,0:T(8,128)(2,1)S(1)}, bf16[128,1024]{1,0:T(8,128)(2,1)S(1)}, u32[]{:S(2)}, u32[]{:S(2)}) collective-permute-start(bf16[128,1024]{1,0:T(8,128)(2,1)S(1)} %bitcast.35), channel_id=1, source_target_pairs={{0,64},{2,66},{4,68},{6,70},{8,72},{10,74},{12,76},{14,78},{16,80}... | collective-permute-start | bytes 786440 | tf_op jit(solution)/shard_map/ppermute | solution.py:265
  55.0 18.7 %collective-permute-start.11 = (bf16[128,1024]{1,0:T(8,128)(2,1)S(1)}, bf16[128,1024]{1,0:T(8,128)(2,1)S(1)}, u32[]{:S(2)}, u32[]{:S(2)}) collective-permute-start(bf16[128,1024]{1,0:T(8,128)(2,1)S(1)} %bitcast.36), channel_id=1, source_target_pairs={{0,80},{2,82},{4,84},{6,86},{8,88},{10,90},{12,92},{14,94},{16,64}... | collective-permute-start | bytes 786440 | tf_op jit(solution)/shard_map/ppermute | solution.py:265
  55.5 20.8 %collective-permute-start.6 = (bf16[128,1024]{1,0:T(8,128)(2,1)S(1)}, bf16[128,1024]{1,0:T(8,128)(2,1)S(1)}, u32[]{:S(2)}, u32[]{:S(2)}) collective-permute-start(bf16[128,1024]{1,0:T(8,128)(2,1)S(1)} %bitcast.37), channel_id=1, source_target_pairs={{0,2},{2,0},{1,3},{3,1},{4,6},{6,4},{5,7},{7,5},{8,10},{10,8},{9,1... | collective-permute-start | bytes 786440 | tf_op jit(solution)/shard_map/ppermute | solution.py:236
  55.5 19.0 %collective-permute-start.1 = (bf16[512,128]{1,0:T(8,128)(2,1)S(1)}, bf16[512,128]{1,0:T(8,128)(2,1)S(1)}, u32[]{:S(2)}, u32[]{:S(2)}) collective-permute-start(bf16[512,128]{1,0:T(8,128)(2,1)S(1)} %copy-done.22), channel_id=1, source_target_pairs={{0,2},{2,0},{1,3},{3,1},{4,6},{6,4},{5,7},{7,5},{8,10},{10,8},{9,1... | collective-permute-start | bytes 393224 | tf_op jit(solution)/shard_map/ppermute | solution.py:236
  65.8 10.8 %collective-permute-start.8 = (bf16[128,1024]{1,0:T(8,128)(2,1)S(1)}, bf16[128,1024]{1,0:T(8,128)(2,1)S(1)}, u32[]{:S(2)}, u32[]{:S(2)}) collective-permute-start(bf16[128,1024]{1,0:T(8,128)(2,1)S(1)} %collective-permute-done.7.refs_6_), channel_id=1, source_target_pairs={{0,2},{2,0},{1,3},{3,1},{4,6},{6,4},{5,7},{7,5},{8,10},{10,8},{9,1... | collective-permute-start | bytes 786440 | tf_op jit(solution)/shard_map/ppermute | solution.py:236
  67.3 11.5 %collective-permute-start.10 = (bf16[128,1024]{1,0:T(8,128)(2,1)S(1)}, bf16[128,1024]{1,0:T(8,128)(2,1)}, u32[]{:S(2)}, u32[]{:S(2)}) collective-permute-start(bf16[128,1024]{1,0:T(8,128)(2,1)S(1)} %collective-permute-done.9.refs_8_), channel_id=1, source_target_pairs={{0,2},{2,0},{1,3},{3,1},{4,6},{6,4},{5,7},{7,5},{8,10},{10,8},{9,1... | collective-permute-start | bytes 786440 | tf_op jit(solution)/shard_map/ppermute | solution.py:236
  73.7 6.2 %collective-permute-start.12 = (bf16[128,1024]{1,0:T(8,128)(2,1)S(1)}, bf16[128,1024]{1,0:T(8,128)(2,1)}, u32[]{:S(2)}, u32[]{:S(2)}) collective-permute-start(bf16[128,1024]{1,0:T(8,128)(2,1)S(1)} %collective-permute-done.11.refs_10_), channel_id=1, source_target_pairs={{0,2},{2,0},{1,3},{3,1},{4,6},{6,4},{5,7},{7,5},{8,10},{10,8},{9,1... | collective-permute-start | bytes 786440 | tf_op jit(solution)/shard_map/ppermute | solution.py:236
  75.7 8.7 %collective-permute-start.2 = (bf16[256,256]{1,0:T(8,128)(2,1)S(1)}, bf16[256,256]{1,0:T(8,128)(2,1)S(1)}, u32[]{:S(2)}, u32[]{:S(2)}) collective-permute-start(bf16[256,256]{1,0:T(8,128)(2,1)S(1)} %get-tuple-element.23), channel_id=1, source_target_pairs={{0,0},{2,2},{4,4},{6,6},{8,8},{10,10},{12,12},{14,14},{16,16},{18,... | collective-permute-start | bytes 393224 | tf_op jit(solution)/shard_map/ppermute | solution.py:265
  76.4 8.0 %collective-permute-start.3 = (bf16[256,256]{1,0:T(8,128)(2,1)S(1)}, bf16[256,256]{1,0:T(8,128)(2,1)S(1)}, u32[]{:S(2)}, u32[]{:S(2)}) collective-permute-start(bf16[256,256]{1,0:T(8,128)(2,1)S(1)} %get-tuple-element.24), channel_id=1, source_target_pairs={{0,16},{2,18},{4,20},{6,22},{8,24},{10,26},{12,28},{14,30},{16,0},... | collective-permute-start | bytes 393224 | tf_op jit(solution)/shard_map/ppermute | solution.py:265
  76.7 7.8 %collective-permute-start.4 = (bf16[256,256]{1,0:T(8,128)(2,1)S(1)}, bf16[256,256]{1,0:T(8,128)(2,1)S(1)}, u32[]{:S(2)}, u32[]{:S(2)}) collective-permute-start(bf16[256,256]{1,0:T(8,128)(2,1)S(1)} %get-tuple-element.25), channel_id=1, source_target_pairs={{0,66},{2,64},{4,70},{6,68},{8,74},{10,72},{12,78},{14,76},{16,82}... | collective-permute-start | bytes 393224 | tf_op jit(solution)/shard_map/ppermute | solution.py:265
  78.8 7.9 %collective-permute-start.5 = (bf16[256,256]{1,0:T(8,128)(2,1)S(1)}, bf16[256,256]{1,0:T(8,128)(2,1)S(1)}, u32[]{:S(2)}, u32[]{:S(2)}) collective-permute-start(bf16[256,256]{1,0:T(8,128)(2,1)S(1)} %get-tuple-element.26), channel_id=1, source_target_pairs={{0,82},{2,80},{4,86},{6,84},{8,90},{10,88},{12,94},{14,92},{16,66}... | collective-permute-start | bytes 393224 | tf_op jit(solution)/shard_map/ppermute | solution.py:265
  79.9 21.7 %collective-permute-start.14 = (bf16[64,8,128]{2,1,0:T(8,128)(2,1)S(1)}, bf16[64,8,128]{2,1,0:T(8,128)(2,1)S(1)}, u32[]{:S(2)}, u32[]{:S(2)}) collective-permute-start(bf16[64,8,128]{2,1,0:T(8,128)(2,1)S(1)} %get-tuple-element.28), channel_id=1, source_target_pairs={{0,1},{1,0},{2,3},{3,2},{4,5},{5,4},{6,7},{7,6},{8,9},{9,8},{10,11... | collective-permute-start | bytes 393224 | tf_op jit(solution)/shard_map/ppermute | solution.py:319
  90.6 16.7 %all-to-all-start.2 = ((bf16[4,128,512]{2,1,0:T(8,128)(2,1)}), bf16[4,128,512]{2,1,0:T(8,128)(2,1)S(1)}, u32[]{:S(2)}, u32[]{:S(2)}) async-start(bf16[4,128,512]{2,1,0:T(8,128)(2,1)} %bitcast.29), calls=%async_computation.2 | async-start | bytes 1048576 | tf_op jit(solution)/shard_map/all_to_all | solution.py:326
  96.9 18.9 %collective-permute-start = (bf16[64,16,128]{2,1,0:T(8,128)(2,1)S(1)}, bf16[64,16,128]{2,1,0:T(8,128)(2,1)S(1)}, u32[]{:S(2)}, u32[]{:S(2)}) collective-permute-start(bf16[64,16,128]{2,1,0:T(8,128)(2,1)S(1)} %slice_bitcast_fusion), channel_id=1, source_target_pairs={{0,2},{2,0},{1,3},{3,1},{4,6},{6,4},{5,7},{7,5},{8,10},{10,8},{9,1... | collective-permute-start | bytes 786440 | tf_op jit(solution)/shard_map/ppermute | solution.py:236
  97.0 17.6 %collective-permute-start.13 = (bf16[64,8,128]{2,1,0:T(8,128)(2,1)S(1)}, bf16[64,8,128]{2,1,0:T(8,128)(2,1)S(1)}, u32[]{:S(2)}, u32[]{:S(2)}) collective-permute-start(bf16[64,8,128]{2,1,0:T(8,128)(2,1)S(1)} %get-tuple-element.27), channel_id=1, source_target_pairs={{0,1},{1,0},{2,3},{3,2},{4,5},{5,4},{6,7},{7,6},{8,9},{9,8},{10,11... | collective-permute-start | bytes 393224 | tf_op jit(solution)/shard_map/ppermute | solution.py:319
  101.6 13.1 %collective-permute-start.15 = (bf16[64,8,128]{2,1,0:T(8,128)(2,1)S(1)}, bf16[64,8,128]{2,1,0:T(8,128)(2,1)S(1)}, u32[]{:S(2)}, u32[]{:S(2)}) collective-permute-start(bf16[64,8,128]{2,1,0:T(8,128)(2,1)S(1)} %add_convert_fusion), channel_id=1, source_target_pairs={{0,2},{2,0},{1,3},{3,1},{4,6},{6,4},{5,7},{7,5},{8,10},{10,8},{9,1... | collective-permute-start | bytes 393224 | tf_op jit(solution)/shard_map/ppermute | solution.py:236
  108.1 14.2 %all-to-all-start.3 = ((bf16[8,16,512]{2,1,0:T(8,128)(2,1)}), bf16[8,16,512]{2,1,0:T(8,128)(2,1)S(1)}, u32[]{:S(2)}, u32[]{:S(2)}) async-start(bf16[8,16,512]{2,1,0:T(8,128)(2,1)} %bitcast.16), calls=%async_computation.3 | async-start | bytes 262144 | tf_op jit(solution)/shard_map/all_to_all | solution.py:353
  (18 other events, 284.6 us)

commit v6 on v5

--- a/solution.py
+++ b/solution.py
@@ -39,13 +39,11 @@
 def block_order():
     index = []
     for half in range(2):
-        for y0 in range(2):
-            for y1 in range(2):
-                for zz in range(4):
-                    for i in range(16):
-                        y = 2 * y1 + y0
-                        x, z, q = (y, zz, i) if half == 0 else (3 - y, 3 - zz, 15 - i)
-                        index.append((16 * x + 4 * (q // 4) + z) * 8 + 4 * half + q % 4)
+        for y in range(4):
+            for zz in range(4):
+                for i in range(16):
+                    x, z, q = (y, zz, i) if half == 0 else (3 - y, 3 - zz, 15 - i)
+                    index.append((16 * x + 4 * (q // 4) + z) * 8 + 4 * half + q % 4)
     return one_hot_rows(np.array(index), 512)
 
 
@@ -169,14 +167,15 @@
         mixed = full[:, base:base + 8].reshape(512, SIDE)
         grads.append(full[:, base + 8:base + 16].reshape(512, SIDE).astype(BF16))
         gates.append((mixed * cot[...].astype(F32)).astype(BF16))
-    for a, group in enumerate((grads, gates)):
+    parts = []
+    for group in (grads, gates):
         rows = dot(blocks[...], jnp.concatenate(group, axis=1))
-        parts = [[rows[(2 * h + q) * SIDE:(2 * h + q + 1) * SIDE] for q in range(2)] for h in range(2)]
+        parts.append((rows[:256], rows[256:]))
+    for far_x in range(2):
+        line = [jnp.where(odd[1] == 1, parts[1 - far_x][h], parts[far_x][h]) for h in range(2)]
         for dx in range(2):
-            line = [jnp.where(odd[0] == 1, parts[1 - dx][q], parts[dx][q]) for q in range(2)]
-            for dy in range(2):
-                part = jnp.where(odd[1] == 1, line[1 - dy], line[dy])
-                outs[2 * dx + dy][a * SIDE:(a + 1) * SIDE, :] = part.astype(BF16)
+            part = jnp.where(odd[0] == 1, line[1 - dx], line[dx])
+            outs[2 * far_x + dx][...] = part.astype(BF16)
 
 
 def weights_kernel(odd, *refs):
@@ -203,23 +202,26 @@
     return jnp.concatenate(low + high, axis=1)
 
 
-def inputs_kernel(core, cot, order, home, far, value_w, gate_w, input_grad, w_buf, stack, sems):
+def natural_kernel(core, cot, order, home, far, rows, stack):
+    near = home[...].astype(F32).reshape(CHIPS, 2 * ROWS, SIDE)
+    other = far[...].astype(F32).reshape(CHIPS, 16, SIDE)
+    for side, full in ((0, near), (1, other)):
+        stack[:, core[0] ^ side] = jnp.concatenate([full[:, :8], full[:, 8:16]], axis=2)
+    natural = natural_order(stack, order)
+    rows[:SIDE, :] = (natural[:SIDE] * cot[...].astype(F32)).astype(BF16)
+    rows[SIDE:, :] = natural[SIDE:].astype(BF16)
+
+
+def inputs_kernel(rows, value_w, gate_w, input_grad, w_buf, sems):
     fetch = [
         pltpu.make_async_copy(w, w_buf.at[i], sems.at[i]) for i, w in enumerate((value_w, gate_w))
     ]
     for copy in fetch:
         copy.start()
-    near = home[...].astype(F32).reshape(CHIPS, 2 * ROWS, SIDE)
-    other = far[...].astype(F32).reshape(CHIPS, 16, SIDE)
-    for side, full in ((0, near), (1, other)):
-        stack[:, core[0] ^ side] = jnp.concatenate([full[:, :8], full[:, 8:16]], axis=2)
-    natural = natural_order(stack, order)
-    gated = (natural[:SIDE] * cot[...].astype(F32)).astype(BF16)
-    grad = natural[SIDE:].astype(BF16)
     fetch[0].wait()
-    total = dot(grad, w_buf[0], 1, 1)
+    total = dot(rows[SIDE:, :], w_buf[0], 1, 1)
     fetch[1].wait()
-    input_grad[...] = (total + dot(gated, w_buf[1], 1, 1)).astype(BF16)
+    input_grad[...] = (total + dot(rows[:SIDE, :], w_buf[1], 1, 1)).astype(BF16)
 
 
 def filter_kernel(core, order, own, far, filter_grad, stack):
@@ -251,23 +253,19 @@
     )
 
 
-def near(a, dx, dy, cross=False):
+def near(a, far_x, dx, cross=False):
     pairs = []
-    for x0 in range(2):
-        for y1 in range(2):
-            for y0 in range(2):
-                for z in range(4):
-                    for c in range(2):
-                        x_to = x0 ^ dx
-                        c_to = c ^ x_to if cross else c
-                        start = (((2 * x0 + y1) * 2 + y0) * 4 + z) * 2 + c
-                        pairs.append((start, (((2 * x_to + y1) * 2 + (y0 ^ dy)) * 4 + z) * 2 + c_to))
-    return lax.ppermute(a, ("x0", "y1", "y0", "z", "c"), pairs)
+    for x in range(4):
+        for c in range(2):
+            x_to = x ^ (2 * far_x + dx)
+            c_to = c ^ (x_to & 1) if cross else c
+            pairs.append((2 * x + c, 2 * x_to + c_to))
+    return lax.ppermute(a, ("x1", "x0", "c"), pairs)
 
 
 def local(inputs, cotangent, value_weight, gate_weight, filter_taps):
     core = lax.axis_index("c").astype(jnp.int32).reshape(1)
-    odd = jnp.stack([lax.axis_index(name).astype(jnp.int32) for name in ("x0", "y0")])
+    odd = jnp.stack([lax.axis_index(name).astype(jnp.int32) for name in ("x0", "x1")])
     order = jnp.asarray(spread_order())
     flat_in = inputs.reshape(SIDE, D)
     cot = cotangent.reshape(SIDE, D)
@@ -321,23 +319,34 @@
     filter_sum = jnp.concatenate(sums, axis=0).reshape(2, CHIPS, 8, SIDE)
     rows = [near(rows[2 * dx + dy], dx, dy, True) for dx in range(2) for dy in range(2)]
     (partial,) = kernel(
-        "weights", weights_kernel, [shape(16, 2, 16, 512)], [SMEM] + [VMEM] * 12, gflop=0.6, mbyte=4.0, limit=56
+        "weights", weights_kernel, [shape(16, 2, 16, 512)], [SMEM] + [VMEM] * 12, gflop=0.6, mbyte=4.0, limit=20
     )(odd, *rows, *ins)
-    parts = lax.all_to_all(partial.reshape(4, SIDE, 512), ("x1", "y1"), 0, 0, tiled=True)
+    parts = lax.all_to_all(partial.reshape(4, SIDE, 512), ("y1", "y0"), 0, 0, tiled=True)
 
     far = swap_cores(shaped[:, 1, :16])
     filter_far = swap_cores(filter_sum[1])
+    (natural,) = kernel(
+        "natural",
+        natural_kernel,
+        [shape(2 * SIDE, D)],
+        [SMEM] + [VMEM] * 4,
+        0,
+        [pltpu.VMEM((CHIPS, 2, 8, 2 * SIDE), F32)],
+        0.2,
+        3.0,
+    )(core, cot, order, home.reshape(3072, SIDE), far.reshape(1024, SIDE))
+    parts, natural = lax.optimization_barrier((parts, natural))
     (input_grad,) = kernel(
         "input_grad",
         inputs_kernel,
         [shape(SIDE, D)],
-        [SMEM] + [VMEM] * 4,
+        [VMEM],
         2,
-        [w_scratch, pltpu.VMEM((CHIPS, 2, 8, 2 * SIDE), F32), sems],
-        0.7,
+        [w_scratch, sems],
+        0.6,
         8.0,
         56,
-    )(core, cot, order, home.reshape(3072, SIDE), far.reshape(1024, SIDE), value_weight, gate_weight)
+    )(natural, value_weight, gate_weight)
     (filter_grad,) = kernel(
         "filter_grad",
         filter_kernel,

time: 123 us -> 122 us (level)
  waiting for transfers between devices: 26.2 us -> 24.3 us
    all_to_all x1, waiting for transfers between devices: 5.54 us -> 2.21 us  [local(): lax.all_to_all(partial.reshape(4, SIDE, 512), ('y1', 'y0'), 0, 0, tiled=T...]
    ppermute x7, starting transfers between devices: 7.75 us -> 10.3 us  [near(): return lax.ppermute(a, ('x1', 'x0', 'c'), pairs)]
    all_to_all x1, starting transfers between devices: 6.22 us -> 4.48 us  [local(): lax.all_to_all(partial.reshape(4, SIDE, 512), ('y1', 'y0'), 0, 0, tiled=T...]
    ppermute x7, waiting for transfers between devices: 19.8 us -> 21.3 us  [near(): return lax.ppermute(a, ('x1', 'x0', 'c'), pairs)]
    pallas_call x1 -> x2, Pallas kernels: 5.78 us -> 5.91 us  [the longest x1 5.48 us: local(): kernel('input_grad', inputs_kernel, [shape(SIDE, D)], [VMEM], 2, [w_scrat...]
  transfers between devices with their start and end apart: 19 -> 19, of which waited for: 6 -> 7; matrix products, arithmetic and copies ran while one was open for 1% -> 2% of each run, Pallas kernels for 9% -> 9%
where the time goes in v6:
time: 122 us
  starting transfers between devices  38.3 us (31%)
  blocking collectives  35 us (29%)
  waiting for transfers between devices  24.3 us (20%)
  Pallas kernels  19.3 us (16%)
  other arithmetic  2.5 us (2%)
  local copies, waits for them, and re-layouts  1.59 us (1%)
    all_to_all x1, blocking collectives, local(): lax.all_to_all(message.reshape(2 * CHIPS, ROWS, SIDE), SEQ, 0, 0, tiled=T...  35 us
    ppermute x7, waiting for transfers between devices, near(): return lax.ppermute(a, ('x1', 'x0', 'c'), pairs)  21.3 us
    ppermute x7, starting transfers between devices, near(): return lax.ppermute(a, ('x1', 'x0', 'c'), pairs)  10.3 us
    ppermute x2, starting transfers between devices, local(): others = [lax.ppermute(cut, 'dp', [(0, 1), (1, 0)]) for cut in cuts]  9.06 us
    all_to_all x1, starting transfers between devices, local(): lax.all_to_all(result.reshape(CHIPS, 2 * ROWS, SIDE), SEQ[:5], 0, 0, tile...  7.32 us
    all_to_all x1, starting transfers between devices, local(): final = lax.all_to_all(rows, ('z', 'dp'), 0, 0, tiled=True)  6.32 us
    pallas_call x1, Pallas kernels, local(): kernel('input_grad', inputs_kernel, [shape(SIDE, D)], [VMEM], 2, [w_scrat...  5.48 us
    pallas_call x1, Pallas kernels, local(): kernel('project', project_kernel, [shape(2 * CHIPS * ROWS, SIDE), shape(5...  5.14 us
  transfers between devices with their start and end apart: 19, of which 7 were waited for; matrix products, arithmetic and copies ran while one was open for 2% of the time, Pallas kernels for 9%

profile of v6, /device:TPU:32, one launch (start us, length us, event | category | flops | bytes accessed | tf_op | source)
XLA Modules:
  0.0 121.9 jit_solution(5800057326338665750)
XLA Ops:
  0.7 5.1 %project.1 = (bf16[3072,128]{1,0:T(8,128)(2,1)}, bf16[512,128]{1,0:T(8,128)(2,1)}, bf16[512,128]{1,0:T(8,128)(2,1)}) custom-call(s32[1]{0:T(128)} %bitcast.2.core, bf16[128,1024]{1,0:T(8,128)(2,1)} %bitcast.29, bf16[128,1024]{1,0:T(8,128)(2,1)} %bitcast.27, bf16[128,1024]{1,0:T(8,128)(2,1)} %taps.1, bf16[256,256]{1,0:T(8,128)(2,1)} %constant.34.clone.order, ...), custom_call_target="tpu_custom_call" | custom-call | flops 800000000 | bytes 8388608 | tf_op jit(solution)/shard_map/project/pallas_call | solution.py:275
  5.9 35.0 %all_to_all.20 = bf16[128,24,128]{2,1,0:T(8,128)(2,1)S(1)} all-to-all(bf16[128,24,128]{2,1,0:T(8,128)(2,1)} %bitcast.38), channel_id=1, replica_groups=mesh['x1'=2,'x0'=2,'y1'=2,'y0'=2,'z'=4,'c'=2,'dp'=2] {'x1','x0','y1','y0..., dimensions={0} | all-to-all | bytes 1572864 | tf_op jit(solution)/shard_map/all_to_all | solution.py:286
  41.0 3.7 %convolve.1 = bf16[3072,128]{1,0:T(8,128)(2,1)} custom-call(s32[1]{0:T(128)} %bitcast.2.core, bf16[3072,128]{1,0:T(8,128)(2,1)S(1)} %bitcast.35, bf16[256,128]{1,0:T(8,128)(2,1)S(1)} %copy-done.9, bf16[2,128,256]{2,1,0:T(8,128)(2,1)S(1)} %copy-done.6, f32[128,128]{1,0:T(8,128)S(1)} %copy-done.10, f32[128,128]{1,0:T(8,128)S(1)} %copy-done.11, ...), custom_call_target="tpu_custom_call" | custom-call | flops 1200000000 | bytes 4194304 | tf_op jit(solution)/shard_map/convolve/pallas_call | solution.py:294
  44.6 7.3 %all-to-all-start.1 = ((bf16[64,48,128]{2,1,0:T(8,128)(2,1)}), bf16[64,48,128]{2,1,0:T(8,128)(2,1)S(1)}, u32[]{:S(2)}, u32[]{:S(2)}) async-start(bf16[64,48,128]{2,1,0:T(8,128)(2,1)} %bitcast.7), calls=%async_computation.1 | async-start | bytes 1572864 | tf_op jit(solution)/shard_map/all_to_all | solution.py:307
  52.0 1.6 %collective-permute-start.6 = (bf16[128,1024]{1,0:T(8,128)(2,1)S(1)}, bf16[128,1024]{1,0:T(8,128)(2,1)S(1)}, u32[]{:S(2)}, u32[]{:S(2)}) collective-permute-start(bf16[128,1024]{1,0:T(8,128)(2,1)S(1)} %bitcast.30), channel_id=1, source_target_pairs={{0,64},{2,66},{64,0},{66,2},{128,192},{130,194},{192,128},{194,130... | collective-permute-start | bytes 786440 | tf_op jit(solution)/shard_map/ppermute | solution.py:263
  53.5 2.9 %collective-permute-start.8 = (bf16[128,1024]{1,0:T(8,128)(2,1)S(1)}, bf16[128,1024]{1,0:T(8,128)(2,1)S(1)}, u32[]{:S(2)}, u32[]{:S(2)}) collective-permute-start(bf16[128,1024]{1,0:T(8,128)(2,1)S(1)} %bitcast.31), channel_id=1, source_target_pairs={{0,128},{2,130},{64,192},{66,194},{128,0},{130,2},{192,64},{194,66... | collective-permute-start | bytes 786440 | tf_op jit(solution)/shard_map/ppermute | solution.py:263
  57.3 10.0 %collective-permute-done.6.refs_6_ = bf16[128,1024]{1,0:T(8,128)(2,1)S(1)} collective-permute-done((bf16[128,1024]{1,0:T(8,128)(2,1)S(1)}, bf16[128,1024]{1,0:T(8,128)(2,1)S(1)}, u32[]{:S(2)}, u32[]{:S(2)}) %collective-permute-start.6) | collective-permute-done | bytes 262176 | tf_op jit(solution)/shard_map/ppermute | solution.py:263
  67.4 7.0 %collective-permute-done.8.refs_8_ = bf16[128,1024]{1,0:T(8,128)(2,1)S(1)} collective-permute-done((bf16[128,1024]{1,0:T(8,128)(2,1)S(1)}, bf16[128,1024]{1,0:T(8,128)(2,1)S(1)}, u32[]{:S(2)}, u32[]{:S(2)}) %collective-permute-start.8) | collective-permute-done | bytes 262176 | tf_op jit(solution)/shard_map/ppermute | solution.py:263
  75.6 1.0 gate.1
  76.6 0.8 collective-permute-start.1
  77.5 2.2 %collective-permute-start.2 = (bf16[256,256]{1,0:T(8,128)(2,1)S(1)}, bf16[256,256]{1,0:T(8,128)(2,1)S(1)}, u32[]{:S(2)}, u32[]{:S(2)}) collective-permute-start(bf16[256,256]{1,0:T(8,128)(2,1)S(1)} %get-tuple-element.26), channel_id=1, source_target_pairs={{0,66},{2,64},{64,0},{66,2},{128,194},{130,192},{192,128},{194,130... | collective-permute-start | bytes 393224 | tf_op jit(solution)/shard_map/ppermute | solution.py:263
  79.7 1.9 %collective-permute-start.3 = (bf16[256,256]{1,0:T(8,128)(2,1)S(1)}, bf16[256,256]{1,0:T(8,128)(2,1)S(1)}, u32[]{:S(2)}, u32[]{:S(2)}) collective-permute-start(bf16[256,256]{1,0:T(8,128)(2,1)S(1)} %get-tuple-element.27), channel_id=1, source_target_pairs={{0,128},{2,130},{64,194},{66,192},{128,0},{130,2},{192,66},{194,64... | collective-permute-start | bytes 393224 | tf_op jit(solution)/shard_map/ppermute | solution.py:263
  82.1 4.5 %collective-permute-start.14 = (bf16[64,8,128]{2,1,0:T(8,128)(2,1)}, bf16[64,8,128]{2,1,0:T(8,128)(2,1)}, u32[]{:S(2)}, u32[]{:S(2)}) collective-permute-start(bf16[64,8,128]{2,1,0:T(8,128)(2,1)} %get-tuple-element.32), channel_id=1, source_target_pairs={{0,1},{1,0},{2,3},{3,2},{4,5},{5,4},{6,7},{7,6},{8,9},{9,8},{10,11... | collective-permute-start | bytes 393224 | tf_op jit(solution)/shard_map/ppermute | solution.py:317
  86.6 1.5 %collective-permute-done.3.refs_2_ = bf16[256,256]{1,0:T(8,128)(2,1)S(1)} collective-permute-done((bf16[256,256]{1,0:T(8,128)(2,1)S(1)}, bf16[256,256]{1,0:T(8,128)(2,1)S(1)}, u32[]{:S(2)}, u32[]{:S(2)}) %collective-permute-start.3) | collective-permute-done | bytes 131104 | tf_op jit(solution)/shard_map/ppermute | solution.py:263
  88.1 2.3 %collective-permute-done.4.refs_3_ = bf16[256,256]{1,0:T(8,128)(2,1)S(1)} collective-permute-done((bf16[256,256]{1,0:T(8,128)(2,1)S(1)}, bf16[256,256]{1,0:T(8,128)(2,1)S(1)}, u32[]{:S(2)}, u32[]{:S(2)}) %collective-permute-start.4) | collective-permute-done | bytes 131104 | tf_op jit(solution)/shard_map/ppermute | solution.py:263
  90.4 2.5 %weights.1 = bf16[16,2,16,512]{3,2,1,0:T(8,128)(2,1)} custom-call(s32[2]{0:T(128)S(1)} %pad_add_fusion.odd, bf16[256,256]{1,0:T(8,128)(2,1)S(1)} %collective-permute-done.1.refs_0_, bf16[256,256]{1,0:T(8,128)(2,1)S(1)} %collective-permute-done.2.refs_1_, bf16[256,256]{1,0:T(8,128)(2,1)S(1)} %collective-permute-done.3.refs_2_, ...), custom_call_target="tpu_custom_call" | custom-call | flops 600000000 | bytes 4194304 | tf_op jit(solution)/shard_map/weights/pallas_call | solution.py:321
  92.9 4.5 %all-to-all-start.2 = ((bf16[4,128,512]{2,1,0:T(8,128)(2,1)}), bf16[4,128,512]{2,1,0:T(8,128)(2,1)S(1)}, u32[]{:S(2)}, u32[]{:S(2)}) async-start(bf16[4,128,512]{2,1,0:T(8,128)(2,1)} %bitcast.12), calls=%async_computation.2 | async-start | bytes 1048576 | tf_op jit(solution)/shard_map/all_to_all | solution.py:324
  97.5 4.6 %collective-permute-start.13 = (bf16[64,8,128]{2,1,0:T(8,128)(2,1)S(1)}, bf16[64,8,128]{2,1,0:T(8,128)(2,1)S(1)}, u32[]{:S(2)}, u32[]{:S(2)}) collective-permute-start(bf16[64,8,128]{2,1,0:T(8,128)(2,1)S(1)} %copy-done.12), channel_id=1, source_target_pairs={{0,1},{1,0},{2,3},{3,2},{4,5},{5,4},{6,7},{7,6},{8,9},{9,8},{10,11... | collective-permute-start | bytes 393224 | tf_op jit(solution)/shard_map/ppermute | solution.py:317
  102.1 1.0 add_convert_fusion
  104.6 2.2 %all-to-all-done.2 = bf16[4,128,512]{2,1,0:T(8,128)(2,1)S(1)} async-done(((bf16[4,128,512]{2,1,0:T(8,128)(2,1)}), bf16[4,128,512]{2,1,0:T(8,128)(2,1)S(1)}, u32[]{:S(2)}, u32[]{:S(2)}) %all-to-all-start.2) | async-done | bytes 524320 | tf_op jit(solution)/shard_map/all_to_all | solution.py:324
  107.5 6.3 %all-to-all-start.3 = ((bf16[8,16,512]{2,1,0:T(8,128)(2,1)}), bf16[8,16,512]{2,1,0:T(8,128)(2,1)S(1)}, u32[]{:S(2)}, u32[]{:S(2)}) async-start(bf16[8,16,512]{2,1,0:T(8,128)(2,1)} %bitcast.16), calls=%async_computation.3 | async-start | bytes 262144 | tf_op jit(solution)/shard_map/all_to_all | solution.py:362
  113.9 1.1 filter_grad.1
  115.0 5.5 %input_grad.1 = bf16[128,1024]{1,0:T(8,128)(2,1)} custom-call(bf16[256,1024]{1,0:T(8,128)(2,1)} %copy-done, bf16[1024,1024]{1,0:T(8,128)(2,1)} %value_w.3, bf16[1024,1024]{1,0:T(8,128)(2,1)} %gate_w.3), custom_call_target="tpu_custom_call" | custom-call | flops 600000000 | bytes 8388608 | tf_op jit(solution)/shard_map/input_grad/pallas_call | solution.py:339
  120.5 0.8 all-to-all-done.3
  (58 shorter events, 5.9 us)
Async XLA Ops:
  0.6 40.3 %copy-start.6 = (bf16[2,128,256]{2,1,0:T(8,128)(2,1)S(1)}, bf16[2,128,256]{2,1,0:T(8,128)(2,1)}, u32[]{:S(2)}) copy-start(bf16[2,128,256]{2,1,0:T(8,128)(2,1)} %constant.36.clone.outer_t) | copy-start | bytes 393220
  0.6 40.3 %copy-start.7 = (bf16[256,256]{1,0:T(8,128)(2,1)S(1)}, bf16[256,256]{1,0:T(8,128)(2,1)}, u32[]{:S(2)}) copy-start(bf16[256,256]{1,0:T(8,128)(2,1)} %constant.39.clone.inner) | copy-start | bytes 393220
  0.7 40.3 %copy-start.8 = (bf16[256,256]{1,0:T(8,128)(2,1)S(1)}, bf16[256,256]{1,0:T(8,128)(2,1)}, u32[]{:S(2)}) copy-start(bf16[256,256]{1,0:T(8,128)(2,1)} %constant.40.clone.inner_t) | copy-start | bytes 393220
  0.7 40.2 %copy-start.9 = (bf16[256,128]{1,0:T(8,128)(2,1)S(1)}, bf16[256,128]{1,0:T(8,128)(2,1)}, u32[]{:S(2)}) copy-start(bf16[256,128]{1,0:T(8,128)(2,1)} %constant.35.clone.outer) | copy-start | bytes 196612
  0.7 40.2 %copy-start.10 = (f32[128,128]{1,0:T(8,128)S(1)}, f32[128,128]{1,0:T(8,128)}, u32[]{:S(2)}) copy-start(f32[128,128]{1,0:T(8,128)} %constant.37.clone.tw_re) | copy-start | bytes 196612
  44.6 30.2 %all-to-all-start.1 = ((bf16[64,48,128]{2,1,0:T(8,128)(2,1)}), bf16[64,48,128]{2,1,0:T(8,128)(2,1)S(1)}, u32[]{:S(2)}, u32[]{:S(2)}) async-start(bf16[64,48,128]{2,1,0:T(8,128)(2,1)} %bitcast.7), calls=%async_computation.1 | async-start | bytes 1572864 | tf_op jit(solution)/shard_map/all_to_all | solution.py:307
  52.0 15.4 %collective-permute-start.6 = (bf16[128,1024]{1,0:T(8,128)(2,1)S(1)}, bf16[128,1024]{1,0:T(8,128)(2,1)S(1)}, u32[]{:S(2)}, u32[]{:S(2)}) collective-permute-start(bf16[128,1024]{1,0:T(8,128)(2,1)S(1)} %bitcast.30), channel_id=1, source_target_pairs={{0,64},{2,66},{64,0},{66,2},{128,192},{130,194},{192,128},{194,130... | collective-permute-start | bytes 786440 | tf_op jit(solution)/shard_map/ppermute | solution.py:263
  53.5 20.8 %collective-permute-start.8 = (bf16[128,1024]{1,0:T(8,128)(2,1)S(1)}, bf16[128,1024]{1,0:T(8,128)(2,1)S(1)}, u32[]{:S(2)}, u32[]{:S(2)}) collective-permute-start(bf16[128,1024]{1,0:T(8,128)(2,1)S(1)} %bitcast.31), channel_id=1, source_target_pairs={{0,128},{2,130},{64,192},{66,194},{128,0},{130,2},{192,64},{194,66... | collective-permute-start | bytes 786440 | tf_op jit(solution)/shard_map/ppermute | solution.py:263
  56.4 18.5 %collective-permute-start.10 = (bf16[128,1024]{1,0:T(8,128)(2,1)S(1)}, bf16[128,1024]{1,0:T(8,128)(2,1)S(1)}, u32[]{:S(2)}, u32[]{:S(2)}) collective-permute-start(bf16[128,1024]{1,0:T(8,128)(2,1)S(1)} %bitcast.32), channel_id=1, source_target_pairs={{0,192},{2,194},{64,128},{66,130},{128,64},{130,66},{192,0},{194,2... | collective-permute-start | bytes 786440 | tf_op jit(solution)/shard_map/ppermute | solution.py:263
  56.8 20.7 %collective-permute-start.5 = (bf16[128,1024]{1,0:T(8,128)(2,1)S(1)}, bf16[128,1024]{1,0:T(8,128)(2,1)S(1)}, u32[]{:S(2)}, u32[]{:S(2)}) collective-permute-start(bf16[128,1024]{1,0:T(8,128)(2,1)S(1)} %bitcast.33), channel_id=1, source_target_pairs={{0,2},{2,0},{1,3},{3,1},{4,6},{6,4},{5,7},{7,5},{8,10},{10,8},{9,1... | collective-permute-start | bytes 786440 | tf_op jit(solution)/shard_map/ppermute | solution.py:238
  56.8 18.8 %collective-permute-start = (bf16[512,128]{1,0:T(8,128)(2,1)S(1)}, bf16[512,128]{1,0:T(8,128)(2,1)S(1)}, u32[]{:S(2)}, u32[]{:S(2)}) collective-permute-start(bf16[512,128]{1,0:T(8,128)(2,1)S(1)} %copy-done.13), channel_id=1, source_target_pairs={{0,2},{2,0},{1,3},{3,1},{4,6},{6,4},{5,7},{7,5},{8,10},{10,8},{9,1... | collective-permute-start | bytes 393224 | tf_op jit(solution)/shard_map/ppermute | solution.py:238
  67.3 12.3 %collective-permute-start.7 = (bf16[128,1024]{1,0:T(8,128)(2,1)S(1)}, bf16[128,1024]{1,0:T(8,128)(2,1)S(1)}, u32[]{:S(2)}, u32[]{:S(2)}) collective-permute-start(bf16[128,1024]{1,0:T(8,128)(2,1)S(1)} %collective-permute-done.6.refs_6_), channel_id=1, source_target_pairs={{0,2},{2,0},{1,3},{3,1},{4,6},{6,4},{5,7},{7,5},{8,10},{10,8},{9,1... | collective-permute-start | bytes 786440 | tf_op jit(solution)/shard_map/ppermute | solution.py:238
  74.3 7.2 %collective-permute-start.9 = (bf16[128,1024]{1,0:T(8,128)(2,1)S(1)}, bf16[128,1024]{1,0:T(8,128)(2,1)S(1)}, u32[]{:S(2)}, u32[]{:S(2)}) collective-permute-start(bf16[128,1024]{1,0:T(8,128)(2,1)S(1)} %collective-permute-done.8.refs_8_), channel_id=1, source_target_pairs={{0,2},{2,0},{1,3},{3,1},{4,6},{6,4},{5,7},{7,5},{8,10},{10,8},{9,1... | collective-permute-start | bytes 786440 | tf_op jit(solution)/shard_map/ppermute | solution.py:238
  74.9 7.3 %collective-permute-start.11 = (bf16[128,1024]{1,0:T(8,128)(2,1)S(1)}, bf16[128,1024]{1,0:T(8,128)(2,1)}, u32[]{:S(2)}, u32[]{:S(2)}) collective-permute-start(bf16[128,1024]{1,0:T(8,128)(2,1)S(1)} %collective-permute-done.10.refs_10_), channel_id=1, source_target_pairs={{0,2},{2,0},{1,3},{3,1},{4,6},{6,4},{5,7},{7,5},{8,10},{10,8},{9,1... | collective-permute-start | bytes 786440 | tf_op jit(solution)/shard_map/ppermute | solution.py:238
  76.6 10.0 %collective-permute-start.1 = (bf16[256,256]{1,0:T(8,128)(2,1)S(1)}, bf16[256,256]{1,0:T(8,128)(2,1)S(1)}, u32[]{:S(2)}, u32[]{:S(2)}) collective-permute-start(bf16[256,256]{1,0:T(8,128)(2,1)S(1)} %get-tuple-element.25), channel_id=1, source_target_pairs={{0,0},{2,2},{64,66},{66,64},{128,128},{130,130},{192,194},{194,192... | collective-permute-start | bytes 393224 | tf_op jit(solution)/shard_map/ppermute | solution.py:263
  77.5 9.2 %collective-permute-start.2 = (bf16[256,256]{1,0:T(8,128)(2,1)S(1)}, bf16[256,256]{1,0:T(8,128)(2,1)S(1)}, u32[]{:S(2)}, u32[]{:S(2)}) collective-permute-start(bf16[256,256]{1,0:T(8,128)(2,1)S(1)} %get-tuple-element.26), channel_id=1, source_target_pairs={{0,66},{2,64},{64,0},{66,2},{128,194},{130,192},{192,128},{194,130... | collective-permute-start | bytes 393224 | tf_op jit(solution)/shard_map/ppermute | solution.py:263
  79.7 8.4 %collective-permute-start.3 = (bf16[256,256]{1,0:T(8,128)(2,1)S(1)}, bf16[256,256]{1,0:T(8,128)(2,1)S(1)}, u32[]{:S(2)}, u32[]{:S(2)}) collective-permute-start(bf16[256,256]{1,0:T(8,128)(2,1)S(1)} %get-tuple-element.27), channel_id=1, source_target_pairs={{0,128},{2,130},{64,194},{66,192},{128,0},{130,2},{192,66},{194,64... | collective-permute-start | bytes 393224 | tf_op jit(solution)/shard_map/ppermute | solution.py:263
  81.5 8.9 %collective-permute-start.4 = (bf16[256,256]{1,0:T(8,128)(2,1)S(1)}, bf16[256,256]{1,0:T(8,128)(2,1)S(1)}, u32[]{:S(2)}, u32[]{:S(2)}) collective-permute-start(bf16[256,256]{1,0:T(8,128)(2,1)S(1)} %get-tuple-element.28), channel_id=1, source_target_pairs={{0,194},{2,192},{64,128},{66,130},{128,66},{130,64},{192,0},{194,2... | collective-permute-start | bytes 393224 | tf_op jit(solution)/shard_map/ppermute | solution.py:263
  82.1 20.0 %collective-permute-start.14 = (bf16[64,8,128]{2,1,0:T(8,128)(2,1)}, bf16[64,8,128]{2,1,0:T(8,128)(2,1)}, u32[]{:S(2)}, u32[]{:S(2)}) collective-permute-start(bf16[64,8,128]{2,1,0:T(8,128)(2,1)} %get-tuple-element.32), channel_id=1, source_target_pairs={{0,1},{1,0},{2,3},{3,2},{4,5},{5,4},{6,7},{7,6},{8,9},{9,8},{10,11... | collective-permute-start | bytes 393224 | tf_op jit(solution)/shard_map/ppermute | solution.py:317
  92.9 13.9 %all-to-all-start.2 = ((bf16[4,128,512]{2,1,0:T(8,128)(2,1)}), bf16[4,128,512]{2,1,0:T(8,128)(2,1)S(1)}, u32[]{:S(2)}, u32[]{:S(2)}) async-start(bf16[4,128,512]{2,1,0:T(8,128)(2,1)} %bitcast.12), calls=%async_computation.2 | async-start | bytes 1048576 | tf_op jit(solution)/shard_map/all_to_all | solution.py:324
  97.4 5.9 %collective-permute-start.12 = (bf16[64,16,128]{2,1,0:T(8,128)(2,1)S(1)}, bf16[64,16,128]{2,1,0:T(8,128)(2,1)S(1)}, u32[]{:S(2)}, u32[]{:S(2)}) collective-permute-start(bf16[64,16,128]{2,1,0:T(8,128)(2,1)S(1)} %slice_bitcast_fusion), channel_id=1, source_target_pairs={{0,2},{2,0},{1,3},{3,1},{4,6},{6,4},{5,7},{7,5},{8,10},{10,8},{9,1... | collective-permute-start | bytes 786440 | tf_op jit(solution)/shard_map/ppermute | solution.py:238
  97.5 16.3 %collective-permute-start.13 = (bf16[64,8,128]{2,1,0:T(8,128)(2,1)S(1)}, bf16[64,8,128]{2,1,0:T(8,128)(2,1)S(1)}, u32[]{:S(2)}, u32[]{:S(2)}) collective-permute-start(bf16[64,8,128]{2,1,0:T(8,128)(2,1)S(1)} %copy-done.12), channel_id=1, source_target_pairs={{0,1},{1,0},{2,3},{3,2},{4,5},{5,4},{6,7},{7,6},{8,9},{9,8},{10,11... | collective-permute-start | bytes 393224 | tf_op jit(solution)/shard_map/ppermute | solution.py:317
  103.1 10.8 %collective-permute-start.15 = (bf16[64,8,128]{2,1,0:T(8,128)(2,1)S(1)}, bf16[64,8,128]{2,1,0:T(8,128)(2,1)S(1)}, u32[]{:S(2)}, u32[]{:S(2)}) collective-permute-start(bf16[64,8,128]{2,1,0:T(8,128)(2,1)S(1)} %add_convert_fusion), channel_id=1, source_target_pairs={{0,2},{2,0},{1,3},{3,1},{4,6},{6,4},{5,7},{7,5},{8,10},{10,8},{9,1... | collective-permute-start | bytes 393224 | tf_op jit(solution)/shard_map/ppermute | solution.py:238
  107.5 13.8 %all-to-all-start.3 = ((bf16[8,16,512]{2,1,0:T(8,128)(2,1)}), bf16[8,16,512]{2,1,0:T(8,128)(2,1)S(1)}, u32[]{:S(2)}, u32[]{:S(2)}) async-start(bf16[8,16,512]{2,1,0:T(8,128)(2,1)} %bitcast.16), calls=%async_computation.3 | async-start | bytes 262144 | tf_op jit(solution)/shard_map/all_to_all | solution.py:362
  (9 other events, 204.2 us)
